TPU v7x, 32 devices: a whole 2x2x4 slice. The times are simulated.
32 devices in a mesh: ctx: 16 (over z, x, core), fsdp: 2 (over y).
Axes of the slice: x: 2, y: 2, z: 4, core: 2. Of those that a mesh axis runs over, the one named last changes fastest.
Arguments:
- tokens: bfloat16 [8192, 1536], P(('ctx', 'fsdp')), may hold values from -6 to 6
- cotangent: bfloat16 [8192, 1536], P(('ctx', 'fsdp')), may hold values from -6 to 6
- lengths: int32 [2, 4], P('fsdp'), may hold values from 1 to 2048, 4096 in all within a row
- block_of: int32 [2, 16], P('fsdp'), may hold values from 0 to 15, each once within a row
- gain_attn: bfloat16 [1536], P('fsdp'), may hold values from 0.5 to 1.5
- w_query: bfloat16 [1536, 1536], P('fsdp'), may hold values from -0.3125 to 0.3125
- w_keyval: bfloat16 [1536, 256], P('fsdp'), may hold values from -0.15625 to 0.15625
- w_out: bfloat16 [1536, 1536], P('fsdp'), may hold values from -1.25 to 1.25
- gain_mlp: bfloat16 [1536], P('fsdp'), may hold values from 0.5 to 1.5
- w_gateup: bfloat16 [1536, 9216], P('fsdp'), may hold values from -0.15625 to 0.15625
- w_down: bfloat16 [4608, 1536], P('fsdp'), may hold values from -0.1875 to 0.1875
Outputs:
- block_output: bfloat16 [8192, 1536], P(('ctx', 'fsdp'))
- grad_tokens: float32 [8192, 1536], P(('ctx', 'fsdp'))
- grad_gain_attn: float32 [1536], P('fsdp')
- grad_query: float32 [1536, 1536], P('fsdp')
- grad_keyval: float32 [1536, 256], P('fsdp')
- grad_out: float32 [1536, 1536], P('fsdp')
- grad_gain_mlp: float32 [1536], P('fsdp')
- grad_gateup: float32 [1536, 9216], P('fsdp')
- grad_down: float32 [4608, 1536], P('fsdp')
Inputs may be any that keep to these rules, and one draw needn't show every extreme that they name: Each row holds the 4 lengths of one group, summing to 4096. `block_of`: each row is a permutation of the 16 pack blocks of one group.
All inputs are finite; a program needn't handle non-finite values.
Results may differ from a plain program's by a relative error of at most 0.024.
Values may be sent and summed in bfloat16 or wider, within the bound.
No kernel may reach another device: no remote copies, remote signals or barrier semaphores. Data moves between devices by JAX's collectives and lax.ppermute only.
A program may use at most 320 MiB of HBM per device.

v0:
```python
import math

import jax
import jax.numpy as jnp
from jax import lax
from jax.sharding import PartitionSpec as P

H = 12
HD = 128
FF = 4608
WINDOW = 1024


EPSILON = 1e-06


def tables(places, width):
    half_width = width // 2
    frequency = jnp.exp(
        jnp.arange(half_width, dtype=jnp.float32) * (-2.0 * math.log(10000.0) / width)
    )
    angles = places.astype(jnp.float32)[:, None] * frequency[None, :]
    return (jnp.cos(angles), jnp.sin(angles))


def rotate(values, cosine, sine_table):
    half_width = values.shape[-1] // 2
    former = values[..., :half_width]
    latter = values[..., half_width:]
    return jnp.concatenate(
        [former * cosine - latter * sine_table, latter * cosine + former * sine_table], axis=-1
    )


def rms_factor(values):
    return lax.rsqrt(jnp.mean(values * values, axis=-1, keepdims=True) + EPSILON)


def norm_back(grad_normed, values, factor, gain):
    scaled = grad_normed * gain
    return factor * scaled - values * factor**3 * jnp.mean(scaled * values, axis=-1, keepdims=True)


def segment_info(places, seq_lengths):
    seq_ends = jnp.cumsum(seq_lengths)
    passed = places[:, None] >= seq_ends[None, :]
    segment = jnp.sum(passed.astype(jnp.int32), axis=1)
    seq_start = jnp.sum(jnp.where(passed, seq_lengths[None, :], 0), axis=1)
    return (segment, places - seq_start)


def masked_scores(heads_first, keys, allowed):
    scores = jnp.einsum("hqd,kd->hqk", heads_first, keys, preferred_element_type=jnp.float32)
    return jnp.where(allowed[None, :, :], scores, -1e30)


def body(
    tokens,
    cotangent,
    lengths,
    block_of,
    gain_attn,
    w_query,
    w_keyval,
    w_out,
    gain_mlp,
    w_gateup,
    w_down,
):
    tok_rows = tokens.shape[0]
    ctx_count = lax.axis_size("ctx")
    own_index = lax.axis_index("ctx")
    device_ids = jnp.arange(ctx_count, dtype=jnp.int32)
    block_row = block_of[0]
    own_block = jnp.sum(jnp.where(device_ids == own_index, block_row, 0))
    own_start = own_block * tok_rows
    owners = jnp.sum(
        jnp.where(block_row[None, :] == device_ids[:, None], device_ids[None, :], 0), axis=1
    )
    seq_lengths = lengths[0]
    query_places = own_start + jnp.arange(tok_rows, dtype=jnp.int32)
    key_places = own_start - WINDOW + jnp.arange(WINDOW + tok_rows, dtype=jnp.int32)
    query_segment, query_position = segment_info(query_places, seq_lengths)
    key_segment = segment_info(key_places, seq_lengths)[0]
    distance = query_places[:, None] - key_places[None, :]
    allowed = (
        (query_segment[:, None] == key_segment[None, :])
        & (key_places >= 0)[None, :]
        & (distance >= 0)
        & (distance < WINDOW)
    )
    cosine, sine_table = tables(query_position, HD)
    g_attn, w_q, w_kv, w_o = (
        lax.all_gather(gain_attn, "fsdp", axis=0, tiled=True),
        lax.all_gather(w_query, "fsdp", axis=0, tiled=True),
        lax.all_gather(w_keyval, "fsdp", axis=0, tiled=True),
        lax.all_gather(w_out, "fsdp", axis=0, tiled=True),
    )
    gain_one = g_attn.astype(jnp.float32)
    inputs = tokens.astype(jnp.float32)
    scale_attn = rms_factor(inputs)
    normed = (inputs * scale_attn * gain_one).astype(jnp.bfloat16)
    query_raw = jnp.dot(normed, w_q, preferred_element_type=jnp.float32).reshape(tok_rows, H, HD)
    queries = (rotate(query_raw, cosine[:, None, :], sine_table[:, None, :]) * HD ** (-0.5)).astype(
        jnp.bfloat16
    )
    heads_first = jnp.swapaxes(queries, 0, 1)
    kv_raw = jnp.dot(normed, w_kv, preferred_element_type=jnp.float32)
    keyval = jnp.concatenate(
        [rotate(kv_raw[:, :HD], cosine, sine_table), kv_raw[:, HD:]], axis=1
    ).astype(jnp.bfloat16)
    all_kv = lax.all_gather(keyval, "ctx", axis=0, tiled=True)
    packed = jnp.take(all_kv.reshape(ctx_count, tok_rows, 2 * HD), owners, axis=0).reshape(
        ctx_count * tok_rows, 2 * HD
    )
    padded = jnp.concatenate([jnp.zeros((WINDOW, 2 * HD), jnp.bfloat16), packed], axis=0)
    window_kv = lax.dynamic_slice_in_dim(padded, own_start, WINDOW + tok_rows, 0)
    keys = window_kv[:, :HD]
    values = window_kv[:, HD:]
    scores = masked_scores(heads_first, keys, allowed)
    row_max = jnp.max(scores, axis=-1, keepdims=True)
    log_total = row_max + jnp.log(jnp.sum(jnp.exp(scores - row_max), axis=-1, keepdims=True))
    softmax_w = jnp.exp(scores - log_total).astype(jnp.bfloat16)
    attended = jnp.einsum("hqk,kd->qhd", softmax_w, values, preferred_element_type=jnp.float32)
    attended = attended.reshape(tok_rows, H * HD).astype(jnp.bfloat16)
    hidden = inputs + jnp.dot(attended, w_o, preferred_element_type=jnp.float32)
    g_mlp, w_gu, w_dn = (
        lax.all_gather(gain_mlp, "fsdp", axis=0, tiled=True),
        lax.all_gather(w_gateup, "fsdp", axis=0, tiled=True),
        lax.all_gather(w_down, "fsdp", axis=0, tiled=True),
    )
    gain_two = g_mlp.astype(jnp.float32)
    scale_mlp = rms_factor(hidden)
    normed2 = (hidden * scale_mlp * gain_two).astype(jnp.bfloat16)
    both_parts = jnp.dot(normed2, w_gu, preferred_element_type=jnp.float32)
    gate_part = both_parts[:, :FF]
    up_part = both_parts[:, FF:]

    def gelu_tanh(values_in):
        return jax.nn.gelu(values_in, approximate=True)

    activated, gelu_back = jax.vjp(gelu_tanh, gate_part)
    inner_act = (activated * up_part).astype(jnp.bfloat16)
    block_output = (hidden + jnp.dot(inner_act, w_dn, preferred_element_type=jnp.float32)).astype(
        jnp.bfloat16
    )
    d_down = jnp.einsum("tf,td->fd", inner_act, cotangent, preferred_element_type=jnp.float32)
    d_inner = jnp.einsum("td,fd->tf", cotangent, w_dn, preferred_element_type=jnp.float32)
    d_gate = gelu_back(d_inner * up_part)[0]
    d_both = jnp.concatenate([d_gate, d_inner * activated], axis=1).astype(jnp.bfloat16)
    d_gateup = jnp.einsum("td,tf->df", normed2, d_both, preferred_element_type=jnp.float32)
    d_normed2 = jnp.einsum("tf,df->td", d_both, w_gu, preferred_element_type=jnp.float32)
    d_gain_mlp = jnp.sum(d_normed2 * hidden * scale_mlp, axis=0)
    d_hidden = cotangent.astype(jnp.float32) + norm_back(d_normed2, hidden, scale_mlp, gain_two)
    shards = (
        lax.psum_scatter(
            d_gain_mlp.astype(jnp.bfloat16), "fsdp", scatter_dimension=0, tiled=True
        ).astype(jnp.float32),
        lax.psum_scatter(
            d_gateup.astype(jnp.bfloat16), "fsdp", scatter_dimension=0, tiled=True
        ).astype(jnp.float32),
        lax.psum_scatter(
            d_down.astype(jnp.bfloat16), "fsdp", scatter_dimension=0, tiled=True
        ).astype(jnp.float32),
    )
    grad_gain_mlp, grad_gateup, grad_down = (
        lax.psum(shards[0].astype(jnp.bfloat16), "ctx").astype(jnp.float32),
        lax.psum(shards[1].astype(jnp.bfloat16), "ctx").astype(jnp.float32),
        lax.psum(shards[2].astype(jnp.bfloat16), "ctx").astype(jnp.float32),
    )
    d_attn = d_hidden.astype(jnp.bfloat16)
    d_out = jnp.einsum("ti,td->id", attended, d_attn, preferred_element_type=jnp.float32)
    d_attended = jnp.einsum("td,id->ti", d_attn, w_o, preferred_element_type=jnp.float32)
    d_attended = jnp.swapaxes(d_attended.astype(jnp.bfloat16).reshape(tok_rows, H, HD), 0, 1)
    soft_again = jnp.exp(masked_scores(heads_first, keys, allowed) - log_total)
    d_soft = jnp.einsum("hqd,kd->hqk", d_attended, values, preferred_element_type=jnp.float32)
    delta = jnp.sum(soft_again * d_soft, axis=-1, keepdims=True)
    d_scores = (soft_again * (d_soft - delta)).astype(jnp.bfloat16)
    soft_low = soft_again.astype(jnp.bfloat16)
    d_query = jnp.einsum("hqk,kd->qhd", d_scores, keys, preferred_element_type=jnp.float32)
    d_key = jnp.einsum("hqk,hqd->kd", d_scores, heads_first, preferred_element_type=jnp.float32)
    d_value = jnp.einsum("hqk,hqd->kd", soft_low, d_attended, preferred_element_type=jnp.float32)
    d_window = jnp.concatenate([d_key, d_value], axis=1)
    d_padded = lax.dynamic_update_slice_in_dim(
        jnp.zeros((WINDOW + ctx_count * tok_rows, 2 * HD), jnp.float32), d_window, own_start, 0
    )
    d_packed = d_padded[WINDOW:].reshape(ctx_count, tok_rows, 2 * HD)
    d_by_device = jnp.take(d_packed, block_row, axis=0).reshape(ctx_count * tok_rows, 2 * HD)
    d_kv_own = lax.psum_scatter(
        d_by_device.astype(jnp.bfloat16), "ctx", scatter_dimension=0, tiled=True
    ).astype(jnp.float32)
    d_query_raw = rotate(d_query * HD ** (-0.5), cosine[:, None, :], -sine_table[:, None, :])
    d_query_raw = d_query_raw.reshape(tok_rows, H * HD).astype(jnp.bfloat16)
    d_kv_raw = jnp.concatenate(
        [rotate(d_kv_own[:, :HD], cosine, -sine_table), d_kv_own[:, HD:]], axis=1
    ).astype(jnp.bfloat16)
    d_query_w = jnp.einsum("td,ti->di", normed, d_query_raw, preferred_element_type=jnp.float32)
    d_keyval_w = jnp.einsum("td,ti->di", normed, d_kv_raw, preferred_element_type=jnp.float32)
    d_normed = jnp.einsum("ti,di->td", d_query_raw, w_q, preferred_element_type=jnp.float32)
    d_normed = d_normed + jnp.einsum(
        "ti,di->td", d_kv_raw, w_kv, preferred_element_type=jnp.float32
    )
    d_gain_attn = jnp.sum(d_normed * inputs * scale_attn, axis=0)
    grad_tokens = d_hidden + norm_back(d_normed, inputs, scale_attn, gain_one)
    shards = (
        lax.psum_scatter(
            d_gain_attn.astype(jnp.bfloat16), "fsdp", scatter_dimension=0, tiled=True
        ).astype(jnp.float32),
        lax.psum_scatter(
            d_query_w.astype(jnp.bfloat16), "fsdp", scatter_dimension=0, tiled=True
        ).astype(jnp.float32),
        lax.psum_scatter(
            d_keyval_w.astype(jnp.bfloat16), "fsdp", scatter_dimension=0, tiled=True
        ).astype(jnp.float32),
        lax.psum_scatter(
            d_out.astype(jnp.bfloat16), "fsdp", scatter_dimension=0, tiled=True
        ).astype(jnp.float32),
    )
    grad_gain_attn, grad_query, grad_keyval, grad_out = (
        lax.psum(shards[0].astype(jnp.bfloat16), "ctx").astype(jnp.float32),
        lax.psum(shards[1].astype(jnp.bfloat16), "ctx").astype(jnp.float32),
        lax.psum(shards[2].astype(jnp.bfloat16), "ctx").astype(jnp.float32),
        lax.psum(shards[3].astype(jnp.bfloat16), "ctx").astype(jnp.float32),
    )
    return (
        block_output,
        grad_tokens,
        grad_gain_attn,
        grad_query,
        grad_keyval,
        grad_out,
        grad_gain_mlp,
        grad_gateup,
        grad_down,
    )


def solution(mesh):
    in_specs = (
        P(("ctx", "fsdp"), None),
        P(("ctx", "fsdp"), None),
        P("fsdp", None),
        P("fsdp", None),
        P("fsdp"),
        P("fsdp", None),
        P("fsdp", None),
        P("fsdp", None),
        P("fsdp"),
        P("fsdp", None),
        P("fsdp", None),
    )
    out_specs = (
        P(("ctx", "fsdp"), None),
        P(("ctx", "fsdp"), None),
        P("fsdp"),
        P("fsdp", None),
        P("fsdp", None),
        P("fsdp", None),
        P("fsdp"),
        P("fsdp", None),
        P("fsdp", None),
    )
    return jax.shard_map(body, mesh=mesh, in_specs=in_specs, out_specs=out_specs, check_vma=False)
```

profile of v0, /device:TPU:0, one launch (start us, length us, event | category | flops | bytes accessed | tf_op | source)
XLA Modules:
  0.0 1969.4 jit_solution(831052641043363315)
XLA Ops:
  9.9 5.2 all-gather
  17.1 10.9 all_gather.25
  40.8 34.6 %all-gather.8.cloned.1.call-done = bf16[4096,256]{0,1:T(8,128)(2,1)} async-done(((bf16[256,256]{0,1:T(8,128)(2,1)}), bf16[4096,256]{0,1:T(8,128)(2,1)}) %all-gather.8.cloned.1.call-update) | async-done | bytes 2097168 | tf_op jit(solution)/shard_map/all_gather | solution.py:112
  82.9 55.6 %all-gather.10.cloned.1.call-done = bf16[1536,1536]{1,0:T(8,128)(2,1)} async-done(((bf16[768,1536]{1,0:T(8,128)(2,1)}), bf16[1536,1536]{1,0:T(8,128)(2,1)}) %all-gather.10.cloned.1.call-update) | async-done | bytes 4718608 | tf_op jit(solution)/shard_map/all_gather | solution.py:95
  138.5 4.4 fusion.62
  161.1 4.9 convolution_convert_fusion.6
  166.1 36.7 %all-gather.12.cloned.1.call-done = bf16[1536,1536]{1,0:T(8,128)(2,1)} async-done(((bf16[768,1536]{1,0:T(8,128)(2,1)}), bf16[1536,1536]{1,0:T(8,128)(2,1)}) %all-gather.12.cloned.1.call-update) | async-done | bytes 4718608 | tf_op jit(solution)/shard_map/all_gather | solution.py:97
  206.8 328.1 %all-gather.14.cloned.1.call-done = bf16[1536,9216]{1,0:T(8,128)(2,1)} async-done(((bf16[768,9216]{1,0:T(8,128)(2,1)}), bf16[1536,9216]{1,0:T(8,128)(2,1)}) %all-gather.14.cloned.1.call-update) | async-done | bytes 28311568 | tf_op jit(solution)/shard_map/all_gather | solution.py:129
  534.9 18.3 fusion.59
  553.2 153.0 %all-gather.16.cloned.1.call-done = bf16[4608,1536]{1,0:T(8,128)(2,1)} async-done(((bf16[2304,1536]{1,0:T(8,128)(2,1)}), bf16[4608,1536]{1,0:T(8,128)(2,1)}) %all-gather.16.cloned.1.call-update) | async-done | bytes 14155792 | tf_op jit(solution)/shard_map/all_gather | solution.py:130
  706.1 13.0 fusion.7
  719.1 14.4 multiply_reduce_fusion.1
  735.2 4.8 convolution_convert_fusion.5
  742.3 14.0 multiply_reduce_fusion
  760.8 7.6 multiply_convert_fusion
  779.2 61.7 %reduce-scatter.7.cloned.1.call-done = bf16[256,256]{0,1:T(8,128)(2,1)} async-done(((bf16[4096,256]{0,1:T(8,128)(2,1)}), bf16[256,256]{0,1:T(8,128)(2,1)}) %reduce-scatter.7.cloned.1.call-update) | async-done | bytes 131088 | tf_op jit(solution)/shard_map/reduce_scatter | solution.py:189
  844.5 4.7 convolution_convert_fusion.2
  850.8 6.8 multiply_bitcast_fusion
  865.9 9.0 convolution_convert_fusion.1
  876.3 15.3 convolution_convert_fusion
  892.0 31.9 %reduce-scatter.13.cloned.1.call-done = bf16[768,1536]{1,0:T(8,128)(2,1)} async-done(((bf16[1536,1536]{1,0:T(8,128)(2,1)}), bf16[768,1536]{1,0:T(8,128)(2,1)}) %reduce-scatter.13.cloned.1.call-update) | async-done | bytes 2359312 | tf_op jit(solution)/shard_map/reduce_scatter | solution.py:215
  923.9 63.0 %reduce-scatter.9.cloned.1.call-done = bf16[768,1536]{1,0:T(8,128)(2,1)} async-done(((bf16[1536,1536]{1,0:T(8,128)(2,1)}), bf16[768,1536]{1,0:T(8,128)(2,1)}) %reduce-scatter.9.cloned.1.call-update) | async-done | bytes 2359312 | tf_op jit(solution)/shard_map/reduce_scatter | solution.py:209
  986.9 164.2 %reduce-scatter.17.cloned.1.call-done = bf16[2304,1536]{1,0:T(8,128)(2,1)} async-done(((bf16[4608,1536]{1,0:T(8,128)(2,1)}), bf16[2304,1536]{1,0:T(8,128)(2,1)}) %reduce-scatter.17.cloned.1.call-update) | async-done | bytes 7077904 | tf_op jit(solution)/shard_map/reduce_scatter | solution.py:162
  1151.1 316.0 %reduce-scatter.15.cloned.1.call-done = bf16[768,9216]{1,0:T(8,128)(2,1)} async-done(((bf16[1536,9216]{1,0:T(8,128)(2,1)}), bf16[768,9216]{1,0:T(8,128)(2,1)}) %reduce-scatter.15.cloned.1.call-update) | async-done | bytes 14155792 | tf_op jit(solution)/shard_map/reduce_scatter | solution.py:159
  1469.0 10.5 fusion.9
  1485.2 5.0 all-reduce.5
  1490.4 34.5 %all-reduce.3 = (bf16[768]{0:T(1024)(128)(2,1)S(1)}, bf16[768]{0:T(1024)(128)(2,1)S(1)}) all-reduce(bf16[768]{0:T(1024)(128)(2,1)S(1)} %dynamic-slice.1, bf16[768]{0:T(1024)(128)(2,1)S(1)} %dynamic-slice.3), channel_id=1, replica_groups=mesh['ctx'=16,'fsdp'=2] {'ctx'}, use_global_device_ids=true, to_apply=%region_16.17 | all-reduce | flops 1536 | bytes 6144 | tf_op jit(solution)/shard_map/psum | solution.py:220
  1529.1 403.6 %all-reduce.8.cloned.1.call-done = (bf16[768,1536]{1,0:T(8,128)(2,1)}, bf16[768,256]{1,0:T(8,128)(2,1)}, bf16[768,1536]{1,0:T(8,128)(2,1)}, bf16[768,9216]{1,0:T(8,128)(2,1)}, bf16[2304,1536]{1,0:T(8,128)(2,1)}) async-done(((bf16[768,1536]{1,0:T(8,128)(2,1)}, bf16[768,256]{1,0:T(8,128)(2,1)}, bf16[768,1536]{1,0:T(8,128)(2,1)}, bf16[768,9216]{1,0:T(8,128)(2,1)}, bf16[2304,1536]{1,0:T(8,128)(2,1)}), ...) | async-done | bytes 26345488 | tf_op jit(solution)/shard_map/psum | solution.py:221
  1932.7 4.9 convert_element_type.156
  1940.3 4.6 convert_element_type.160
  1944.9 9.9 convert_element_type.164
  1954.8 7.3 convert_element_type.166
  (173 shorter events, 94.5 us)
Async XLA Ops:
  7.2 68.2 %all-gather.8.cloned.1.call-start = ((), (), s32[]{:S(2)}) async-start(), calls=%async_computation.6 | async-start | bytes 2228224 | tf_op jit(solution)/shard_map/all_gather | solution.py:112
  32.4 106.1 %all-gather.10.cloned.1.call-start = ((), (), s32[]{:S(2)}) async-start(), calls=%async_computation.7 | async-start | bytes 7077888 | tf_op jit(solution)/shard_map/all_gather | solution.py:95
  33.1 169.6 %all-gather.12.cloned.1.call-start = ((), (), s32[]{:S(2)}) async-start(), calls=%async_computation.8 | async-start | bytes 7077888 | tf_op jit(solution)/shard_map/all_gather | solution.py:97
  33.9 501.0 %all-gather.14.cloned.1.call-start = ((), (), s32[]{:S(2)}) async-start(), calls=%async_computation.9 | async-start | bytes 42467328 | tf_op jit(solution)/shard_map/all_gather | solution.py:129
  34.5 671.7 %all-gather.16.cloned.1.call-start = ((), (), s32[]{:S(2)}) async-start(), calls=%async_computation.10 | async-start | bytes 21233664 | tf_op jit(solution)/shard_map/all_gather | solution.py:130
  35.0 805.8 %reduce-scatter.7.cloned.1.call-start = ((), (), s32[]{:S(2)}) async-start(), calls=%async_computation.11 | async-start | bytes 2228224 | tf_op jit(solution)/shard_map/reduce_scatter | solution.py:189
  35.3 114.5 %copy-start.21 = (f32[256,64]{1,0:T(8,128)}, f32[256,64]{1,0:T(8,128)S(1)}, u32[]{:S(2)}) copy-start(f32[256,64]{1,0:T(8,128)S(1)} %copy.67) | copy-start | bytes 196612
  80.6 57.9 %copy-start.4 = (bf16[256,1536]{1,0:T(8,128)(2,1)S(1)}, bf16[256,1536]{1,0:T(8,128)(2,1)}, u32[]{:S(2)}) copy-start(bf16[256,1536]{1,0:T(8,128)(2,1)} %param.11) | copy-start | bytes 2359300
  82.9 76.3 %copy-start.1 = (bf16[4096,256]{1,0:T(8,128)(2,1)}, bf16[4096,256]{1,0:T(8,128)(2,1)S(1)}, u32[]{:S(2)}) copy-start(bf16[4096,256]{1,0:T(8,128)(2,1)S(1)} %bitcast_select_fusion) | copy-start | bytes 6291460
  206.8 526.7 %copy-start.6 = (f32[256,1536]{1,0:T(8,128)}, f32[256,1536]{1,0:T(8,128)S(1)}, u32[]{:S(2)}) copy-start(f32[256,1536]{1,0:T(8,128)S(1)} %get-tuple-element.47) | copy-start | bytes 4718596
  534.9 171.2 %copy-start.12 = (bf16[256,1536]{1,0:T(8,128)(2,1)S(1)}, bf16[256,1536]{1,0:T(8,128)(2,1)}, u32[]{:S(2)}) copy-start(bf16[256,1536]{1,0:T(8,128)(2,1)} %param.12) | copy-start | bytes 2359300
  735.2 21.0 %slice-start = ((s8[15728640]{0:T(1024)(128)(4,1)}), s8[3145728]{0:T(1024)(128)(4,1)S(1)}, s32[]{:S(2)}) async-start(s8[15728640]{0:T(1024)(128)(4,1)} %bitcast.76), calls=%async_computation.18 | async-start | bytes 6291456
  742.2 14.0 slice-start.1
  742.2 14.0 slice-start.2
  742.2 14.8 slice-start.3
  742.2 15.0 copy-start.20
  760.8 7.7 copy-start.15
  779.1 63.9 %copy-start.5 = (bf16[256,1536]{1,0:T(8,128)(2,1)S(1)}, bf16[256,1536]{1,0:T(8,128)(2,1)}, u32[]{:S(2)}) copy-start(bf16[256,1536]{1,0:T(8,128)(2,1)} %param.11) | copy-start | bytes 2359300
  779.1 65.4 %copy-start.10 = (f32[256,1536]{1,0:T(8,128)S(1)}, f32[256,1536]{1,0:T(8,128)}, u32[]{:S(2)}) copy-start(f32[256,1536]{1,0:T(8,128)} %copy-done.9) | copy-start | bytes 4718596
  779.1 112.9 %reduce-scatter.11.cloned.1.call-start = ((), (), s32[]{:S(2)}) async-start(), calls=%async_computation.13 | async-start | bytes 1179648 | tf_op jit(solution)/shard_map/reduce_scatter | solution.py:212
  844.4 79.5 %reduce-scatter.13.cloned.1.call-start = ((), (), s32[]{:S(2)}) async-start(), calls=%async_computation.14 | async-start | bytes 7077888 | tf_op jit(solution)/shard_map/reduce_scatter | solution.py:215
  849.2 8.5 copy-start.22
  849.2 137.7 %reduce-scatter.9.cloned.1.call-start = ((), (), s32[]{:S(2)}) async-start(), calls=%async_computation.12 | async-start | bytes 7077888 | tf_op jit(solution)/shard_map/reduce_scatter | solution.py:209
  864.8 286.3 %reduce-scatter.17.cloned.1.call-start = ((), (), s32[]{:S(2)}) async-start(), calls=%async_computation.16 | async-start | bytes 21233664 | tf_op jit(solution)/shard_map/reduce_scatter | solution.py:162
  874.9 592.2 %reduce-scatter.15.cloned.1.call-start = ((), (), s32[]{:S(2)}) async-start(), calls=%async_computation.15 | async-start | bytes 42467328 | tf_op jit(solution)/shard_map/reduce_scatter | solution.py:159
  891.7 1041.0 %all-reduce.8.cloned.1.call-start = ((), (), s32[]{:S(2)}) async-start(), calls=%async_computation.17 | async-start | bytes 52690944 | tf_op jit(solution)/shard_map/psum | solution.py:221
  1469.0 10.5 copy-start.19
  1483.4 42.7 %copy-start.11 = (f32[256,1536]{1,0:T(8,128)S(1)}, f32[256,1536]{1,0:T(8,128)}, u32[]{:S(2)}) copy-start(f32[256,1536]{1,0:T(8,128)} %copy-done.9) | copy-start | bytes 4718596
  1483.4 42.7 %copy-start.23 = (f32[256]{0:T(256)S(1)}, f32[256]{0:T(256)}, u32[]{:S(2)}) copy-start(f32[256]{0:T(256)} %get-tuple-element.40) | copy-start | bytes 3076
  1932.7 12.2 copy-start.8
  1940.3 14.5 slice-start.4
  1944.9 9.9 slice-start.5
  (13 other events, 32.2 us)
Sparse Core Ops, SparseCore 0:
  32.5 42.8 all-gather.7
  76.9 61.5 all-gather.9
  140.0 62.6 all-gather.11
  204.1 330.7 all-gather.13
  536.3 169.7 all-gather.15
  779.2 61.6 reduce-scatter.6
  844.5 16.4 reduce-scatter.10
  863.9 59.9 reduce-scatter.12
  926.9 59.9 reduce-scatter.8
  989.6 161.4 reduce-scatter.16
  1154.0 313.1 reduce-scatter.14
  1472.3 460.3 all-reduce.7
where the time goes:
time: 1980 us; the launch traced here: 1970 us
  waiting for transfers between devices  1650 us (83%)
  matrix products  144 us (7%)
  other arithmetic  63.5 us (3%)
  blocking collectives  60 us (3%)
  local copies, waits for them, and re-layouts  33.5 us (2%)
    psum x1, waiting for transfers between devices, body(): lax.psum(shards[1].astype(jnp.bfloat16), 'ctx').astype(jnp.float32)  404 us
    all_gather x1, waiting for transfers between devices, body(): lax.all_gather(w_gateup, 'fsdp', axis=0, tiled=True)  328 us
    reduce_scatter x1, waiting for transfers between devices, body(): lax.psum_scatter(d_gateup.astype(jnp.bfloat16), 'fsdp', scatter_dimension...  316 us
    reduce_scatter x1, waiting for transfers between devices, body(): lax.psum_scatter(d_down.astype(jnp.bfloat16), 'fsdp', scatter_dimension=0...  164 us
    all_gather x1, waiting for transfers between devices, body(): lax.all_gather(w_down, 'fsdp', axis=0, tiled=True)  153 us
    reduce_scatter x1, waiting for transfers between devices, body(): lax.psum_scatter(d_query_w.astype(jnp.bfloat16), 'fsdp', scatter_dimensio...  63 us
    reduce_scatter x1, waiting for transfers between devices, body(): lax.psum_scatter(d_by_device.astype(jnp.bfloat16), 'ctx', scatter_dimensi...  61.7 us
    all_gather x1, waiting for transfers between devices, body(): lax.all_gather(w_query, 'fsdp', axis=0, tiled=True)  55.6 us
  transfers between devices with their start and end apart: 12, of which 11 were waited for; matrix products, arithmetic and copies ran while one was open for 6% of the time, Pallas kernels for 0%

commit v1 on v0

v1 whole, which is shorter than its diff:
```python
import math

import jax
import jax.numpy as jnp
from jax import lax
from jax.sharding import Mesh
from jax.sharding import PartitionSpec as P

H = 12
HD = 128
FF = 4608
WINDOW = 1024
EPSILON = 1e-06
BF = jnp.bfloat16
F32 = jnp.float32


def tables(places, width):
    half_width = width // 2
    frequency = jnp.exp(
        jnp.arange(half_width, dtype=jnp.float32) * (-2.0 * math.log(10000.0) / width)
    )
    angles = places.astype(jnp.float32)[:, None] * frequency[None, :]
    return (jnp.cos(angles), jnp.sin(angles))


def rotate(values, cosine, sine_table):
    half_width = values.shape[-1] // 2
    former = values[..., :half_width]
    latter = values[..., half_width:]
    return jnp.concatenate(
        [former * cosine - latter * sine_table, latter * cosine + former * sine_table], axis=-1
    )


def rms_factor(values):
    return lax.rsqrt(jnp.mean(values * values, axis=-1, keepdims=True) + EPSILON)


def norm_back(grad_normed, values, factor, gain):
    scaled = grad_normed * gain
    return factor * scaled - values * factor**3 * jnp.mean(scaled * values, axis=-1, keepdims=True)


def segment_info(places, seq_lengths):
    seq_ends = jnp.cumsum(seq_lengths)
    passed = places[:, None] >= seq_ends[None, :]
    segment = jnp.sum(passed.astype(jnp.int32), axis=1)
    seq_start = jnp.sum(jnp.where(passed, seq_lengths[None, :], 0), axis=1)
    return (segment, places - seq_start)


def masked_scores(heads_first, keys, allowed):
    scores = jnp.einsum("hqd,kd->hqk", heads_first, keys, preferred_element_type=jnp.float32)
    return jnp.where(allowed[None, :, :], scores, -1e30)


def dot(a, b):
    return jnp.dot(a, b, preferred_element_type=F32)


def dot_t(a, b):
    return lax.dot_general(a, b, (((1,), (1,)), ((), ())), preferred_element_type=F32)


def t_dot(a, b):
    return lax.dot_general(a, b, (((0,), (0,)), ((), ())), preferred_element_type=F32)


def bits_of(axis):
    count = lax.axis_size(axis).bit_length() - 1
    return [(axis, k) for k in reversed(range(count))]


def own_bit(bit):
    return (lax.axis_index(bit[0]) >> bit[1]) & 1


def flip(array, bit):
    axis, k = bit
    return lax.ppermute(array, axis, [(i, i ^ (1 << k)) for i in range(lax.axis_size(axis))])


def pick(array, index, dim):
    return lax.dynamic_index_in_dim(array, index, dim, keepdims=False)


def gather_rel(array, bits):
    held = array[None]
    for bit in bits:
        held = jnp.concatenate([held, flip(held, bit)], axis=0)
    return held


def scatter_rel(array, bits):
    for bit in reversed(bits):
        half = array.shape[0] // 2
        array = (array[:half].astype(F32) + flip(array[half:].astype(BF), bit).astype(F32)).astype(BF)
    return array[0]


def join(own, other, bit, dim):
    low = jnp.concatenate([own, other], axis=dim)
    high = jnp.concatenate([other, own], axis=dim)
    return jnp.where(own_bit(bit) == 0, low, high)


def gather_abs(array, bits, dim):
    for bit in bits:
        array = join(array, flip(array, bit), bit, dim)
    return array


def scatter_abs(array, bits, dim=0):
    rows = array.shape[dim]
    lead = array.shape[:dim]
    tail = array.shape[dim + 1 :]
    count = len(bits)
    array = array.reshape(lead + (2,) * count + (rows >> count,) + tail)
    for place in reversed(range(count)):
        bit = bits[place]
        mine = own_bit(bit)
        sent = pick(array, 1 - mine, dim + place)
        kept = pick(array, mine, dim + place)
        array = (kept.astype(F32) + flip(sent, bit).astype(F32)).astype(BF)
    return array


def body(
    tokens,
    cotangent,
    lengths,
    block_of,
    gain_attn,
    w_query,
    w_keyval,
    w_out,
    gain_mlp,
    w_gateup,
    w_down,
):
    tok_rows, width = tokens.shape
    y_count, z_count = lax.axis_size("y"), lax.axis_size("z")
    ctx_count = 4 * z_count
    x_bit, c_bit = ("x", 0), ("c", 0)
    y_bits, z_bits = bits_of("y"), bits_of("z")
    up_z = list(reversed(z_bits))
    x_at, c_at, y_at = lax.axis_index("x"), lax.axis_index("c"), lax.axis_index("y")
    own_index = (lax.axis_index("z") * 2 + x_at) * 2 + c_at

    def whole_weight(shard, share):
        piece = shard
        rows = shard.shape[0]
        if share:
            for bit in share:
                rows = rows // 2
                piece = lax.dynamic_slice_in_dim(piece, own_bit(bit) * rows, rows, 0)
        others = gather_rel(piece, y_bits)
        parts = []
        for r in range(1, y_count):
            part = others[r]
            for bit in reversed(share):
                part = join(part, flip(part, bit), bit, 0)
            parts.append(part)
        if y_count == 2:
            return join(shard, parts[0], y_bits[0], 0)
        rel = jnp.stack([shard] + parts)
        order = jnp.arange(y_count, dtype=jnp.int32) ^ y_at
        return jnp.take(rel, order, axis=0).reshape((y_count * shard.shape[0],) + shard.shape[1:])

    gains = whole_weight(jnp.stack([gain_attn, gain_mlp], axis=1), [])
    gain_one = gains[:, 0].astype(F32)
    gain_two = gains[:, 1].astype(F32)
    w_kv = whole_weight(w_keyval, [c_bit])
    w_q = whole_weight(w_query, [c_bit, x_bit])
    w_o = whole_weight(w_out, [c_bit, x_bit])

    units = FF // (2 * y_count)
    gu = w_gateup.reshape(w_gateup.shape[0], 2, y_count, 2, units)
    wide = gu.shape[0]

    def unit_columns(rows, part, y_index):
        return lax.dynamic_slice_in_dim(
            rows, part * FF + (y_index * 2 + x_at) * units, units, 1
        )

    rows_half = wide // 2
    half_rows = lax.dynamic_slice_in_dim(w_gateup, c_at * rows_half, rows_half, 0)
    gu_parts = {}
    for r in range(1, y_count):
        piece = jnp.concatenate([unit_columns(half_rows, part, y_at ^ r) for part in (0, 1)], axis=1)
        piece = lax.ppermute(piece, "y", [(i, i ^ r) for i in range(y_count)])
        gu_parts[r] = join(piece, flip(piece, c_bit), c_bit, 0)
    gu_parts[0] = jnp.concatenate([unit_columns(w_gateup, part, y_at) for part in (0, 1)], axis=1)
    if y_count == 2:
        w_gu = join(gu_parts[0], gu_parts[1], y_bits[0], 0)
    else:
        order = jnp.arange(y_count, dtype=jnp.int32) ^ y_at
        w_gu = jnp.take(jnp.stack([gu_parts[r] for r in range(y_count)]), order, axis=0)
        w_gu = w_gu.reshape(width, 2 * units)
    w_dn = lax.dynamic_slice_in_dim(w_down, x_at * units, units, 0)

    half_tok = tok_rows // 2
    group = 2 * y_count
    order_a = y_bits + [x_bit]
    order_b = [x_bit] + y_bits

    def group_gather(array):
        first = gather_rel(array[:half_tok], order_a).reshape(group * half_tok, -1)
        second = gather_rel(array[half_tok:], order_b).reshape(group * half_tok, -1)
        return jnp.concatenate([first, second], axis=0)

    def group_scatter(array):
        array = array.astype(BF).reshape(2, group, half_tok, -1)
        return jnp.concatenate(
            [scatter_rel(array[0], order_a), scatter_rel(array[1], order_b)], axis=0
        ).astype(F32)

    cot_all = group_gather(cotangent)

    device_ids = jnp.arange(ctx_count, dtype=jnp.int32)
    block_row = block_of[0]
    own_block = jnp.sum(jnp.where(device_ids == own_index, block_row, 0))
    own_start = own_block * tok_rows
    owners = jnp.sum(
        jnp.where(block_row[None, :] == device_ids[:, None], device_ids[None, :], 0), axis=1
    )
    seq_lengths = lengths[0]
    query_places = own_start + jnp.arange(tok_rows, dtype=jnp.int32)
    key_places = own_start - WINDOW + jnp.arange(WINDOW + tok_rows, dtype=jnp.int32)
    query_segment, query_position = segment_info(query_places, seq_lengths)
    key_segment = segment_info(key_places, seq_lengths)[0]
    distance = query_places[:, None] - key_places[None, :]
    allowed = (
        (query_segment[:, None] == key_segment[None, :])
        & (key_places >= 0)[None, :]
        & (distance >= 0)
        & (distance < WINDOW)
    )
    cosine, sine_table = tables(query_position, HD)

    inputs = tokens.astype(F32)
    scale_attn = rms_factor(inputs)
    normed = (inputs * scale_attn * gain_one).astype(BF)
    kv_raw = dot(normed, w_kv)
    keyval = jnp.concatenate(
        [rotate(kv_raw[:, :HD], cosine, sine_table), kv_raw[:, HD:]], axis=1
    ).astype(BF)
    kv_bits = [x_bit] + z_bits + [c_bit]
    all_kv = gather_rel(keyval, kv_bits)

    def rel_place(ctx_index):
        differ = ctx_index ^ own_index
        place = (differ >> 1) & 1
        for n, (_, k) in enumerate(z_bits):
            place = place | (((differ >> (2 + k)) & 1) << (1 + n))
        return place | ((differ & 1) << (1 + len(z_bits)))

    query_raw = dot(normed, w_q).reshape(tok_rows, H, HD)
    queries = (rotate(query_raw, cosine[:, None, :], sine_table[:, None, :]) * HD ** (-0.5)).astype(BF)
    heads_first = jnp.swapaxes(queries, 0, 1)

    spans = WINDOW // tok_rows
    window_blocks = own_block - spans + jnp.arange(spans + 1, dtype=jnp.int32)
    window_places = rel_place(jnp.take(owners, jnp.clip(window_blocks, 0, ctx_count - 1)))
    window_kv = jnp.take(all_kv, window_places, axis=0).reshape(WINDOW + tok_rows, 2 * HD)
    keys = window_kv[:, :HD]
    values = window_kv[:, HD:]
    scores = masked_scores(heads_first, keys, allowed)
    row_max = jnp.max(scores, axis=-1, keepdims=True)
    log_total = row_max + jnp.log(jnp.sum(jnp.exp(scores - row_max), axis=-1, keepdims=True))
    softmax_w = jnp.exp(scores - log_total).astype(BF)
    attended = jnp.einsum("hqk,kd->qhd", softmax_w, values, preferred_element_type=F32)
    attended = attended.reshape(tok_rows, H * HD).astype(BF)
    hidden = inputs + dot(attended, w_o)

    scale_mlp = rms_factor(hidden)
    normed2 = group_gather((hidden * scale_mlp * gain_two).astype(BF))
    both_parts = dot(normed2, w_gu)
    gate_part = both_parts[:, :units]
    up_part = both_parts[:, units:]

    def gelu_tanh(values_in):
        return jax.nn.gelu(values_in, approximate=True)

    activated, gelu_back = jax.vjp(gelu_tanh, gate_part)
    inner_act = (activated * up_part).astype(BF)
    d_inner = dot_t(cot_all, w_dn)
    d_gate = gelu_back(d_inner * up_part)[0].astype(BF)
    d_up = (d_inner * activated).astype(BF)
    d_normed2 = group_scatter(dot_t(jnp.concatenate([d_gate, d_up], axis=1), w_gu))

    def core_sum(left, kept, sent):
        mine, theirs = t_dot(left, kept).astype(BF), t_dot(left, sent).astype(BF)
        return (mine.astype(F32) + flip(theirs, c_bit).astype(F32)).astype(BF)

    low_cot, high_cot = cot_all[:, : width // 2], cot_all[:, width // 2 :]
    down_sum = core_sum(
        inner_act,
        jnp.where(c_at == 0, low_cot, high_cot),
        jnp.where(c_at == 0, high_cot, low_cot),
    )
    down_sum = scatter_abs(down_sum, z_bits)
    down_half = gather_abs(down_sum, up_z[::-1] if False else z_bits, 0) if False else None
    up_sum = core_sum(
        normed2, jnp.where(c_at == 0, d_gate, d_up), jnp.where(c_at == 0, d_up, d_gate)
    )
    up_sum = scatter_abs(up_sum.reshape(y_count, width // y_count, units), z_bits, 1)

    def spread_z(array, dim):
        return gather_z(array, dim)

    def gather_z(array, dim):
        held = array[None]
        for bit in z_bits:
            held = jnp.concatenate([held, flip(held, bit)], axis=0)
        z_at = lax.axis_index("z")
        count = len(z_bits)
        order = []
        for place in range(z_count):
            differ = place ^ z_at
            rel = 0
            for n, (_, k) in enumerate(z_bits):
                rel = rel | (((differ >> k) & 1) << n)
            order.append(rel)
        del count
        return jnp.concatenate([pick(held, rel, 0) for rel in order], axis=dim)

    down_half = gather_z(down_sum, 0)
    down_half = gather_abs(down_half, [x_bit], 0)
    grad_down = gather_abs(down_half, [c_bit], 1).astype(F32)

    pieces = [pick(up_sum, y_at, 0)]
    for r in range(1, y_count):
        pieces.append(
            lax.ppermute(
                pick(up_sum, y_at ^ r, 0), "y", [(i, i ^ r) for i in range(y_count)]
            )
        )
    if y_count == 2:
        up_rows = join(pieces[0][:, None], pieces[1][:, None], y_bits[0], 1)
    else:
        order = jnp.arange(y_count, dtype=jnp.int32) ^ y_at
        up_rows = jnp.take(jnp.stack(pieces, axis=1), order, axis=1)
    up_rows = gather_z(up_rows, 0)
    up_rows = gather_abs(up_rows[:, :, None], [x_bit], 2)
    up_rows = up_rows.reshape(up_rows.shape[0], FF)
    grad_gateup = gather_abs(up_rows, [c_bit], 1).astype(F32)

    block_output = (hidden + group_scatter(dot(inner_act, w_dn))).astype(BF)

    d_gain_mlp = jnp.sum(d_normed2 * hidden * scale_mlp, axis=0)
    d_hidden = cotangent.astype(F32) + norm_back(d_normed2, hidden, scale_mlp, gain_two)

    def attn_grad(left, right):
        half = right.shape[1] // 2
        low_part, high_part = right[:, :half], right[:, half:]
        total = core_sum(
            left,
            jnp.where(c_at == 0, low_part, high_part),
            jnp.where(c_at == 0, high_part, low_part),
        )
        total = scatter_abs(total, z_y_x)
        return total

    z_y_x = y_bits
    def attn_finish(total):
        total = scatter_abs(total, z_bits + [x_bit])
        total = gather_z_x(total)
        return gather_abs(total, [c_bit], 1).astype(F32)

    def gather_z_x(total):
        rows, cols = total.shape
        total = gather_z(total[None], 0)
        total = gather_abs(total[:, None], [x_bit], 1)
        return total.reshape(z_count * 2 * rows, cols)

    d_attn = d_hidden.astype(BF)
    grad_out = attn_finish(attn_grad(attended, d_attn))
    d_attended = dot_t(d_attn, w_o)
    d_attended = jnp.swapaxes(d_attended.astype(BF).reshape(tok_rows, H, HD), 0, 1)
    soft_again = jnp.exp(masked_scores(heads_first, keys, allowed) - log_total)
    d_soft = jnp.einsum("hqd,kd->hqk", d_attended, values, preferred_element_type=F32)
    delta = jnp.sum(soft_again * d_soft, axis=-1, keepdims=True)
    d_scores = (soft_again * (d_soft - delta)).astype(BF)
    soft_low = soft_again.astype(BF)
    d_key = jnp.einsum("hqk,hqd->kd", d_scores, heads_first, preferred_element_type=F32)
    d_value = jnp.einsum("hqk,hqd->kd", soft_low, d_attended, preferred_element_type=F32)
    d_window = jnp.concatenate([d_key, d_value], axis=1).astype(BF)
    d_window = d_window.reshape(spans + 1, tok_rows, 2 * HD)
    d_window = jnp.concatenate([d_window, jnp.zeros_like(d_window[:1])], axis=0)
    rel_ids = jnp.zeros((ctx_count,), jnp.int32)
    rel_r = jnp.arange(ctx_count, dtype=jnp.int32)
    for n, (_, k) in enumerate(kv_bits):
        axis = kv_bits[n][0]
        shift = {"c": 0, "x": 1, "z": 2 + k}[axis]
        rel_ids = rel_ids | (((rel_r >> n) & 1) << shift)
    rel_ids = rel_ids ^ own_index
    entry = jnp.take(block_row, rel_ids) - (own_block - spans)
    entry = jnp.where((entry >= 0) & (entry <= spans), entry, spans + 1)
    d_rel = jnp.take(d_window, entry, axis=0)
    d_kv_own = scatter_rel(d_rel, kv_bits).astype(F32)

    d_query = jnp.einsum("hqk,kd->qhd", d_scores, keys, preferred_element_type=F32)
    d_query_raw = rotate(d_query * HD ** (-0.5), cosine[:, None, :], -sine_table[:, None, :])
    d_query_raw = d_query_raw.reshape(tok_rows, H * HD).astype(BF)
    grad_query = attn_finish(attn_grad(normed, d_query_raw))
    d_normed = dot_t(d_query_raw, w_q)
    d_kv_raw = jnp.concatenate(
        [rotate(d_kv_own[:, :HD], cosine, -sine_table), d_kv_own[:, HD:]], axis=1
    ).astype(BF)
    grad_keyval = attn_finish(attn_grad(normed, d_kv_raw))
    d_normed = d_normed + dot_t(d_kv_raw, w_kv)
    d_gain_attn = jnp.sum(d_normed * inputs * scale_attn, axis=0)
    grad_tokens = d_hidden + norm_back(d_normed, inputs, scale_attn, gain_one)

    d_gains = lax.psum(jnp.stack([d_gain_attn, d_gain_mlp]), ("z", "x", "c", "y"))
    d_gains = lax.dynamic_slice_in_dim(d_gains, y_at * gain_attn.shape[0], gain_attn.shape[0], 1)
    return (
        block_output,
        grad_tokens,
        d_gains[0],
        grad_query,
        grad_keyval,
        grad_out,
        d_gains[1],
        grad_gateup,
        grad_down,
    )


def solution(mesh):
    ctx_count, y_count = mesh.shape["ctx"], mesh.shape["fsdp"]
    fine = Mesh(mesh.devices.reshape(ctx_count // 4, 2, 2, y_count), ("z", "x", "c", "y"))
    rows, shard = P(("z", "x", "c", "y"), None), P("y", None)
    in_specs = (rows, rows, shard, shard, P("y"), shard, shard, shard, P("y"), shard, shard)
    out_specs = (rows, rows, P("y"), shard, shard, shard, P("y"), shard, shard)
    return jax.shard_map(body, mesh=fine, in_specs=in_specs, out_specs=out_specs, check_vma=False)
```

time: 1980 us -> 963 us (0.49)
  waiting for transfers between devices: 1650 us -> 450 us
  other arithmetic: 63.5 us -> 142 us
  local copies, waits for them, and re-layouts: 33.5 us -> 112 us
  starting transfers between devices: 0.95 us -> 72.1 us
  blocking collectives: 60 us -> 39.3 us
    reduce_scatter x6 -> x0, waiting for transfers between devices: 637 us -> none  [the longest x1 316 us: body(): lax.psum_scatter(d_gateup.astype(jnp.bfloat16), 'fsdp', scatter_dimension...]
    all_gather x5 -> x0, waiting for transfers between devices: 608 us -> none  [the longest x1 328 us: body(): lax.all_gather(w_gateup, 'fsdp', axis=0, tiled=True)]
    ppermute x0 -> x77, waiting for transfers between devices: none -> 450 us  [the longest x75 447 us: flip(): lax.ppermute(array, axis, [(i, i ^ 1 << k) for i in range(lax.axis_size(a...]
    psum x1 -> x0, waiting for transfers between devices: 404 us -> none  [body(): lax.psum(shards[1].astype(jnp.bfloat16), 'ctx').astype(jnp.float32)]
    ppermute x0 -> x77, starting transfers between devices: none -> 72.1 us  [the longest x75 68.5 us: flip(): lax.ppermute(array, axis, [(i, i ^ 1 << k) for i in range(lax.axis_size(a...]
    unnamed x73 -> x228, local copies, waits for them, and re-layouts: 17.6 us -> 53.7 us
    select_n x3 -> x19, other arithmetic: 2.27 us -> 29.3 us  [the longest x13 24.1 us: join(): return jnp.where(own_bit(bit) == 0, low, high)]
    concatenate x1 -> x24, other arithmetic: 0.05 us -> 24.9 us  [the longest x11 17.4 us: gather_rel(): held = jnp.concatenate([held, flip(held, bit)], axis=0)]
  transfers between devices with their start and end apart: 12 -> 77, of which waited for: 11 -> 29; matrix products, arithmetic and copies ran while one was open for 6% -> 28% of each run, Pallas kernels for 0% -> 0%
where the time goes in v1:
time: 963 us; the launch traced here: 955 us
  waiting for transfers between devices  450 us (47%)
  other arithmetic  142 us (15%)
  matrix products  135 us (14%)
  local copies, waits for them, and re-layouts  112 us (12%)
  starting transfers between devices  72.1 us (7%)
  blocking collectives  39.3 us (4%)
    ppermute x75, waiting for transfers between devices, flip(): lax.ppermute(array, axis, [(i, i ^ 1 << k) for i in range(lax.axis_size(a...  447 us
    ppermute x75, starting transfers between devices, flip(): lax.ppermute(array, axis, [(i, i ^ 1 << k) for i in range(lax.axis_size(a...  68.5 us
    unnamed x228, local copies, waits for them, and re-layouts  53.7 us
    dot_general x5, matrix products, dot_t(): lax.dot_general(a, b, (((1,), (1,)), ((), ())), preferred_element_type=F32)  40.5 us
    psum x1, blocking collectives, body(): lax.psum(jnp.stack([d_gain_attn, d_gain_mlp]), ('z', 'x', 'c', 'y'))  39.3 us
    dot_general x5, matrix products, dot(): return jnp.dot(a, b, preferred_element_type=F32)  31.5 us
    convert_element_type x1, other arithmetic, body(): grad_gateup = gather_abs(up_rows, [c_bit], 1).astype(F32)  27.1 us
    dot_general x10, matrix products, t_dot(): lax.dot_general(a, b, (((0,), (0,)), ((), ())), preferred_element_type=F32)  26.1 us
  transfers between devices with their start and end apart: 77, of which 29 were waited for; matrix products, arithmetic and copies ran while one was open for 28% of the time, Pallas kernels for 0%

profile of v1, /device:TPU:0, one launch (start us, length us, event | category | flops | bytes accessed | tf_op | source)
XLA Modules:
  0.0 955.3 jit_solution(11124305891210778637)
XLA Ops:
  44.5 11.5 %collective-permute-done.4 = bf16[2,256,256]{1,2,0:T(8,128)(2,1)S(1)} collective-permute-done((bf16[2,256,256]{1,2,0:T(8,128)(2,1)S(1)}, bf16[2,256,256]{1,2,0:T(8,128)(2,1)S(1)}, u32[]{:S(2)}, u32[]{:S(2)}) %collective-permute-start.4) | collective-permute-done | bytes 262176 | tf_op jit(solution)/shard_map/ppermute | solution.py:81
  58.6 10.3 %collective-permute-done.5 = bf16[4,256,256]{1,2,0:T(8,128)(2,1)S(1)} collective-permute-done((bf16[4,256,256]{1,2,0:T(8,128)(2,1)S(1)}, bf16[4,256,256]{1,2,0:T(8,128)(2,1)S(1)}, u32[]{:S(2)}, u32[]{:S(2)}) %collective-permute-start.5) | collective-permute-done | bytes 524320 | tf_op jit(solution)/shard_map/ppermute | solution.py:81
  78.1 8.7 collective-permute-done.11
  151.5 16.6 %collective-permute-done.13 = bf16[1,128,1536]{2,1,0:T(8,128)(2,1)} collective-permute-done((bf16[1,128,1536]{2,1,0:T(8,128)(2,1)}, bf16[1,128,1536]{2,1,0:T(8,128)(2,1)}, u32[]{:S(2)}, u32[]{:S(2)}) %collective-permute-start.13) | collective-permute-done | bytes 393248 | tf_op jit(solution)/shard_map/ppermute | solution.py:81
  176.0 8.2 collective-permute-done.16
  194.7 17.2 %fusion.72 = f32[1024,2304]{1,0:T(8,128)} fusion(bf16[512,1536]{1,0:T(8,128)(2,1)} %bitcast.315, bf16[512,1536]{1,0:T(8,128)(2,1)} %bitcast.321, bf16[768,2304]{1,0:T(8,128)(2,1)} %maximum_select_fusion.6, bf16[768,1152]{1,0:T(8,128)(2,1)} %get-tuple-element.50, bf16[768,1152]{1,0:T(8,128)(2,1)} %get-tuple-element.49, pred[]{:T(512)S(6)} %eq.35), kind=kOutput, calls=%fused_computation.170 | convolution fusion | flops 7300055040 | bytes 19660800 | tf_op jit(solution)/shard_map/dot_general | solution.py:59
  211.9 13.6 %fusion.10 = (bf16[1024,1152]{1,0:T(8,128)(2,1)}, bf16[1024,1152]{1,0:T(8,128)(2,1)}, bf16[1024,1152]{1,0:T(8,128)(2,1)}) fusion(f32[1024,2304]{1,0:T(8,128)} %fusion.72, bf16[2304,1536]{1,0:T(8,128)(2,1)} %param.21, s32[]{:T(128)S(6)} %select_n.552, bf16[512,1536]{1,0:T(8,128)(2,1)} %bitcast.312, bf16[512,1536]{1,0:T(8,128)(2,1)} %bitcast.318), kind=kOutput, calls=%fused_computation.28 | convolution fusion | flops 3660840960 | bytes 23199748 | tf_op jit(solution)/shard_map/dot_general | solution.py:63
  225.5 16.6 %fusion.15 = bf16[1024,1536]{1,0:T(8,128)(2,1)} fusion(bf16[1024,1152]{1,0:T(8,128)(2,1)} %get-tuple-element.48, bf16[1024,1152]{1,0:T(8,128)(2,1)} %get-tuple-element.47, bf16[768,2304]{1,0:T(8,128)(2,1)} %maximum_select_fusion.6, bf16[768,1152]{1,0:T(8,128)(2,1)} %get-tuple-element.50, bf16[768,1152]{1,0:T(8,128)(2,1)} %get-tuple-element.49, pred[]{:T(512)S(6)} %eq.35), kind=kOutput, calls=%fused_computation.45 | convolution fusion | flops 7304773632 | bytes 14942209 | tf_op jit(solution)/shard_map/dot_general | solution.py:63
  245.9 6.7 convolution_convert_fusion.2
  265.6 16.8 %collective-permute-done.27 = bf16[2,128,1536]{2,1,0:T(8,128)(2,1)S(1)} collective-permute-done((bf16[2,128,1536]{2,1,0:T(8,128)(2,1)S(1)}, bf16[2,128,1536]{2,1,0:T(8,128)(2,1)S(1)}, u32[]{:S(2)}, u32[]{:S(2)}) %collective-permute-start.27) | collective-permute-done | bytes 786464 | tf_op jit(solution)/shard_map/ppermute | solution.py:81
  285.8 13.5 %collective-permute-done.19 = bf16[2,128,1536]{2,1,0:T(8,128)(2,1)S(1)} collective-permute-done((bf16[2,128,1536]{2,1,0:T(8,128)(2,1)S(1)}, bf16[2,128,1536]{2,1,0:T(8,128)(2,1)S(1)}, u32[]{:S(2)}, u32[]{:S(2)}) %collective-permute-start.19) | collective-permute-done | bytes 786464 | tf_op jit(solution)/shard_map/ppermute | solution.py:81
  311.1 6.3 convolution_convert_fusion.9
  319.7 10.3 %fusion.23 = bf16[1280,128]{1,0:T(8,128)(2,1)} fusion(bf16[12,256,128]{1,2,0:T(8,128)(2,1)} %bitcast.306, f32[12,256,1280]{2,1,0:T(8,128)} %copy-done.1, f32[12,256]{1,0:T(8,128)S(1)} %copy-done.66, pred[256,1280]{1,0:T(8,128)(4,1)S(1)} %fusion.67), kind=kOutput, calls=%fused_computation.75 | convolution fusion | flops 1018593280 | bytes 17182720 | tf_op jit(solution)/shard_map/hqk,hqd->kd/dot_general | solution.py:388
  330.1 12.1 %multiply_reduce_fusion = (f32[12,256]{1,0:T(8,128)S(1)}, f32[12,256,1280]{2,1,0:T(8,128)}) fusion(f32[12,256,1280]{2,1,0:T(8,128)} %copy-done.1, f32[12,256]{1,0:T(8,128)S(1)} %copy-done.66, pred[256,1280]{1,0:T(8,128)(4,1)S(1)} %fusion.67, bf16[12,256,128]{1,2,0:T(8,128)(2,1)S(1)} %bitcast.307, bf16[1280,256]{1,0:T(8,128)(2,1)S(1)} %copy-done.11), kind=kOutput, calls=%fused_computation.5 | convolution fusion | flops 1022358528 | bytes 32927744 | tf_op jit(solution)/shard_map/hqd,kd->hqk/dot_general | solution.py:383
  342.2 7.7 multiply_convert_fusion
  388.5 6.3 add_convert_fusion
  401.8 7.5 collective-permute-done.71
  412.9 54.1 %collective-permute-done.32 = bf16[4,256,256]{1,2,0:T(8,128)(2,1)S(1)} collective-permute-done((bf16[4,256,256]{1,2,0:T(8,128)(2,1)S(1)}, bf16[4,256,256]{1,2,0:T(8,128)(2,1)S(1)}, u32[]{:S(2)}, u32[]{:S(2)}) %collective-permute-start.32) | collective-permute-done | bytes 524320 | tf_op jit(solution)/shard_map/ppermute | solution.py:81
  470.8 31.1 %collective-permute-done.33 = bf16[2,256,256]{1,2,0:T(8,128)(2,1)S(1)} collective-permute-done((bf16[2,256,256]{1,2,0:T(8,128)(2,1)S(1)}, bf16[2,256,256]{1,2,0:T(8,128)(2,1)S(1)}, u32[]{:S(2)}, u32[]{:S(2)}) %collective-permute-start.33) | collective-permute-done | bytes 262176 | tf_op jit(solution)/shard_map/ppermute | solution.py:81
  507.9 22.4 %collective-permute-done.64 = bf16[2,192,1152]{2,1,0:T(8,128)(2,1)S(1)} collective-permute-done((bf16[2,192,1152]{2,1,0:T(8,128)(2,1)S(1)}, bf16[2,192,1152]{2,1,0:T(8,128)(2,1)S(1)}, u32[]{:S(2)}, u32[]{:S(2)}) %collective-permute-start.64) | collective-permute-done | bytes 884768 | tf_op jit(solution)/shard_map/ppermute | solution.py:81
  543.2 35.5 %collective-permute-done.66 = bf16[1,192,2,1152]{3,1,2,0:T(8,128)(2,1)S(1)} collective-permute-done((bf16[1,192,2,1152]{3,1,2,0:T(8,128)(2,1)S(1)}, bf16[1,192,2,1152]{3,1,2,0:T(8,128)(2,1)S(1)}, u32[]{:S(2)}, u32[]{:S(2)}) %collective-permute-start.66) | collective-permute-done | bytes 884768 | tf_op jit(solution)/shard_map/ppermute | solution.py:81
  586.6 49.9 %collective-permute-done.47 = bf16[2,96,128]{2,1,0:T(8,128)(2,1)S(1)} collective-permute-done((bf16[2,96,128]{2,1,0:T(8,128)(2,1)S(1)}, bf16[2,96,128]{2,1,0:T(8,128)(2,1)S(1)}, u32[]{:S(2)}, u32[]{:S(2)}) %collective-permute-start.47) | collective-permute-done | bytes 49184 | tf_op jit(solution)/shard_map/ppermute | solution.py:81
  650.2 83.7 %collective-permute-done.55 = bf16[2,2,96,768]{3,2,1,0:T(8,128)(2,1)S(1)} collective-permute-done((bf16[2,2,96,768]{3,2,1,0:T(8,128)(2,1)S(1)}, bf16[2,2,96,768]{3,2,1,0:T(8,128)(2,1)S(1)}, u32[]{:S(2)}, u32[]{:S(2)}) %collective-permute-start.55) | collective-permute-done | bytes 589856 | tf_op jit(solution)/shard_map/ppermute | solution.py:81
  735.8 10.6 %collective-permute-done.37 = bf16[2,2,96,768]{3,2,1,0:T(8,128)(2,1)S(1)} collective-permute-done((bf16[2,2,96,768]{3,2,1,0:T(8,128)(2,1)S(1)}, bf16[2,2,96,768]{3,2,1,0:T(8,128)(2,1)S(1)}, u32[]{:S(2)}, u32[]{:S(2)}) %collective-permute-start.37) | collective-permute-done | bytes 589856 | tf_op jit(solution)/shard_map/ppermute | solution.py:81
  760.9 7.3 collective-permute-done.39
  772.0 10.3 %copy.94 = bf16[768,2,2,1152]{0,3,2,1:T(8,128)(2,1)} copy(bf16[768,2,2,1152]{3,0,2,1:T(8,128)(2,1)} %maximum_select_fusion.2) | data formatting | bytes 14155776 | tf_op jit(solution)/shard_map/jit(_where)/select_n | solution.py:105
  808.1 12.4 %collective-permute-done.42 = bf16[4,1,96,768]{3,2,1,0:T(8,128)(2,1)S(1)} collective-permute-done((bf16[4,1,96,768]{3,2,1,0:T(8,128)(2,1)S(1)}, bf16[4,1,96,768]{3,2,1,0:T(8,128)(2,1)S(1)}, u32[]{:S(2)}, u32[]{:S(2)}) %collective-permute-start.42) | collective-permute-done | bytes 589856 | tf_op jit(solution)/shard_map/ppermute | solution.py:81
  821.6 10.4 %collective-permute-done.60 = bf16[4,1,96,768]{3,2,1,0:T(8,128)(2,1)S(1)} collective-permute-done((bf16[4,1,96,768]{3,2,1,0:T(8,128)(2,1)S(1)}, bf16[4,1,96,768]{3,2,1,0:T(8,128)(2,1)S(1)}, u32[]{:S(2)}, u32[]{:S(2)}) %collective-permute-start.60) | collective-permute-done | bytes 589856 | tf_op jit(solution)/shard_map/ppermute | solution.py:81
  836.5 39.3 %psum.7 = f32[2,1536]{1,0:T(2,128)S(1)} all-reduce(f32[2,1536]{1,0:T(2,128)S(1)} %pad_maximum_fusion.35), channel_id=1, replica_groups=mesh['z'=4,'x'=2,'c'=2,'y'=2] {'z','x','c','y'}, use_global_device_ids=true, to_apply=%region_15.16 | all-reduce | flops 3072 | bytes 24576 | tf_op jit(solution)/shard_map/psum | solution.py:417
  888.3 11.6 %fusion.3 = f32[2304,1536]{1,0:T(8,128)} fusion(bf16[2304,768]{1,0:T(8,128)(2,1)} %collective-permute-done.76, bf16[2304,768]{1,0:T(8,128)(2,1)} %broadcast_select_fusion, pred[]{:T(512)S(6)} %eq.36), kind=kLoop, calls=%fused_computation.18 | loop fusion | flops 35389440 | bytes 21233664 | tf_op jit(solution)/shard_map/convert_element_type | solution.py:331
  900.0 27.1 %fusion = f32[768,9216]{0,1:T(8,128)} fusion(bf16[768,4608]{0,1:T(8,128)(2,1)} %collective-permute-done.69, bf16[768,4608]{0,1:T(8,128)(2,1)} %bitcast.288, pred[]{:T(512)S(6)} %eq.36), kind=kLoop, calls=%fused_computation.9 | loop fusion | flops 70778880 | bytes 42467328 | tf_op jit(solution)/shard_map/convert_element_type | solution.py:348
  927.0 27.7 %copy.95 = f32[768,9216]{1,0:T(8,128)} copy(f32[768,9216]{0,1:T(8,128)} %fusion) | data formatting | bytes 56623104
  (559 shorter events, 327.4 us)
Async XLA Ops:
  8.7 48.8 %collective-permute-start.7 = (bf16[1,192,1536]{2,1,0:T(8,128)(2,1)}, bf16[1,192,1536]{2,1,0:T(8,128)(2,1)}, u32[]{:S(2)}, u32[]{:S(2)}) collective-permute-start(bf16[1,192,1536]{2,1,0:T(8,128)(2,1)} %dynamic-slice_bitcast_fusion.12), channel_id=1, source_target_pairs={{0,1},{1,0},{2,3},{3,2},{4,5},{5,4},{6,7},{7,6},{8,9},{9,8},{10,11... | collective-permute-start | bytes 1769480 | tf_op jit(solution)/shard_map/ppermute | solution.py:81
  12.8 57.9 %collective-permute-start.10 = (bf16[1,192,1536]{2,1,0:T(8,128)(2,1)}, bf16[1,192,1536]{2,1,0:T(8,128)(2,1)}, u32[]{:S(2)}, u32[]{:S(2)}) collective-permute-start(bf16[1,192,1536]{2,1,0:T(8,128)(2,1)} %dynamic-slice_bitcast_fusion.11), channel_id=1, source_target_pairs={{0,1},{1,0},{2,3},{3,2},{4,5},{5,4},{6,7},{7,6},{8,9},{9,8},{10,11... | collective-permute-start | bytes 1769480 | tf_op jit(solution)/shard_map/ppermute | solution.py:81
  16.6 123.9 %collective-permute-start.17 = (bf16[384,2304]{1,0:T(8,128)(2,1)}, bf16[384,2304]{1,0:T(8,128)(2,1)}, u32[]{:S(2)}, u32[]{:S(2)}) collective-permute-start(bf16[384,2304]{1,0:T(8,128)(2,1)} %pad_maximum_fusion.4), channel_id=1, source_target_pairs={{0,1},{1,0},{2,3},{3,2},{4,5},{5,4},{6,7},{7,6},{8,9},{9,8},{10,11... | collective-permute-start | bytes 5308424 | tf_op jit(solution)/shard_map/ppermute | solution.py:192
  28.3 108.7 %collective-permute-start.25 = (bf16[1,128,1536]{2,1,0:T(8,128)(2,1)S(1)}, bf16[1,128,1536]{2,1,0:T(8,128)(2,1)}, u32[]{:S(2)}, u32[]{:S(2)}) collective-permute-start(bf16[1,128,1536]{2,1,0:T(8,128)(2,1)S(1)} %get-tuple-element.81), channel_id=1, source_target_pairs={{0,4},{4,0},{1,5},{5,1},{2,6},{6,2},{3,7},{7,3},{8,12},{12,8},{9,1... | collective-permute-start | bytes 1179656 | tf_op jit(solution)/shard_map/ppermute | solution.py:81
  86.8 54.3 %collective-permute-start.23 = (bf16[1,128,1536]{2,1,0:T(8,128)(2,1)S(1)}, bf16[1,128,1536]{2,1,0:T(8,128)(2,1)}, u32[]{:S(2)}, u32[]{:S(2)}) collective-permute-start(bf16[1,128,1536]{2,1,0:T(8,128)(2,1)S(1)} %get-tuple-element.80), channel_id=1, source_target_pairs={{0,1},{1,0},{2,3},{3,2},{4,5},{5,4},{6,7},{7,6},{8,9},{9,8},{10,11... | collective-permute-start | bytes 1179656 | tf_op jit(solution)/shard_map/ppermute | solution.py:81
  140.5 49.4 %collective-permute-start.18 = (bf16[384,2304]{1,0:T(8,128)(2,1)}, bf16[384,2304]{1,0:T(8,128)(2,1)}, u32[]{:S(2)}, u32[]{:S(2)}) collective-permute-start(bf16[384,2304]{1,0:T(8,128)(2,1)} %collective-permute-done.17), channel_id=1, source_target_pairs={{0,2},{2,0},{1,3},{3,1},{4,6},{6,4},{5,7},{7,5},{8,10},{10,8},{9,1... | collective-permute-start | bytes 5308424 | tf_op jit(solution)/shard_map/ppermute | solution.py:81
  264.9 123.6 %collective-permute-start.62 = (bf16[1536,1152]{1,0:T(8,128)(2,1)}, bf16[1536,1152]{1,0:T(8,128)(2,1)}, u32[]{:S(2)}, u32[]{:S(2)}) collective-permute-start(bf16[1536,1152]{1,0:T(8,128)(2,1)} %convolution_convert_fusion), channel_id=1, source_target_pairs={{0,2},{2,0},{1,3},{3,1},{4,6},{6,4},{5,7},{7,5},{8,10},{10,8},{9,1... | collective-permute-start | bytes 10616840 | tf_op jit(solution)/shard_map/ppermute | solution.py:81
  264.9 117.2 %collective-permute-start.70 = (bf16[1152,768]{1,0:T(8,128)(2,1)}, bf16[1152,768]{1,0:T(8,128)(2,1)}, u32[]{:S(2)}, u32[]{:S(2)}) collective-permute-start(bf16[1152,768]{1,0:T(8,128)(2,1)} %convolution_convert_fusion.3), channel_id=1, source_target_pairs={{0,2},{2,0},{1,3},{3,1},{4,6},{6,4},{5,7},{7,5},{8,10},{10,8},{9,1... | collective-permute-start | bytes 5308424 | tf_op jit(solution)/shard_map/ppermute | solution.py:81
  299.3 99.5 %collective-permute-start.22 = (bf16[1,128,1536]{2,1,0:T(8,128)(2,1)}, bf16[1,128,1536]{2,1,0:T(8,128)(2,1)}, u32[]{:S(2)}, u32[]{:S(2)}) collective-permute-start(bf16[1,128,1536]{2,1,0:T(8,128)(2,1)} %slice.283), channel_id=1, source_target_pairs={{0,4},{4,0},{1,5},{5,1},{2,6},{6,2},{3,7},{7,3},{8,12},{12,8},{9,1... | collective-permute-start | bytes 1179656 | tf_op jit(solution)/shard_map/ppermute | solution.py:81
  307.7 72.0 %collective-permute-start.20 = (bf16[1,128,1536]{2,1,0:T(8,128)(2,1)}, bf16[1,128,1536]{2,1,0:T(8,128)(2,1)}, u32[]{:S(2)}, u32[]{:S(2)}) collective-permute-start(bf16[1,128,1536]{2,1,0:T(8,128)(2,1)} %slice.279), channel_id=1, source_target_pairs={{0,1},{1,0},{2,3},{3,2},{4,5},{5,4},{6,7},{7,6},{8,9},{9,8},{10,11... | collective-permute-start | bytes 1179656 | tf_op jit(solution)/shard_map/ppermute | solution.py:81
  379.8 159.7 %collective-permute-start.53 = (bf16[1536,768]{1,0:T(8,128)(2,1)S(1)}, bf16[1536,768]{1,0:T(8,128)(2,1)S(1)}, u32[]{:S(2)}, u32[]{:S(2)}) collective-permute-start(bf16[1536,768]{1,0:T(8,128)(2,1)S(1)} %convolution_convert_fusion.5), channel_id=1, source_target_pairs={{0,2},{2,0},{1,3},{3,1},{4,6},{6,4},{5,7},{7,5},{8,10},{10,8},{9,1... | collective-permute-start | bytes 7077896 | tf_op jit(solution)/shard_map/ppermute | solution.py:81
  395.0 74.8 %collective-permute-start.63 = (bf16[2,2,192,1152]{3,2,1,0:T(8,128)(2,1)S(1)}, bf16[2,2,192,1152]{3,2,1,0:T(8,128)(2,1)S(1)}, u32[]{:S(2)}, u32[]{:S(2)}) collective-permute-start(bf16[2,2,192,1152]{3,2,1,0:T(8,128)(2,1)S(1)} %dynamic-slice_bitcast_fusion), channel_id=1, source_target_pairs={{0,8},{8,0},{16,24},{24,16},{1,9},{9,1},{17,25},{25,17},{2,10},{10... | collective-permute-start | bytes 5308424 | tf_op jit(solution)/shard_map/ppermute | solution.py:81
  397.1 185.6 %collective-permute-start.35 = (bf16[1536,768]{1,0:T(8,128)(2,1)S(1)}, bf16[1536,768]{1,0:T(8,128)(2,1)S(1)}, u32[]{:S(2)}, u32[]{:S(2)}) collective-permute-start(bf16[1536,768]{1,0:T(8,128)(2,1)S(1)} %convolution_convert_fusion.7), channel_id=1, source_target_pairs={{0,2},{2,0},{1,3},{3,1},{4,6},{6,4},{5,7},{7,5},{8,10},{10,8},{9,1... | collective-permute-start | bytes 7077896 | tf_op jit(solution)/shard_map/ppermute | solution.py:81
  398.8 68.1 %collective-permute-start.32 = (bf16[4,256,256]{1,2,0:T(8,128)(2,1)S(1)}, bf16[4,256,256]{1,2,0:T(8,128)(2,1)S(1)}, u32[]{:S(2)}, u32[]{:S(2)}) collective-permute-start(bf16[4,256,256]{1,2,0:T(8,128)(2,1)S(1)} %slice.297), channel_id=1, source_target_pairs={{0,8},{8,0},{16,24},{24,16},{1,9},{9,1},{17,25},{25,17},{2,10},{10... | collective-permute-start | bytes 1572872 | tf_op jit(solution)/shard_map/ppermute | solution.py:81
  409.5 94.0 %collective-permute-start.72 = (bf16[288,768]{1,0:T(8,128)(2,1)S(1)}, bf16[288,768]{1,0:T(8,128)(2,1)S(1)}, u32[]{:S(2)}, u32[]{:S(2)}) collective-permute-start(bf16[288,768]{1,0:T(8,128)(2,1)S(1)} %dynamic-slice_bitcast_fusion.17), channel_id=1, source_target_pairs={{0,16},{8,24},{16,0},{24,8},{1,17},{9,25},{17,1},{25,9},{2,18},{10... | collective-permute-start | bytes 1327112 | tf_op jit(solution)/shard_map/ppermute | solution.py:81
  470.4 59.9 %collective-permute-start.64 = (bf16[2,192,1152]{2,1,0:T(8,128)(2,1)S(1)}, bf16[2,192,1152]{2,1,0:T(8,128)(2,1)S(1)}, u32[]{:S(2)}, u32[]{:S(2)}) collective-permute-start(bf16[2,192,1152]{2,1,0:T(8,128)(2,1)S(1)} %dynamic-slice_bitcast_fusion.8), channel_id=1, source_target_pairs={{0,16},{8,24},{16,0},{24,8},{1,17},{9,25},{17,1},{25,9},{2,18},{10... | collective-permute-start | bytes 2654216 | tf_op jit(solution)/shard_map/ppermute | solution.py:81
  503.6 75.3 %collective-permute-start.73 = (bf16[1,288,768]{2,1,0:T(8,128)(2,1)S(1)}, bf16[1,288,768]{2,1,0:T(8,128)(2,1)S(1)}, u32[]{:S(2)}, u32[]{:S(2)}) collective-permute-start(bf16[1,288,768]{2,1,0:T(8,128)(2,1)S(1)} %fusion.79), channel_id=1, source_target_pairs={{0,16},{8,24},{16,0},{24,8},{1,17},{9,25},{17,1},{25,9},{2,18},{10... | collective-permute-start | bytes 1327112 | tf_op jit(solution)/shard_map/ppermute | solution.py:81
  540.4 105.0 %collective-permute-start.54 = (bf16[768,768]{1,0:T(8,128)(2,1)S(1)}, bf16[768,768]{1,0:T(8,128)(2,1)S(1)}, u32[]{:S(2)}, u32[]{:S(2)}) collective-permute-start(bf16[768,768]{1,0:T(8,128)(2,1)S(1)} %dynamic-slice_bitcast_fusion.1), channel_id=1, source_target_pairs={{0,1},{1,0},{2,3},{3,2},{4,5},{5,4},{6,7},{7,6},{8,9},{9,8},{10,11... | collective-permute-start | bytes 3538952 | tf_op jit(solution)/shard_map/ppermute | solution.py:81
  578.8 61.4 %collective-permute-start.67 = (bf16[2,192,2,1152]{3,1,2,0:T(8,128)(2,1)S(1)}, bf16[2,192,2,1152]{3,1,2,0:T(8,128)(2,1)S(1)}, u32[]{:S(2)}, u32[]{:S(2)}) collective-permute-start(bf16[2,192,2,1152]{3,1,2,0:T(8,128)(2,1)S(1)} %pad_maximum_fusion.5), channel_id=1, source_target_pairs={{0,8},{8,0},{16,24},{24,16},{1,9},{9,1},{17,25},{25,17},{2,10},{10... | collective-permute-start | bytes 5308424 | tf_op jit(solution)/shard_map/ppermute | solution.py:81
  579.0 61.1 %collective-permute-start.74 = (bf16[2,288,768]{2,1,0:T(8,128)(2,1)S(1)}, bf16[2,288,768]{2,1,0:T(8,128)(2,1)S(1)}, u32[]{:S(2)}, u32[]{:S(2)}) collective-permute-start(bf16[2,288,768]{2,1,0:T(8,128)(2,1)S(1)} %pad_maximum_fusion.16), channel_id=1, source_target_pairs={{0,8},{8,0},{16,24},{24,16},{1,9},{9,1},{17,25},{25,17},{2,10},{10... | collective-permute-start | bytes 2654216 | tf_op jit(solution)/shard_map/ppermute | solution.py:81
  585.9 50.6 %collective-permute-start.47 = (bf16[2,96,128]{2,1,0:T(8,128)(2,1)S(1)}, bf16[2,96,128]{2,1,0:T(8,128)(2,1)S(1)}, u32[]{:S(2)}, u32[]{:S(2)}) collective-permute-start(bf16[2,96,128]{2,1,0:T(8,128)(2,1)S(1)} %dynamic-slice_bitcast_fusion.35), channel_id=1, source_target_pairs={{0,8},{8,0},{16,24},{24,16},{1,9},{9,1},{17,25},{25,17},{2,10},{10... | collective-permute-start | bytes 147464 | tf_op jit(solution)/shard_map/ppermute | solution.py:81
  586.1 60.3 %collective-permute-start.36 = (bf16[768,768]{1,0:T(8,128)(2,1)S(1)}, bf16[768,768]{1,0:T(8,128)(2,1)S(1)}, u32[]{:S(2)}, u32[]{:S(2)}) collective-permute-start(bf16[768,768]{1,0:T(8,128)(2,1)S(1)} %dynamic-slice_bitcast_fusion.2), channel_id=1, source_target_pairs={{0,1},{1,0},{2,3},{3,2},{4,5},{5,4},{6,7},{7,6},{8,9},{9,8},{10,11... | collective-permute-start | bytes 3538952 | tf_op jit(solution)/shard_map/ppermute | solution.py:81
  637.2 145.1 %collective-permute-start.48 = (bf16[96,128]{1,0:T(8,128)(2,1)}, bf16[96,128]{1,0:T(8,128)(2,1)}, u32[]{:S(2)}, u32[]{:S(2)}) collective-permute-start(bf16[96,128]{1,0:T(8,128)(2,1)} %dynamic-slice_bitcast_fusion.40), channel_id=1, source_target_pairs={{0,16},{8,24},{16,0},{24,8},{1,17},{9,25},{17,1},{25,9},{2,18},{10... | collective-permute-start | bytes 73736 | tf_op jit(solution)/shard_map/ppermute | solution.py:81
  641.7 126.7 %collective-permute-start.68 = (bf16[768,2,1,1152]{3,0,2,1:T(8,128)(2,1)S(1)}, bf16[768,2,1,1152]{3,0,2,1:T(8,128)(2,1)S(1)}, u32[]{:S(2)}, u32[]{:S(2)}) collective-permute-start(bf16[768,2,1,1152]{3,0,2,1:T(8,128)(2,1)S(1)} %maximum_bitcast_fusion), channel_id=1, source_target_pairs={{0,4},{4,0},{1,5},{5,1},{2,6},{6,2},{3,7},{7,3},{8,12},{12,8},{9,1... | collective-permute-start | bytes 10616840 | tf_op jit(solution)/shard_map/ppermute | solution.py:81
  645.8 88.1 %collective-permute-start.55 = (bf16[2,2,96,768]{3,2,1,0:T(8,128)(2,1)S(1)}, bf16[2,2,96,768]{3,2,1,0:T(8,128)(2,1)S(1)}, u32[]{:S(2)}, u32[]{:S(2)}) collective-permute-start(bf16[2,2,96,768]{3,2,1,0:T(8,128)(2,1)S(1)} %dynamic-slice_bitcast_fusion.9), channel_id=1, source_target_pairs={{0,4},{4,0},{1,5},{5,1},{2,6},{6,2},{3,7},{7,3},{8,12},{12,8},{9,1... | collective-permute-start | bytes 1769480 | tf_op jit(solution)/shard_map/ppermute | solution.py:81
  646.7 99.7 %collective-permute-start.37 = (bf16[2,2,96,768]{3,2,1,0:T(8,128)(2,1)S(1)}, bf16[2,2,96,768]{3,2,1,0:T(8,128)(2,1)S(1)}, u32[]{:S(2)}, u32[]{:S(2)}) collective-permute-start(bf16[2,2,96,768]{3,2,1,0:T(8,128)(2,1)S(1)} %dynamic-slice_bitcast_fusion.10), channel_id=1, source_target_pairs={{0,4},{4,0},{1,5},{5,1},{2,6},{6,2},{3,7},{7,3},{8,12},{12,8},{9,1... | collective-permute-start | bytes 1769480 | tf_op jit(solution)/shard_map/ppermute | solution.py:81
  649.6 140.4 %collective-permute-start.75 = (bf16[1152,768]{1,0:T(8,128)(2,1)}, bf16[1152,768]{1,0:T(8,128)(2,1)}, u32[]{:S(2)}, u32[]{:S(2)}) collective-permute-start(bf16[1152,768]{1,0:T(8,128)(2,1)} %pad_maximum_fusion.7), channel_id=1, source_target_pairs={{0,4},{4,0},{1,5},{5,1},{2,6},{6,2},{3,7},{7,3},{8,12},{12,8},{9,1... | collective-permute-start | bytes 5308424 | tf_op jit(solution)/shard_map/ppermute | solution.py:81
  782.3 117.7 %collective-permute-start.69 = (bf16[768,4608]{0,1:T(8,128)(2,1)}, bf16[768,4608]{0,1:T(8,128)(2,1)}, u32[]{:S(2)}, u32[]{:S(2)}) collective-permute-start(bf16[768,4608]{0,1:T(8,128)(2,1)} %bitcast.287), channel_id=1, source_target_pairs={{0,2},{2,0},{1,3},{3,1},{4,6},{6,4},{5,7},{7,5},{8,10},{10,8},{9,1... | collective-permute-start | bytes 21233672 | tf_op jit(solution)/shard_map/ppermute | solution.py:81
  797.3 91.1 %collective-permute-start.76 = (bf16[2304,768]{1,0:T(8,128)(2,1)}, bf16[2304,768]{1,0:T(8,128)(2,1)}, u32[]{:S(2)}, u32[]{:S(2)}) collective-permute-start(bf16[2304,768]{1,0:T(8,128)(2,1)} %broadcast_select_fusion), channel_id=1, source_target_pairs={{0,2},{2,0},{1,3},{3,1},{4,6},{6,4},{5,7},{7,5},{8,10},{10,8},{9,1... | collective-permute-start | bytes 10616840 | tf_op jit(solution)/shard_map/ppermute | solution.py:81
  821.6 56.0 %collective-permute-start.43 = (bf16[768,768]{1,0:T(8,128)(2,1)}, bf16[768,768]{1,0:T(8,128)(2,1)}, u32[]{:S(2)}, u32[]{:S(2)}) collective-permute-start(bf16[768,768]{1,0:T(8,128)(2,1)} %bitcast.76), channel_id=1, source_target_pairs={{0,2},{2,0},{1,3},{3,1},{4,6},{6,4},{5,7},{7,5},{8,10},{10,8},{9,1... | collective-permute-start | bytes 3538952 | tf_op jit(solution)/shard_map/ppermute | solution.py:81
  833.1 49.8 %collective-permute-start.61 = (bf16[768,768]{1,0:T(8,128)(2,1)}, bf16[768,768]{1,0:T(8,128)(2,1)}, u32[]{:S(2)}, u32[]{:S(2)}) collective-permute-start(bf16[768,768]{1,0:T(8,128)(2,1)} %bitcast.111), channel_id=1, source_target_pairs={{0,2},{2,0},{1,3},{3,1},{4,6},{6,4},{5,7},{7,5},{8,10},{10,8},{9,1... | collective-permute-start | bytes 3538952 | tf_op jit(solution)/shard_map/ppermute | solution.py:81
  836.0 40.6 %collective-permute-start.52 = (bf16[768,128]{1,0:T(8,128)(2,1)S(1)}, bf16[768,128]{1,0:T(8,128)(2,1)S(1)}, u32[]{:S(2)}, u32[]{:S(2)}) collective-permute-start(bf16[768,128]{1,0:T(8,128)(2,1)S(1)} %bitcast.331), channel_id=1, source_target_pairs={{0,2},{2,0},{1,3},{3,1},{4,6},{6,4},{5,7},{7,5},{8,10},{10,8},{9,1... | collective-permute-start | bytes 589832 | tf_op jit(solution)/shard_map/ppermute | solution.py:81
  (151 other events, 1965.6 us)

commit v2 on v0

v2 whole, which is shorter than its diff:
```python
import functools
import math

import jax
import jax.numpy as jnp
from jax import lax
from jax.experimental import pallas as pl
from jax.experimental.pallas import tpu as pltpu
from jax.sharding import Mesh
from jax.sharding import PartitionSpec as P

H = 12
HD = 128
FF = 4608
WINDOW = 1024
EPSILON = 1e-06
BF = jnp.bfloat16
F32 = jnp.float32
VMEM_LIMIT = 48 * 1024 * 1024


def tables(places, width):
    half_width = width // 2
    frequency = jnp.exp(
        jnp.arange(half_width, dtype=jnp.float32) * (-2.0 * math.log(10000.0) / width)
    )
    angles = places.astype(jnp.float32)[:, None] * frequency[None, :]
    return (jnp.cos(angles), jnp.sin(angles))


def rotate(values, cosine, sine):
    turned = jnp.concatenate([values[:, HD // 2 :], values[:, : HD // 2]], axis=1)
    return values * cosine + turned * sine


def rms_factor(values):
    return lax.rsqrt(jnp.mean(values * values, axis=-1, keepdims=True) + EPSILON)


def norm_back(grad_normed, values, factor, gain):
    scaled = grad_normed * gain
    return factor * scaled - values * factor**3 * jnp.mean(scaled * values, axis=-1, keepdims=True)


def segment_info(places, seq_lengths):
    seq_ends = jnp.cumsum(seq_lengths)
    passed = places[:, None] >= seq_ends[None, :]
    segment = jnp.sum(passed.astype(jnp.int32), axis=1)
    seq_start = jnp.sum(jnp.where(passed, seq_lengths[None, :], 0), axis=1)
    return (segment, places - seq_start)


def dot(a, b):
    return jnp.dot(a, b, preferred_element_type=F32)


def dot_t(a, b):
    return lax.dot_general(a, b, (((1,), (1,)), ((), ())), preferred_element_type=F32)


def t_dot(a, b):
    return lax.dot_general(a, b, (((0,), (0,)), ((), ())), preferred_element_type=F32)


def after(value, *earlier):
    return lax.optimization_barrier((value,) + earlier)[0]


def shift(array, axis, mask):
    return lax.ppermute(array, axis, [(i, i ^ mask) for i in range(lax.axis_size(axis))])


def bit(axis, k=0):
    return (lax.axis_index(axis) >> k) & 1


def pick(array, index, dim):
    return lax.dynamic_index_in_dim(array, index, dim, keepdims=False)


def add(a, b):
    return (a.astype(F32) + b.astype(F32)).astype(BF)


def by_place(entries, axis_name):
    if len(entries) == 2:
        low, high = jnp.stack(entries), jnp.stack(entries[::-1])
        return jnp.where(lax.axis_index(axis_name) == 0, low, high)
    order = jnp.arange(len(entries), dtype=jnp.int32) ^ lax.axis_index(axis_name)
    return jnp.take(jnp.stack(entries), order, axis=0)


def kernel_call(function, **options):
    return pl.pallas_call(
        function,
        compiler_params=pltpu.CompilerParams(vmem_limit_bytes=VMEM_LIMIT),
        cost_estimate=pl.CostEstimate(flops=1000, bytes_accessed=1000, transcendentals=0),
        **options,
    )


def whole_spec(array):
    zeros = (0,) * array.ndim
    return pl.BlockSpec(array.shape, lambda *_: zeros)


ANY = pl.BlockSpec(memory_space=pl.ANY)


def load_rows(target, pieces, rows, sem):
    copies = []
    for n, piece in enumerate(pieces):
        start = pl.multiple_of(rows[n], 16)
        copies.append(
            pltpu.make_async_copy(piece, target.at[pl.ds(start, piece.shape[0])], sem.at[n])
        )
    for copy in copies:
        copy.start()
    return copies


def copy_kernel(blocks, spots, *refs):
    parts, out, sem = refs[:-2], refs[-2], refs[-1]
    copies = []
    for n, (part, rows, columns) in enumerate(blocks):
        at = [pl.multiple_of(spots[n, 0], 16), pl.multiple_of(spots[n, 1], 128)]
        to = [pl.multiple_of(spots[n, 2], 16), pl.multiple_of(spots[n, 3], 128)]
        copies.append(
            pltpu.make_async_copy(
                parts[part].at[pl.ds(at[0], rows), pl.ds(at[1], columns)],
                out.at[pl.ds(to[0], rows), pl.ds(to[1], columns)],
                sem.at[n],
            )
        )
    for copy in copies:
        copy.start()
    for copy in copies:
        copy.wait()


def lay_out(shape, parts, moves):
    aligned = all(size[0] % 16 == 0 and size[1] % 128 == 0 for _, size, _, _ in moves)
    if not aligned:
        out = jnp.zeros(shape, parts[0].dtype)
        for part, size, at, to in moves:
            out = lax.dynamic_update_slice(out, lax.dynamic_slice(parts[part], at, size), to)
        return out
    spots = jnp.stack(
        [jnp.stack([jnp.asarray(v, jnp.int32) for v in at + to]) for _, _, at, to in moves]
    )
    blocks = tuple((part,) + size for part, size, _, _ in moves)
    return kernel_call(
        functools.partial(copy_kernel, blocks),
        out_shape=jax.ShapeDtypeStruct(shape, parts[0].dtype),
        in_specs=[pl.BlockSpec(memory_space=pltpu.SMEM)] + [ANY] * len(parts),
        out_specs=pl.BlockSpec(memory_space=pltpu.VMEM),
        scratch_shapes=[pltpu.SemaphoreType.DMA((len(moves),))],
    )(spots, *parts)


def widen_kernel(maps, *refs):
    parts, out = refs[:4], refs[-1]
    source = pl.program_id(1) ^ maps[0]
    for n in range(4):

        @pl.when(source == n)
        def _(n=n):
            out[...] = parts[n][...].reshape(out.shape).astype(F32)


def widen(parts, z_places, out_shape, spot, so_far=None):
    z_count, rows, columns = parts[0].shape
    x_at, c_at = lax.axis_index("x"), lax.axis_index("c")
    if columns % 128 or rows % 16:
        out = jnp.zeros(out_shape, F32) if so_far is None else so_far
        ordered = jnp.stack(parts)
        for z in range(z_count):
            for c in range(2):
                for x in range(2):
                    block = ordered[(c * 2 + x) ^ (c_at * 2 + x_at), z_places[z]]
                    at = spot(z, c, x)
                    out = lax.dynamic_update_slice(
                        out, block.astype(F32), (at[0] * rows, at[1] * columns)
                    )
        return out
    maps = jnp.concatenate(
        [jnp.stack([c_at * 2 + x_at, lax.axis_index("y")]).astype(jnp.int32), z_places]
    )
    specs = [pl.BlockSpec((1, rows, columns), lambda z, k, maps: (maps[2 + z], 0, 0))] * 4
    operands = list(parts)
    aliases = {}
    if so_far is not None:
        specs.append(ANY)
        operands.append(so_far)
        aliases = {5: 0}
    return kernel_call(
        widen_kernel,
        grid_spec=pltpu.PrefetchScalarGridSpec(
            num_scalar_prefetch=1,
            grid=(z_count, 4),
            in_specs=specs,
            out_specs=pl.BlockSpec(
                (rows, columns), lambda z, k, maps: spot(z, k // 2, k % 2, maps[1])
            ),
        ),
        out_shape=jax.ShapeDtypeStruct(out_shape, F32),
        input_output_aliases=aliases,
    )(maps, *operands)


def attend_kernel(n_q, n_o, spans, maps, *refs):
    normed, tokens, gain, bias, cosine, sine = refs[:6]
    blocks = refs[6 : 6 + spans]
    at = 6 + spans
    q_pieces, o_pieces = refs[at : at + n_q], refs[at + n_q : at + n_q + n_o]
    queries, attended, hidden, own_norm, factor = refs[at + n_q + n_o : at + n_q + n_o + 5]
    w_q, w_o, keys, values, total, q_sem, o_sem = refs[at + n_q + n_o + 5 :]
    step = pl.program_id(0)
    rows = normed.shape[0]

    @pl.when(step == 0)
    def _():
        first = load_rows(w_q, q_pieces, [maps[spans + n] for n in range(n_q)], q_sem)
        second = load_rows(w_o, o_pieces, [maps[spans + n_q + n] for n in range(n_o)], o_sem)
        for n in range(spans):
            keys[n * rows : (n + 1) * rows, :] = blocks[n][0, :, :HD]
            values[n * rows : (n + 1) * rows, :] = blocks[n][0, :, HD:]
        total[...] = tokens[...].astype(F32)
        for copy in first + second:
            copy.wait()

    columns = pl.ds(pl.multiple_of(step * 2 * HD, 2 * HD), 2 * HD)
    raw = dot(normed[...], w_q[:, columns])
    done = []
    for n in range(2):
        turned = rotate(raw[:, n * HD : (n + 1) * HD], cosine[...], sine[...])
        query = (turned * HD ** (-0.5)).astype(BF)
        queries[:, n * HD : (n + 1) * HD] = query
        scores = dot_t(query, keys[...]) + bias[...]
        weights = jnp.exp(scores - jnp.max(scores, axis=-1, keepdims=True))
        share = 1.0 / jnp.sum(weights, axis=-1, keepdims=True)
        done.append(dot((weights * share).astype(BF), values[...]).astype(BF))
    both = jnp.concatenate(done, axis=1)
    attended[...] = both
    total[...] += dot(both, w_o[columns, :])

    @pl.when(step == pl.num_programs(0) - 1)
    def _():
        out = total[...]
        hidden[...] = out
        scale = rms_factor(out)
        factor[...] = jnp.broadcast_to(scale, factor.shape)
        own_norm[...] = (out * scale * gain[...]).astype(BF)


def attend_back_kernel(n_o, spans, entry_count, maps, *refs):
    d_attn, queries, bias, cosine, sine = refs[:5]
    blocks = refs[5 : 5 + spans]
    pieces = refs[5 + spans : 5 + spans + n_o]
    d_raw, kept, sent = refs[5 + spans + n_o : 8 + spans + n_o]
    w_o, keys, values, d_keys, d_values, d_window, sem = refs[8 + spans + n_o :]
    step = pl.program_id(0)
    rows = d_attn.shape[0]

    @pl.when(step == 0)
    def _():
        base = spans + entry_count
        copies = load_rows(w_o, pieces, [maps[base + n] for n in range(n_o)], sem)
        for n in range(spans):
            keys[n * rows : (n + 1) * rows, :] = blocks[n][0, :, :HD]
            values[n * rows : (n + 1) * rows, :] = blocks[n][0, :, HD:]
        d_keys[...] = jnp.zeros_like(d_keys)
        d_values[...] = jnp.zeros_like(d_values)
        for copy in copies:
            copy.wait()

    w_rows = pl.ds(pl.multiple_of(step * 2 * HD, 2 * HD), 2 * HD)
    d_both = dot_t(d_attn[...], w_o[w_rows, :]).astype(BF)
    for n in range(2):
        query = queries[:, n * HD : (n + 1) * HD]
        d_out = d_both[:, n * HD : (n + 1) * HD]
        scores = dot_t(query, keys[...]) + bias[...]
        weights = jnp.exp(scores - jnp.max(scores, axis=-1, keepdims=True))
        soft = weights * (1.0 / jnp.sum(weights, axis=-1, keepdims=True))
        d_soft = dot_t(d_out, values[...])
        delta = jnp.sum(soft * d_soft, axis=-1, keepdims=True)
        d_scores = (soft * (d_soft - delta)).astype(BF)
        d_query = dot(d_scores, keys[...]) * HD ** (-0.5)
        d_raw[:, n * HD : (n + 1) * HD] = rotate(d_query, cosine[...], -sine[...]).astype(BF)
        d_keys[...] += t_dot(query, d_scores)
        d_values[...] += t_dot(d_out, soft.astype(BF))

    @pl.when(step == pl.num_programs(0) - 1)
    def _():
        d_window[: spans * rows, :HD] = d_keys[...].T.astype(BF)
        d_window[: spans * rows, HD:] = d_values[...].T.astype(BF)
        d_window[spans * rows :, :] = jnp.zeros((rows, 2 * HD), BF)
        for n in range(entry_count):
            out = kept if n < entry_count // 2 else sent
            start = pl.multiple_of(maps[spans + n] * rows, rows)
            out[n % (entry_count // 2)] = d_window[pl.ds(start, rows), :]


ROOT = math.sqrt(2.0 / math.pi)


def forward_kernel(maps, normed, cot, w_gate, w_up, w_down, inner, d_both):
    gate, up = dot(normed[...], w_gate[...]), dot(normed[...], w_up[...])
    d_inner = dot_t(cot[...], w_down[...])
    square = gate * gate
    bent = jnp.tanh(ROOT * (gate + 0.044715 * (square * gate)))
    half = 0.5 * (1.0 + bent)
    active = gate * half
    slope = half + 0.5 * gate * (1.0 - bent * bent) * (ROOT * (1.0 + 3 * 0.044715 * square))
    inner[...] = (active * up).astype(BF)
    d_both[0] = (d_inner * up * slope).astype(BF)
    d_both[1] = (d_inner * active).astype(BF)


def cut_rows(result, outs):
    at = 0
    for out in outs:
        out[...] = result[at : at + out.shape[0]].astype(BF)
        at += out.shape[0]


def back_kernel(d_both, w_gu, *outs):
    units = d_both.shape[2]
    result = dot_t(d_both[0], w_gu[:, :units]) + dot_t(d_both[1], w_gu[:, units:])
    cut_rows(result, outs)


def down_kernel(maps, inner, w_down, *outs):
    cut_rows(dot(inner[...], w_down[...]), outs)


def grad_kernel(groups, block_rows, added, maps, left, right, *refs):
    result = t_dot(left[...], right[...].reshape(right.shape[-2:]))
    if added:
        result = result + refs[0][...].astype(F32)
    outs = refs[1:] if added else refs
    if groups is None:
        outs[0][...] = result.astype(BF)
        return
    total = outs[-1]
    total[...] = result
    place = 0
    for n, count in enumerate(groups):
        for k in range(count):
            start = pl.multiple_of(maps[2 + place] * block_rows, 16)
            outs[n][k] = total[pl.ds(start, block_rows), :].astype(BF)
            place += 1


def grad(left, left_block, left_columns, right, half, added=None, groups=None, order=None):
    tokens = left.shape[0]
    if right.ndim == 3:
        columns = right.shape[2]
    else:
        columns = right.shape[1] // 2
    blocks = 0 if groups is None else sum(groups)
    block_rows = 0 if groups is None else left_columns // blocks
    if columns % 128 or left_columns % 128 or block_rows % 16:
        cut = lax.dynamic_slice_in_dim(left, left_block * left_columns, left_columns, 1)
        if right.ndim == 3:
            other = pick(right, half, 0)
        else:
            other = lax.dynamic_slice_in_dim(right, half * columns, columns, 1)
        result = t_dot(cut, other)
        if added is not None:
            result = result + added.astype(F32)
        result = result.astype(BF)
        if groups is None:
            return result
        result = jnp.take(result.reshape(blocks, block_rows, columns), order, axis=0)
        outs, at = [], 0
        for count in groups:
            outs.append(result[at : at + count])
            at += count
        return outs
    wide = 384 if columns % 384 == 0 else (256 if columns % 256 == 0 else 128)
    steps = columns // wide
    maps = jnp.stack([jnp.asarray(left_block, jnp.int32), jnp.asarray(half, jnp.int32)])
    if groups is not None:
        maps = jnp.concatenate([maps, order.astype(jnp.int32)])
    in_specs = [pl.BlockSpec((tokens, left_columns), lambda i, maps: (0, maps[0]))]
    if right.ndim == 3:
        in_specs.append(pl.BlockSpec((1, tokens, wide), lambda i, maps: (maps[1], 0, i)))
    else:
        in_specs.append(pl.BlockSpec((tokens, wide), lambda i, maps: (0, maps[1] * steps + i)))
    operands = [left, right]
    if added is not None:
        in_specs.append(pl.BlockSpec((left_columns, wide), lambda i, maps: (0, i)))
        operands.append(added)
    scratch = []
    if groups is None:
        shapes = [jax.ShapeDtypeStruct((left_columns, columns), BF)]
        out_specs = [pl.BlockSpec((left_columns, wide), lambda i, maps: (0, i))]
    else:
        shapes = [jax.ShapeDtypeStruct((count, block_rows, columns), BF) for count in groups]
        out_specs = [
            pl.BlockSpec((count, block_rows, wide), lambda i, maps: (0, 0, i)) for count in groups
        ]
        scratch = [pltpu.VMEM((left_columns, wide), F32)]
    outs = kernel_call(
        functools.partial(grad_kernel, groups, block_rows, added is not None),
        grid_spec=pltpu.PrefetchScalarGridSpec(
            num_scalar_prefetch=1,
            grid=(steps,),
            in_specs=in_specs,
            out_specs=out_specs,
            scratch_shapes=scratch,
        ),
        out_shape=shapes,
    )(maps, *operands)
    return outs[0] if groups is None else outs


class Clock:
    def __init__(self):
        self.marks = ()

    def tie(self, value):
        return after(value, *self.marks) if self.marks else value

    def mark(self, *values):
        self.marks = values


def body(
    tokens,
    cotangent,
    lengths,
    block_of,
    gain_attn,
    w_query,
    w_keyval,
    w_out,
    gain_mlp,
    w_gateup,
    w_down,
):
    tok_rows, width = tokens.shape
    y_count, z_count = lax.axis_size("y"), lax.axis_size("z")
    ctx_count = 4 * z_count
    z_levels = z_count.bit_length() - 1
    x_at, c_at, y_at, z_at = (lax.axis_index(name) for name in ("x", "c", "y", "z"))
    own_index = (z_at * 2 + x_at) * 2 + c_at
    deep = w_query.shape[0]
    quarter = deep // 4
    units = FF // (2 * y_count)
    half_tok = tok_rows // 2
    group = 2 * y_count
    others = range(1, y_count)
    clock = Clock()
    tie, mark = clock.tie, clock.mark

    gain_rows = -(-(-(-2 * deep // (2 * HD))) // 16) * 16
    gain_pack = jnp.concatenate([gain_attn, gain_mlp])
    gain_pack = jnp.pad(gain_pack, (0, gain_rows * 2 * HD - 2 * deep)).reshape(gain_rows, 2 * HD)
    pack = jnp.concatenate([w_keyval, gain_pack], axis=0)
    packs = [pack] + [shift(pack, "y", r) for r in others]
    place_cx = c_at * 2 + x_at
    place_cz = c_at * 2 + (z_at & 1)

    def rows_of(weight, place):
        return lax.dynamic_slice_in_dim(weight, place * quarter, quarter, 0)

    wq_piece = after(rows_of(w_query, place_cx), pack)
    wq_found = {r: [shift(wq_piece, "y", r)] for r in others}
    wo_piece = after(rows_of(w_out, place_cx), wq_piece)
    wo_found = {r: [shift(wo_piece, "y", r)] for r in others}
    cot_first = after(cotangent[:half_tok], wo_piece)
    cot_second = cotangent[half_tok:]
    cot_first = jnp.concatenate([cot_first] + [shift(cot_first, "y", r) for r in others], axis=0)
    cot_second = jnp.concatenate([cot_second, shift(cot_second, "x", 1)], axis=0)
    gu_found = {}
    for r in others:
        column = ((y_at ^ r) * 2 + x_at) * units
        moves = [
            (0, (quarter, units), (place_cz * quarter, part * FF + column), (0, part * units))
            for part in (0, 1)
        ]
        piece = lay_out((quarter, 2 * units), [after(w_gateup, wo_piece)], moves)
        gu_found[r] = [shift(piece, "y", r)]

    def with_sharer(found, axis):
        return {r: [pieces[0], shift(pieces[0], axis, 1)] for r, pieces in found.items()}

    def with_core(found):
        return {r: pair + [shift(p, "c", 1) for p in pair] for r, pair in found.items()}

    def listed(shard, found, place):
        pieces, rows = [shard], [y_at * deep]
        for r, quarters in found.items():
            for s, piece in enumerate(quarters):
                pieces.append(piece)
                rows.append((y_at ^ r) * deep + (place ^ s) * quarter)
        return pieces, rows

    device_ids = jnp.arange(ctx_count, dtype=jnp.int32)
    block_row = block_of[0]
    own_block = jnp.sum(jnp.where(device_ids == own_index, block_row, 0))
    own_start = own_block * tok_rows
    owners = jnp.sum(
        jnp.where(block_row[None, :] == device_ids[:, None], device_ids[None, :], 0), axis=1
    )
    seq_lengths = lengths[0]
    query_places = own_start + jnp.arange(tok_rows, dtype=jnp.int32)
    key_places = own_start - WINDOW + jnp.arange(WINDOW + tok_rows, dtype=jnp.int32)
    query_segment, query_position = segment_info(query_places, seq_lengths)
    key_segment = segment_info(key_places, seq_lengths)[0]
    distance = query_places[:, None] - key_places[None, :]
    allowed = (
        (query_segment[:, None] == key_segment[None, :])
        & (key_places >= 0)[None, :]
        & (distance >= 0)
        & (distance < WINDOW)
    )
    bias = jnp.where(allowed, 0.0, -1e30).astype(F32)
    cosine, sine = tables(query_position, HD)
    cosine = jnp.concatenate([cosine, cosine], axis=1)
    sine = jnp.concatenate([-sine, sine], axis=1)
    spans = WINDOW // tok_rows + 1
    first_block = own_block - (spans - 1)

    def entry_of(ctx_index):
        differ = ctx_index ^ own_index
        return (differ >> 2) | (((differ >> 1) & 1) << z_levels) | ((differ & 1) << (z_levels + 1))

    window = first_block + jnp.arange(spans, dtype=jnp.int32)
    window = entry_of(jnp.take(owners, jnp.clip(window, 0, ctx_count - 1)))
    entries = jnp.arange(ctx_count, dtype=jnp.int32)
    differ = (entries & (z_count - 1)) << 2
    differ = differ | (((entries >> z_levels) & 1) << 1) | (entries >> (z_levels + 1))
    entry_block = jnp.take(block_row, differ ^ own_index) - first_block
    entry_block = jnp.where((entry_block >= 0) & (entry_block < spans), entry_block, spans)

    inputs = tokens.astype(F32)
    scale_attn = rms_factor(inputs)
    w_kv = by_place([p[:deep] for p in packs], "y").reshape(width, 2 * HD)
    flat = [p[deep:].reshape(-1)[: 2 * deep].reshape(2, deep) for p in packs]
    gains = jnp.swapaxes(by_place(flat, "y"), 0, 1).reshape(2, width).astype(F32)
    gain_one, gain_two = gains[0], gains[1]
    normed = (inputs * scale_attn * gain_one).astype(BF)
    kv_raw = dot(normed, w_kv)
    keyval = jnp.concatenate(
        [rotate(kv_raw[:, :HD], cosine, sine), kv_raw[:, HD:]], axis=1
    ).astype(BF)
    all_kv = jnp.stack([keyval] + [shift(keyval, "z", d) for d in range(1, z_count)])
    all_kv = jnp.concatenate([all_kv, shift(all_kv, "x", 1)], axis=0)
    all_kv = jnp.concatenate([all_kv, shift(all_kv, "c", 1)], axis=0)

    q_pieces, q_rows = listed(w_query, with_core(with_sharer(wq_found, "x")), place_cx)
    o_pieces, o_rows = listed(w_out, with_core(with_sharer(wo_found, "x")), place_cx)
    n_q, n_o = len(q_pieces), len(o_pieces)
    pairs = H // 2
    kv_specs = [
        pl.BlockSpec((1, tok_rows, 2 * HD), lambda i, maps, n=n: (maps[n], 0, 0))
        for n in range(spans)
    ]
    pair_spec = pl.BlockSpec((tok_rows, 2 * HD), lambda i, maps: (0, i))
    token_spec = pl.BlockSpec((tok_rows, width), lambda i, maps: (0, 0))
    maps = jnp.concatenate([window, jnp.stack(q_rows + o_rows).astype(jnp.int32)])
    small = [gain_two[None], bias, cosine, sine]
    queries, attended, hidden, own_norm, factor = kernel_call(
        functools.partial(attend_kernel, n_q, n_o, spans),
        grid_spec=pltpu.PrefetchScalarGridSpec(
            num_scalar_prefetch=1,
            grid=(pairs,),
            in_specs=[token_spec, token_spec]
            + [whole_spec(a) for a in small]
            + kv_specs
            + [ANY] * (n_q + n_o),
            out_specs=[
                pair_spec,
                pair_spec,
                token_spec,
                token_spec,
                pl.BlockSpec((tok_rows, HD), lambda i, maps: (0, 0)),
            ],
            scratch_shapes=[
                pltpu.VMEM((width, H * HD), BF),
                pltpu.VMEM((H * HD, width), BF),
                pltpu.VMEM((spans * tok_rows, HD), BF),
                pltpu.VMEM((spans * tok_rows, HD), BF),
                pltpu.VMEM((tok_rows, width), F32),
                pltpu.SemaphoreType.DMA((n_q,)),
                pltpu.SemaphoreType.DMA((n_o,)),
            ],
        ),
        out_shape=[
            jax.ShapeDtypeStruct((tok_rows, H * HD), BF),
            jax.ShapeDtypeStruct((tok_rows, H * HD), BF),
            jax.ShapeDtypeStruct((tok_rows, width), F32),
            jax.ShapeDtypeStruct((tok_rows, width), BF),
            jax.ShapeDtypeStruct((tok_rows, HD), F32),
        ],
    )(maps, normed, tokens, *small, *([all_kv] * spans), *q_pieces, *o_pieces)
    scale_mlp = factor[:, :1]

    cot_first = jnp.concatenate([cot_first, shift(cot_first, "x", 1)], axis=0)
    cot_second = jnp.concatenate(
        [cot_second] + [shift(cot_second, "y", r) for r in others], axis=0
    )
    cot_all = jnp.concatenate([cot_first, cot_second], axis=0)
    gu_moves = [
        (0, (deep, units), (0, part * FF + (y_at * 2 + x_at) * units), (y_at * deep, part * units))
        for part in (0, 1)
    ]
    gu_pieces, gu_rows = listed(w_gateup, with_core(with_sharer(gu_found, "z")), place_cz)
    for n in range(1, len(gu_pieces)):
        gu_moves.append((n, (quarter, 2 * units), (0, 0), (gu_rows[n], 0)))
    w_gu = lay_out((width, 2 * units), gu_pieces, gu_moves)

    first, second = own_norm[:half_tok], own_norm[half_tok:]
    first = jnp.concatenate([first] + [shift(first, "y", r) for r in others], axis=0)
    second = jnp.concatenate([second, shift(second, "x", 1)], axis=0)
    first = jnp.concatenate([first, shift(first, "x", 1)], axis=0)
    second = jnp.concatenate([second] + [shift(second, "y", r) for r in others], axis=0)
    normed2 = jnp.concatenate([first, second], axis=0)
    many = group * tok_rows
    fits = units % 128 == 0
    cuts = [many // 4] * 2 + [many // 2 // y_count] * y_count
    cut_shapes = [jax.ShapeDtypeStruct((count, width), BF) for count in cuts]
    x_maps = jnp.stack([x_at]).astype(jnp.int32)

    def cut(result):
        outs, at = [], 0
        for count in cuts:
            outs.append(result[at : at + count].astype(BF))
            at += count
        return outs

    if fits:
        wide = 384 if units % 384 == 0 else 128
        steps = units // wide
        inner_act, d_both = kernel_call(
            forward_kernel,
            grid_spec=pltpu.PrefetchScalarGridSpec(
                num_scalar_prefetch=1,
                grid=(steps,),
                in_specs=[
                    pl.BlockSpec((many, width), lambda i, maps: (0, 0)),
                    pl.BlockSpec((many, width), lambda i, maps: (0, 0)),
                    pl.BlockSpec((width, wide), lambda i, maps: (0, i)),
                    pl.BlockSpec((width, wide), lambda i, maps: (0, steps + i)),
                    pl.BlockSpec((wide, width), lambda i, maps: (maps[0] * steps + i, 0)),
                ],
                out_specs=[
                    pl.BlockSpec((many, wide), lambda i, maps: (0, i)),
                    pl.BlockSpec((2, many, wide), lambda i, maps: (0, 0, i)),
                ],
            ),
            out_shape=[
                jax.ShapeDtypeStruct((many, units), BF),
                jax.ShapeDtypeStruct((2, many, units), BF),
            ],
        )(x_maps, normed2, cot_all, w_gu, w_gu, w_down)
        block = 512
        d_cut = kernel_call(
            back_kernel,
            grid=(width // block,),
            in_specs=[
                whole_spec(d_both),
                pl.BlockSpec((block, 2 * units), lambda i: (i, 0)),
            ],
            out_specs=[pl.BlockSpec((count, block), lambda i: (0, i)) for count in cuts],
            out_shape=cut_shapes,
        )(d_both, w_gu)

        def down_cut():
            return kernel_call(
                down_kernel,
                grid_spec=pltpu.PrefetchScalarGridSpec(
                    num_scalar_prefetch=1,
                    grid=(width // block,),
                    in_specs=[
                        pl.BlockSpec((many, units), lambda i, maps: (0, 0)),
                        pl.BlockSpec((units, block), lambda i, maps: (maps[0], i)),
                    ],
                    out_specs=[
                        pl.BlockSpec((count, block), lambda i, maps: (0, i)) for count in cuts
                    ],
                ),
                out_shape=cut_shapes,
            )(x_maps, tie(inner_act), w_down)

    else:
        w_dn = lax.dynamic_slice_in_dim(w_down, x_at * units, units, 0)
        d_inner = dot_t(cot_all, w_dn)
        both_parts = dot(normed2, w_gu)
        active, back = jax.vjp(
            lambda values: jax.nn.gelu(values, approximate=True), both_parts[:, :units]
        )
        up_part = both_parts[:, units:]
        inner_act = (active * up_part).astype(BF)
        d_both = jnp.stack([back(d_inner * up_part)[0], d_inner * active]).astype(BF)
        d_cut = cut(dot_t(d_both[0], w_gu[:, :units]) + dot_t(d_both[1], w_gu[:, units:]))

        def down_cut():
            return cut(dot(tie(inner_act), w_dn))

    mark(*d_cut)

    def group_back(cuts_in, result):
        keep_a, send_a, keep_b, send_b = cuts_in[0], cuts_in[1], cuts_in[2], cuts_in[3:]
        got_a = shift(send_a, "x", 1)
        got_b = [shift(part, "y", r) for r, part in zip(others, send_b, strict=True)]
        yield
        got_a, got_b = tie(got_a), [tie(part) for part in got_b]
        keep_a, got_a = (v.reshape(y_count, half_tok, width) for v in (keep_a, got_a))
        parts_b = [v.reshape(2, half_tok, width) for v in [keep_b] + got_b]
        left_a = [add(keep_a[r], got_a[r]) for r in range(y_count)]
        left_b = [sum(part[n].astype(F32) for part in parts_b).astype(BF) for n in range(2)]
        mark(*left_a[1:], left_b[1])
        got_a = [shift(left_a[r], "y", r) for r in others]
        got_b = shift(left_b[1], "x", 1)
        yield
        got_a, got_b = [tie(part) for part in got_a], tie(got_b)
        first = sum(v.astype(F32) for v in [left_a[0]] + got_a)
        second = left_b[0].astype(F32) + got_b.astype(F32)
        result.append(jnp.concatenate([first, second], axis=0))

    def scatter_z(kept, sent):
        for level in range(z_levels):
            got = shift(sent, "z", 1 << level)
            yield
            got = tie(got)
            half = kept.shape[0] // 2
            if half:
                sent = add(kept[half:], got[half:])
                kept = add(kept[:half], got[:half])
                mark(sent)
            else:
                kept = add(kept[0], got[0])
        return kept

    def spread(piece, finish):
        held = piece[None]
        for level in reversed(range(z_levels)):
            mark(held)
            got = shift(held, "z", 1 << level)
            yield
            held = jnp.concatenate([held, tie(got)], axis=0)
        mark(held)
        beside, across = shift(held, "x", 1), shift(held, "c", 1)
        yield
        beside = tie(beside)
        mark(beside)
        corner = shift(beside, "c", 1)
        yield
        mark(finish([held, beside, tie(across), tie(corner)]))

    z_places = jnp.zeros((z_count,), jnp.int32)
    z_differ = jnp.arange(z_count, dtype=jnp.int32) ^ z_at
    for n, level in enumerate(reversed(range(z_levels))):
        z_places = z_places | (((z_differ >> level) & 1) << n)
    z_order = jnp.zeros((z_count,), jnp.int32)
    for level in range(z_levels):
        z_order = z_order | (
            ((jnp.arange(z_count, dtype=jnp.int32) >> (z_levels - 1 - level)) & 1) << level
        )
    z_order = z_order ^ z_at
    z_groups = [z_count // 2, z_count // 2]

    found = {}

    def finish_down(parts):
        found["down"] = widen(
            parts, z_places, (w_down.shape[0], width), lambda z, c, x, y=None: (x * z_count + z, c)
        )
        return found["down"]

    def finish_up(r):
        def finish(parts):
            found["up"] = widen(
                parts,
                z_places,
                (deep, 2 * FF),
                lambda z, c, x, y=y_at: (z, (c * y_count + (y ^ r)) * 2 + x),
                found.get("up"),
            )
            return found["up"]

        return finish

    def finish_attn(name, columns):
        def finish(parts):
            found[name] = widen(
                parts, z_places, (deep, columns), lambda z, c, x, y=None: (z * 2 + x, c)
            )
            return found[name]

        return finish

    def ffn_chain(job, finish, r):
        left, left_block, left_columns, right = job
        theirs = grad(tie(left), left_block, left_columns, right, 1 - c_at)
        mark(theirs)
        got = shift(theirs, "c", 1)
        yield
        kept, sent = grad(
            tie(left), left_block, left_columns, right, c_at, got, z_groups, z_order
        )
        mark(sent)
        piece = yield from scatter_z(kept, sent)
        if r:
            mark(piece)
            piece = shift(piece, "y", r)
            yield
            piece = tie(piece)
        yield from spread(piece, finish)

    def attn_chain(left, right, finish, column=None):
        theirs = grad(tie(left), 0, width, right, 1 - c_at)
        if column is not None:
            lane = jnp.arange(HD) == 0
            own = jnp.where(c_at == 0, column[0], column[1])[:, None]
            other = jnp.where(c_at == 0, column[1], column[0])[:, None]
            theirs = jnp.concatenate([theirs, jnp.where(lane, other, 0).astype(BF)], axis=1)
        mark(theirs)
        got = shift(theirs, "c", 1)
        yield
        y_order = jnp.arange(y_count, dtype=jnp.int32) ^ y_at
        cols = right.shape[1] // 2
        parts = grad(
            tie(left), 0, width, right, c_at, got[:, :cols], [1] * y_count, y_order
        )
        parts = [part[0] for part in parts]
        if column is not None:
            extra = add(jnp.where(lane, own, 0), got[:, cols:]).reshape(y_count, deep, HD)
            parts = [
                jnp.concatenate([part, pick(extra, y_at ^ r, 0)], axis=1)
                for r, part in enumerate(parts)
            ]
        mark(*parts[1:])
        got = [shift(part, "y", r) for r, part in zip(others, parts[1:], strict=True)]
        yield
        got = [tie(part) for part in got]
        total = sum(v.astype(F32) for v in [parts[0]] + got).astype(BF)
        blocks = total.reshape(z_count, 2, deep // (2 * z_count), total.shape[1])
        kept = jnp.take(pick(blocks, x_at, 1), z_order, axis=0)
        sent = jnp.take(pick(blocks, 1 - x_at, 1), z_order, axis=0)
        mark(sent)
        got = shift(sent, "x", 1)
        yield
        got = tie(got)
        half = z_count // 2
        sent = add(kept[half:], got[half:])
        kept = add(kept[:half], got[:half])
        mark(sent)
        piece = yield from scatter_z(kept, sent)
        yield from spread(piece, finish)

    def step(chain):
        return next(chain, None)

    d_result, out_result = [], []
    d_chain = group_back(d_cut, d_result)
    step(d_chain)
    chain_down = ffn_chain((inner_act, 0, units, cot_all), finish_down, 0)
    chains_up = [
        ffn_chain((normed2, y_at ^ r, deep, d_both), finish_up(r), r)
        for r in list(others) + [0]
    ]
    ffn = chains_up[:-1] + [chain_down, chains_up[-1]]
    for chain in ffn:
        step(chain)
    for chain in ffn:
        step(chain)
    step(d_chain)
    out_cut = down_cut()
    mark(*out_cut)
    out_chain = group_back(out_cut, out_result)
    step(out_chain)
    step(ffn[0])
    step(d_chain)
    d_normed2 = d_result[0]
    d_gain_mlp = jnp.sum(d_normed2 * hidden * scale_mlp, axis=0)
    d_hidden = cotangent.astype(F32) + norm_back(d_normed2, hidden, scale_mlp, gain_two)
    d_attn = d_hidden.astype(BF)
    mark(d_attn)
    chain_out = attn_chain(attended, d_attn, finish_attn("out", width))
    step(chain_out)
    step(ffn[1])
    step(chain_out)

    maps = jnp.concatenate([window, entry_block, jnp.stack(o_rows).astype(jnp.int32)])
    entry_spec = pl.BlockSpec((ctx_count // 2, tok_rows, 2 * HD), lambda i, maps: (0, 0, 0))
    entry_shape = jax.ShapeDtypeStruct((ctx_count // 2, tok_rows, 2 * HD), BF)
    small = [bias, cosine, sine]
    d_query_raw, d_kept, d_sent = kernel_call(
        functools.partial(attend_back_kernel, n_o, spans, ctx_count),
        grid_spec=pltpu.PrefetchScalarGridSpec(
            num_scalar_prefetch=1,
            grid=(pairs,),
            in_specs=[token_spec, pair_spec]
            + [whole_spec(a) for a in small]
            + kv_specs
            + [ANY] * n_o,
            out_specs=[pair_spec, entry_spec, entry_spec],
            scratch_shapes=[
                pltpu.VMEM((H * HD, width), BF),
                pltpu.VMEM((spans * tok_rows, HD), BF),
                pltpu.VMEM((spans * tok_rows, HD), BF),
                pltpu.VMEM((HD, spans * tok_rows), F32),
                pltpu.VMEM((HD, spans * tok_rows), F32),
                pltpu.VMEM(((spans + 1) * tok_rows, 2 * HD), BF),
                pltpu.SemaphoreType.DMA((n_o,)),
            ],
        ),
        out_shape=[jax.ShapeDtypeStruct((tok_rows, H * HD), BF), entry_shape, entry_shape],
    )(maps, tie(d_attn), queries, *small, *([all_kv] * spans), *o_pieces)
    mark(d_sent)

    def kv_back(result):
        kept, sent = d_kept, d_sent
        for axis in ("c", "x"):
            got = shift(sent, axis, 1)
            yield
            got = tie(got)
            half = kept.shape[0] // 2
            if axis == "c":
                sent = add(kept[half:], got[half:])
                kept = add(kept[:half], got[:half])
                mark(sent)
            else:
                left = [add(kept[d], got[d]) for d in range(z_count)]
                mark(*left[1:])
        got = [shift(left[d], "z", d) for d in range(1, z_count)]
        yield
        got = [tie(part) for part in got]
        result.append(sum(v.astype(F32) for v in [left[0]] + got))

    kv_result = []
    kv_chain = kv_back(kv_result)
    step(kv_chain)
    step(ffn[2])
    step(kv_chain)
    chain_query = attn_chain(normed, d_query_raw, finish_attn("query", width))
    step(chain_query)
    step(ffn[0])
    step(ffn[1])
    step(kv_chain)
    step(chain_query)
    step(ffn[0])
    step(out_chain)
    step(kv_chain)
    d_kv_own = kv_result[0]
    d_kv_raw = jnp.concatenate(
        [rotate(d_kv_own[:, :HD], cosine, -sine), d_kv_own[:, HD:]], axis=1
    ).astype(BF)
    w_q = lay_out(
        (width, H * HD),
        q_pieces,
        [(n, p.shape, (0, 0), (q_rows[n], 0)) for n, p in enumerate(q_pieces)],
    )
    d_normed = dot_t(d_query_raw, w_q) + dot_t(d_kv_raw, w_kv)
    d_gain_attn = jnp.sum(d_normed * inputs * scale_attn, axis=0)
    grad_tokens = d_hidden + norm_back(d_normed, inputs, scale_attn, gain_one)
    mark(d_kv_raw, d_gain_attn)
    chain_kv = attn_chain(
        normed, d_kv_raw, finish_attn("keyval", 4 * HD), (d_gain_attn, d_gain_mlp)
    )
    step(chain_kv)
    step(out_chain)
    block_output = (hidden + out_result[0]).astype(BF)
    mark(block_output)

    waiting = [ffn[2], chain_out, ffn[1], chain_kv, ffn[0], chain_query] + ffn[3:]
    alive = list(waiting)
    while alive:
        for chain in list(alive):
            try:
                next(chain)
            except StopIteration:
                alive.remove(chain)
    last = found["keyval"]
    grad_keyval = jnp.concatenate([last[:, :HD], last[:, 2 * HD : 3 * HD]], axis=1)
    return (
        block_output,
        grad_tokens,
        last[:, HD],
        found["query"],
        grad_keyval,
        found["out"],
        last[:, 3 * HD],
        found["up"],
        found["down"],
    )


def solution(mesh):
    ctx_count, y_count = mesh.shape["ctx"], mesh.shape["fsdp"]
    fine = Mesh(mesh.devices.reshape(ctx_count // 4, 2, 2, y_count), ("z", "x", "c", "y"))
    rows, shard = P(("z", "x", "c", "y"), None), P("y", None)
    in_specs = (rows, rows, shard, shard, P("y"), shard, shard, shard, P("y"), shard, shard)
    out_specs = (rows, rows, P("y"), shard, shard, shard, P("y"), shard, shard)
    return jax.shard_map(body, mesh=fine, in_specs=in_specs, out_specs=out_specs, check_vma=False)
```

time: 1980 us -> 764 us (0.39)
  waiting for transfers between devices: 1650 us -> 334 us
  Pallas kernels: 0 us -> 199 us
  matrix products: 144 us -> 4.17 us
  starting transfers between devices: 0.95 us -> 95.9 us
  blocking collectives: 60 us -> 0 us
    reduce_scatter x6 -> x0, waiting for transfers between devices: 637 us -> none  [the longest x1 316 us: body(): lax.psum_scatter(d_gateup.astype(jnp.bfloat16), 'fsdp', scatter_dimension...]
    all_gather x5 -> x0, waiting for transfers between devices: 608 us -> none  [the longest x1 328 us: body(): lax.all_gather(w_gateup, 'fsdp', axis=0, tiled=True)]
    psum x1 -> x0, waiting for transfers between devices: 404 us -> none  [body(): lax.psum(shards[1].astype(jnp.bfloat16), 'ctx').astype(jnp.float32)]
    ppermute x0 -> x94, waiting for transfers between devices: none -> 334 us  [shift(): lax.ppermute(array, axis, [(i, i ^ mask) for i in range(lax.axis_size(axi...]
    pallas_call x0 -> x26, Pallas kernels: none -> 199 us  [the longest x12 51.9 us: grad(): kernel_call(functools.partial(grad_kernel, groups, block_rows, added is n...]
    dot_general x21 -> x3, matrix products: 144 us -> 4.17 us  [the longest x2 3.8 us: dot_t(): lax.dot_general(a, b, (((1,), (1,)), ((), ())), preferred_element_type=F32)]
    ppermute x0 -> x94, starting transfers between devices: none -> 95.9 us  [shift(): lax.ppermute(array, axis, [(i, i ^ mask) for i in range(lax.axis_size(axi...]
    psum x1 -> x0, blocking collectives: 34.5 us -> none  [body(): lax.psum(shards[0].astype(jnp.bfloat16), 'ctx').astype(jnp.float32)]
  transfers between devices with their start and end apart: 12 -> 94, of which waited for: 11 -> 37; matrix products, arithmetic and copies ran while one was open for 6% -> 13% of each run, Pallas kernels for 0% -> 20%
where the time goes in v2:
time: 764 us; the launch traced here: 754 us
  waiting for transfers between devices  334 us (44%)
  Pallas kernels  199 us (26%)
  starting transfers between devices  95.9 us (13%)
  other arithmetic  73 us (10%)
  local copies, waits for them, and re-layouts  44.3 us (6%)
    ppermute x94, waiting for transfers between devices, shift(): lax.ppermute(array, axis, [(i, i ^ mask) for i in range(lax.axis_size(axi...  334 us
    ppermute x94, starting transfers between devices, shift(): lax.ppermute(array, axis, [(i, i ^ mask) for i in range(lax.axis_size(axi...  95.9 us
    pallas_call x12, Pallas kernels, grad(): kernel_call(functools.partial(grad_kernel, groups, block_rows, added is n...  51.9 us
    pallas_call x6, Pallas kernels, widen(): kernel_call(widen_kernel, grid_spec=pltpu.PrefetchScalarGridSpec(num_scal...  50.3 us
    pallas_call x1, Pallas kernels, body(): kernel_call(functools.partial(attend_kernel, n_q, n_o, spans), grid_spec=...  23.1 us
    pallas_call x1, Pallas kernels, body(): kernel_call(functools.partial(attend_back_kernel, n_o, spans, ctx_count),...  21.7 us
    convert_element_type x20, other arithmetic, add(): return (a.astype(F32) + b.astype(F32)).astype(BF)  21.2 us
    pallas_call x1, Pallas kernels, body(): kernel_call(forward_kernel, grid_spec=pltpu.PrefetchScalarGridSpec(num_sc...  21.1 us
  transfers between devices with their start and end apart: 94, of which 37 were waited for; matrix products, arithmetic and copies ran while one was open for 13% of the time, Pallas kernels for 20%

profile of v2, /device:TPU:0, one launch (start us, length us, event | category | flops | bytes accessed | tf_op | source)
XLA Modules:
  0.0 754.1 jit_solution(7647357866831804441)
XLA Ops:
  22.7 28.4 %collective-permute-done.18 = bf16[128,1536]{1,0:T(8,128)(2,1)} collective-permute-done((bf16[128,1536]{1,0:T(8,128)(2,1)S(1)}, bf16[128,1536]{1,0:T(8,128)(2,1)}, u32[]{:S(2)}, u32[]{:S(2)}) %collective-permute-start.18) | collective-permute-done | bytes 393248 | tf_op jit(solution)/shard_map/ppermute | solution.py:70
  76.8 27.4 %collective-permute-done.4 = bf16[4,256,256]{2,1,0:T(8,128)(2,1)S(1)} collective-permute-done((bf16[4,256,256]{2,1,0:T(8,128)(2,1)S(1)}, bf16[4,256,256]{2,1,0:T(8,128)(2,1)S(1)}, u32[]{:S(2)}, u32[]{:S(2)}) %collective-permute-start.4) | collective-permute-done | bytes 524320 | tf_op jit(solution)/shard_map/ppermute | solution.py:70
  108.2 8.7 %collective-permute-done.11.refs_18_.refs_12_ = bf16[192,1536]{1,0:T(8,128)(2,1)S(1)} collective-permute-done((bf16[192,1536]{1,0:T(8,128)(2,1)S(1)}, bf16[192,1536]{1,0:T(8,128)(2,1)S(1)}, u32[]{:S(2)}, u32[]{:S(2)}) %collective-permute-start.11) | collective-permute-done | bytes 589856 | tf_op jit(solution)/shard_map/ppermute | solution.py:70
  116.9 10.7 %collective-permute-done.7.refs_13_.refs_2_ = bf16[192,1536]{1,0:T(8,128)(2,1)S(1)} collective-permute-done((bf16[192,1536]{1,0:T(8,128)(2,1)S(1)}, bf16[192,1536]{1,0:T(8,128)(2,1)S(1)}, u32[]{:S(2)}, u32[]{:S(2)}) %collective-permute-start.7) | collective-permute-done | bytes 589856 | tf_op jit(solution)/shard_map/ppermute | solution.py:70
  130.3 23.1 %shard_map.178 = (bf16[256,1536]{1,0:T(8,128)(2,1)S(1)}, bf16[256,1536]{1,0:T(8,128)(2,1)}, f32[256,1536]{1,0:T(8,128)}, bf16[256,1536]{1,0:T(8,128)(2,1)}, f32[256,128]{1,0:T(8,128)S(1)}) custom-call(s32[15]{0:T(128)S(1)} %concatenate.156.maps, bf16[256,1536]{1,0:T(8,128)(2,1)} %copy-done.1, bf16[256,1536]{1,0:T(8,128)(2,1)} %refs_1_.1, ...), custom_call_target="tpu_custom_call" | custom-call | flops 1000 | bytes 1000 | tf_op jit(solution)/shard_map/pallas_call | solution.py:566
  162.0 6.1 collective-permute-done.14
  171.2 12.9 %collective-permute-done.21 = bf16[256,1536]{1,0:T(8,128)(2,1)} collective-permute-done((bf16[256,1536]{1,0:T(8,128)(2,1)}, bf16[256,1536]{1,0:T(8,128)(2,1)}, u32[]{:S(2)}, u32[]{:S(2)}) %collective-permute-start.21) | collective-permute-done | bytes 786464 | tf_op jit(solution)/shard_map/ppermute | solution.py:70
  188.9 6.1 shard_map.180.w_gate.w_up.w_gu
  196.2 8.8 %collective-permute-done.17 = bf16[256,1536]{1,0:T(8,128)(2,1)S(1)} collective-permute-done((bf16[256,1536]{1,0:T(8,128)(2,1)S(1)}, bf16[256,1536]{1,0:T(8,128)(2,1)S(1)}, u32[]{:S(2)}, u32[]{:S(2)}) %collective-permute-start.17) | collective-permute-done | bytes 786464 | tf_op jit(solution)/shard_map/ppermute | solution.py:70
  205.0 21.1 %shard_map.181 = (bf16[1024,1152]{1,0:T(8,128)(2,1)S(1)}, bf16[2,1024,1152]{2,1,0:T(8,128)(2,1)}) custom-call(s32[1]{0:T(128)} %bitcast.20.maps, bf16[1024,1536]{1,0:T(8,128)(2,1)S(1)} %constant_dynamic-update-slice_fusion.11.normed.left, bf16[1024,1536]{1,0:T(8,128)(2,1)} %constant_dynamic-update-slice_fusion.17.cot.right, ...), custom_call_target="tpu_custom_call" | custom-call | flops 1000 | bytes 1000 | tf_op jit(solution)/shard_map/pallas_call | solution.py:638
  226.1 13.5 %shard_map.182 = (bf16[256,1536]{1,0:T(8,128)(2,1)S(1)}, bf16[256,1536]{1,0:T(8,128)(2,1)}, bf16[256,1536]{1,0:T(8,128)(2,1)S(1)}, bf16[256,1536]{1,0:T(8,128)(2,1)}) custom-call(bf16[2,1024,1152]{2,1,0:T(8,128)(2,1)} %get-tuple-element.128.d_both.right, bf16[1536,2304]{1,0:T(8,128)(2,1)} %shard_map.180.w_gate.w_up.w_gu), custom_call_target="tpu_custom_call" | custom-call | flops 1000 | bytes 1000 | tf_op jit(solution)/shard_map/pallas_call | solution.py:661
  262.3 6.2 shard_map.186
  275.9 6.0 shard_map.188
  285.3 6.3 shard_map.189
  305.1 19.8 %collective-permute-done.36 = bf16[2,288,768]{2,1,0:T(8,128)(2,1)} collective-permute-done((bf16[2,288,768]{2,1,0:T(8,128)(2,1)}, bf16[2,288,768]{2,1,0:T(8,128)(2,1)}, u32[]{:S(2)}, u32[]{:S(2)}) %collective-permute-start.36) | collective-permute-done | bytes 884768 | tf_op jit(solution)/shard_map/ppermute | solution.py:70
  331.9 21.7 %shard_map.192 = (bf16[256,1536]{1,0:T(8,128)(2,1)S(1)}, bf16[8,256,256]{2,1,0:T(8,128)(2,1)S(1)}, bf16[8,256,256]{2,1,0:T(8,128)(2,1)}) custom-call(s32[26]{0:T(128)S(1)} %concatenate.177.maps, bf16[256,1536]{1,0:T(8,128)(2,1)S(1)} %get-tuple-element.160.right.refs_0_, bf16[256,1536]{1,0:T(8,128)(2,1)S(1)} %copy-done.42, ...), custom_call_target="tpu_custom_call" | custom-call | flops 1000 | bytes 1000 | tf_op jit(solution)/shard_map/pallas_call | solution.py:893
  375.8 17.9 %collective-permute-done.33 = bf16[1,192,1152]{2,1,0:T(8,128)(2,1)} collective-permute-done((bf16[1,192,1152]{2,1,0:T(8,128)(2,1)}, bf16[1,192,1152]{2,1,0:T(8,128)(2,1)}, u32[]{:S(2)}, u32[]{:S(2)}) %collective-permute-start.33) | collective-permute-done | bytes 442400 | tf_op jit(solution)/shard_map/ppermute | solution.py:70
  424.5 13.3 %collective-permute-start.50 = (bf16[1,288,768]{2,1,0:T(8,128)(2,1)}, bf16[1,288,768]{2,1,0:T(8,128)(2,1)}, u32[]{:S(2)}, u32[]{:S(2)}) collective-permute-start(bf16[1,288,768]{2,1,0:T(8,128)(2,1)} %add_convert_fusion.4), channel_id=1, source_target_pairs={{0,16},{8,24},{16,0},{24,8},{1,17},{9,25},{17,1},{25,9},{2,18},{10... | collective-permute-start | bytes 1327112 | tf_op jit(solution)/shard_map/ppermute | solution.py:70
  465.5 12.1 %collective-permute-done.50 = bf16[1,288,768]{2,1,0:T(8,128)(2,1)} collective-permute-done((bf16[1,288,768]{2,1,0:T(8,128)(2,1)}, bf16[1,288,768]{2,1,0:T(8,128)(2,1)}, u32[]{:S(2)}, u32[]{:S(2)}) %collective-permute-start.50) | collective-permute-done | bytes 442400 | tf_op jit(solution)/shard_map/ppermute | solution.py:70
  501.9 12.9 %collective-permute-done.55 = bf16[2,288,768]{2,1,0:T(8,128)(2,1)} collective-permute-done((bf16[2,288,768]{2,1,0:T(8,128)(2,1)}, bf16[2,288,768]{2,1,0:T(8,128)(2,1)}, u32[]{:S(2)}, u32[]{:S(2)}) %collective-permute-start.55) | collective-permute-done | bytes 884768 | tf_op jit(solution)/shard_map/ppermute | solution.py:70
  525.6 8.2 %collective-permute-done.65 = bf16[2,192,1152]{2,1,0:T(8,128)(2,1)} collective-permute-done((bf16[2,192,1152]{2,1,0:T(8,128)(2,1)}, bf16[2,192,1152]{2,1,0:T(8,128)(2,1)}, u32[]{:S(2)}, u32[]{:S(2)}) %collective-permute-start.65) | collective-permute-done | bytes 884768 | tf_op jit(solution)/shard_map/ppermute | solution.py:70
  538.4 14.2 %collective-permute-done.63 = bf16[2,192,1152]{2,1,0:T(8,128)(2,1)} collective-permute-done((bf16[2,192,1152]{2,1,0:T(8,128)(2,1)}, bf16[2,192,1152]{2,1,0:T(8,128)(2,1)}, u32[]{:S(2)}, u32[]{:S(2)}) %collective-permute-start.63) | collective-permute-done | bytes 884768 | tf_op jit(solution)/shard_map/ppermute | solution.py:70
  556.1 9.4 %collective-permute-done.62 = bf16[2,96,768]{2,1,0:T(8,128)(2,1)S(1)} collective-permute-done((bf16[2,96,768]{2,1,0:T(8,128)(2,1)S(1)}, bf16[2,96,768]{2,1,0:T(8,128)(2,1)S(1)}, u32[]{:S(2)}, u32[]{:S(2)}) %collective-permute-start.62) | collective-permute-done | bytes 294944 | tf_op jit(solution)/shard_map/ppermute | solution.py:70
  566.0 71.0 %collective-permute-done.60 = bf16[4,96,256]{2,1,0:T(8,128)(2,1)S(1)} collective-permute-done((bf16[4,96,256]{2,1,0:T(8,128)(2,1)S(1)}, bf16[4,96,256]{2,1,0:T(8,128)(2,1)S(1)}, u32[]{:S(2)}, u32[]{:S(2)}) %collective-permute-start.60) | collective-permute-done | bytes 196640 | tf_op jit(solution)/shard_map/ppermute | solution.py:70
  637.7 7.3 collective-permute-done.70
  646.5 8.7 %collective-permute-done.68 = bf16[1,96,768]{2,1,0:T(8,128)(2,1)S(1)} collective-permute-done((bf16[1,96,768]{2,1,0:T(8,128)(2,1)S(1)}, bf16[1,96,768]{2,1,0:T(8,128)(2,1)S(1)}, u32[]{:S(2)}, u32[]{:S(2)}) %collective-permute-start.68) | collective-permute-done | bytes 147488 | tf_op jit(solution)/shard_map/ppermute | solution.py:70
  657.2 11.7 %shard_map.198 = f32[2304,1536]{1,0:T(8,128)} custom-call(s32[6]{0:T(128)S(1)} %pad_add_fusion.28.maps, bf16[4,288,768]{2,1,0:T(8,128)(2,1)S(1)} %pad_maximum_fusion.refs_0_, bf16[4,288,768]{2,1,0:T(8,128)(2,1)S(1)} %collective-permute-done.61.refs_1_, bf16[4,288,768]{2,1,0:T(8,128)(2,1)S(1)} %collective-permute-done.67.refs_2_, bf16[4,288,768]{2,1,0:T(8,128)(2,1)} %copy-done.69), custom_call_target="tpu_custom_call" | custom-call | flops 1000 | bytes 1000 | tf_op jit(solution)/shard_map/pallas_call | solution.py:196
  675.6 11.7 %shard_map.199.refs_4_ = f32[768,9216]{1,0:T(8,128)} custom-call(s32[6]{0:T(128)S(1)} %pad_add_fusion.28.maps, bf16[4,192,1152]{2,1,0:T(8,128)(2,1)S(1)} %pad_maximum_fusion.1.refs_0_, bf16[4,192,1152]{2,1,0:T(8,128)(2,1)S(1)} %collective-permute-done.71.refs_1_, bf16[4,192,1152]{2,1,0:T(8,128)(2,1)S(1)} %collective-permute-done.77.refs_2_, ...), custom_call_target="tpu_custom_call" | custom-call | flops 1000 | bytes 1000 | tf_op jit(solution)/shard_map/pallas_call | solution.py:196
  687.6 11.8 %shard_map.200 = f32[768,9216]{1,0:T(8,128)} custom-call(s32[6]{0:T(128)S(1)} %pad_add_fusion.28.maps, bf16[4,192,1152]{2,1,0:T(8,128)(2,1)S(1)} %pad_maximum_fusion.2.refs_0_, bf16[4,192,1152]{2,1,0:T(8,128)(2,1)S(1)} %collective-permute-done.69.refs_1_, bf16[4,192,1152]{2,1,0:T(8,128)(2,1)S(1)} %collective-permute-done.75.refs_2_, ...), custom_call_target="tpu_custom_call", output_to_operand_aliasing={{}: (5, {})} | custom-call | flops 1000 | bytes 1000 | tf_op jit(solution)/shard_map/pallas_call | solution.py:196
  717.1 6.5 collective-permute-done.84.refs_1_
  735.3 6.7 shard_map.201
  743.6 6.7 shard_map.202
  (572 shorter events, 293.5 us)
Async XLA Ops:
  4.8 48.2 %collective-permute-start = (bf16[784,256]{1,0:T(8,128)(2,1)}, bf16[784,256]{1,0:T(8,128)(2,1)}, u32[]{:S(2)}, u32[]{:S(2)}) collective-permute-start(bf16[784,256]{1,0:T(8,128)(2,1)} %constant_dynamic-update-slice_fusion), channel_id=1, source_target_pairs={{0,1},{1,0},{2,3},{3,2},{4,5},{5,4},{6,7},{7,6},{8,9},{9,8},{10,11... | collective-permute-start | bytes 1204232 | tf_op jit(solution)/shard_map/ppermute | solution.py:70
  10.2 66.1 %collective-permute-start.6 = (bf16[192,1536]{1,0:T(8,128)(2,1)}, bf16[192,1536]{1,0:T(8,128)(2,1)S(1)}, u32[]{:S(2)}, u32[]{:S(2)}) collective-permute-start(bf16[192,1536]{1,0:T(8,128)(2,1)} %get-tuple-element.121), channel_id=1, source_target_pairs={{0,1},{1,0},{2,3},{3,2},{4,5},{5,4},{6,7},{7,6},{8,9},{9,8},{10,11... | collective-permute-start | bytes 1769480 | tf_op jit(solution)/shard_map/ppermute | solution.py:70
  10.2 64.5 %collective-permute-start.10 = (bf16[192,1536]{1,0:T(8,128)(2,1)}, bf16[192,1536]{1,0:T(8,128)(2,1)S(1)}, u32[]{:S(2)}, u32[]{:S(2)}) collective-permute-start(bf16[192,1536]{1,0:T(8,128)(2,1)} %get-tuple-element.122), channel_id=1, source_target_pairs={{0,1},{1,0},{2,3},{3,2},{4,5},{5,4},{6,7},{7,6},{8,9},{9,8},{10,11... | collective-permute-start | bytes 1769480 | tf_op jit(solution)/shard_map/ppermute | solution.py:70
  12.3 38.8 %collective-permute-start.18 = (bf16[128,1536]{1,0:T(8,128)(2,1)S(1)}, bf16[128,1536]{1,0:T(8,128)(2,1)}, u32[]{:S(2)}, u32[]{:S(2)}) collective-permute-start(bf16[128,1536]{1,0:T(8,128)(2,1)S(1)} %slice.301), channel_id=1, source_target_pairs={{0,1},{1,0},{2,3},{3,2},{4,5},{5,4},{6,7},{7,6},{8,9},{9,8},{10,11... | collective-permute-start | bytes 1179656 | tf_op jit(solution)/shard_map/ppermute | solution.py:70
  66.7 41.5 %collective-permute-start.22 = (bf16[192,2304]{1,0:T(8,128)(2,1)S(1)}, bf16[192,2304]{1,0:T(8,128)(2,1)}, u32[]{:S(2)}, u32[]{:S(2)}) collective-permute-start(bf16[192,2304]{1,0:T(8,128)(2,1)S(1)} %shard_map.179), channel_id=1, source_target_pairs={{0,1},{1,0},{2,3},{3,2},{4,5},{5,4},{6,7},{7,6},{8,9},{9,8},{10,11... | collective-permute-start | bytes 2654216 | tf_op jit(solution)/shard_map/ppermute | solution.py:70
  72.5 34.2 %collective-permute-start.19 = (bf16[256,1536]{1,0:T(8,128)(2,1)S(1)}, bf16[256,1536]{1,0:T(8,128)(2,1)S(1)}, u32[]{:S(2)}, u32[]{:S(2)}) collective-permute-start(bf16[256,1536]{1,0:T(8,128)(2,1)S(1)} %copy-done.84), channel_id=1, source_target_pairs={{0,4},{4,0},{1,5},{5,1},{2,6},{6,2},{3,7},{7,3},{8,12},{12,8},{9,1... | collective-permute-start | bytes 2359304 | tf_op jit(solution)/shard_map/ppermute | solution.py:70
  74.7 42.1 %collective-permute-start.11 = (bf16[192,1536]{1,0:T(8,128)(2,1)S(1)}, bf16[192,1536]{1,0:T(8,128)(2,1)S(1)}, u32[]{:S(2)}, u32[]{:S(2)}) collective-permute-start(bf16[192,1536]{1,0:T(8,128)(2,1)S(1)} %collective-permute-done.10.refs_17_.refs_11_), channel_id=1, source_target_pairs={{0,4},{4,0},{1,5},{5,1},{2,6},{6,2},{3,7},{7,3},{8,12},{12,8},{9,1... | collective-permute-start | bytes 1769480 | tf_op jit(solution)/shard_map/ppermute | solution.py:70
  76.3 51.2 %collective-permute-start.7 = (bf16[192,1536]{1,0:T(8,128)(2,1)S(1)}, bf16[192,1536]{1,0:T(8,128)(2,1)S(1)}, u32[]{:S(2)}, u32[]{:S(2)}) collective-permute-start(bf16[192,1536]{1,0:T(8,128)(2,1)S(1)} %collective-permute-done.6.refs_12_.refs_1_), channel_id=1, source_target_pairs={{0,4},{4,0},{1,5},{5,1},{2,6},{6,2},{3,7},{7,3},{8,12},{12,8},{9,1... | collective-permute-start | bytes 1769480 | tf_op jit(solution)/shard_map/ppermute | solution.py:70
  303.5 50.2 %collective-permute-start.39 = (bf16[2,192,1152]{2,1,0:T(8,128)(2,1)}, bf16[2,192,1152]{2,1,0:T(8,128)(2,1)S(1)}, u32[]{:S(2)}, u32[]{:S(2)}) collective-permute-start(bf16[2,192,1152]{2,1,0:T(8,128)(2,1)} %copy-done.47), channel_id=1, source_target_pairs={{0,8},{8,0},{16,24},{24,16},{1,9},{9,1},{17,25},{25,17},{2,10},{10... | collective-permute-start | bytes 2654216 | tf_op jit(solution)/shard_map/ppermute | solution.py:70
  360.8 47.4 %collective-permute-start.43 = (bf16[1536,768]{1,0:T(8,128)(2,1)}, bf16[1536,768]{1,0:T(8,128)(2,1)}, u32[]{:S(2)}, u32[]{:S(2)}) collective-permute-start(bf16[1536,768]{1,0:T(8,128)(2,1)} %shard_map.193), channel_id=1, source_target_pairs={{0,2},{2,0},{1,3},{3,1},{4,6},{6,4},{5,7},{7,5},{8,10},{10,8},{9,1... | collective-permute-start | bytes 7077896 | tf_op jit(solution)/shard_map/ppermute | solution.py:70
  360.9 32.7 %collective-permute-start.33 = (bf16[1,192,1152]{2,1,0:T(8,128)(2,1)}, bf16[1,192,1152]{2,1,0:T(8,128)(2,1)}, u32[]{:S(2)}, u32[]{:S(2)}) collective-permute-start(bf16[1,192,1152]{2,1,0:T(8,128)(2,1)} %add_convert_fusion.9), channel_id=1, source_target_pairs={{0,16},{8,24},{16,0},{24,8},{1,17},{9,25},{17,1},{25,9},{2,18},{10... | collective-permute-start | bytes 1327112 | tf_op jit(solution)/shard_map/ppermute | solution.py:70
  370.8 46.6 %collective-permute-start.31 = (bf16[256,1536]{1,0:T(8,128)(2,1)S(1)}, bf16[256,1536]{1,0:T(8,128)(2,1)}, u32[]{:S(2)}, u32[]{:S(2)}) collective-permute-start(bf16[256,1536]{1,0:T(8,128)(2,1)S(1)} %copy-done.49), channel_id=1, source_target_pairs={{0,4},{4,0},{1,5},{5,1},{2,6},{6,2},{3,7},{7,3},{8,12},{12,8},{9,1... | collective-permute-start | bytes 2359304 | tf_op jit(solution)/shard_map/ppermute | solution.py:70
  372.6 44.8 %collective-permute-start.46 = (bf16[256,1536]{1,0:T(8,128)(2,1)S(1)}, bf16[256,1536]{1,0:T(8,128)(2,1)}, u32[]{:S(2)}, u32[]{:S(2)}) collective-permute-start(bf16[256,1536]{1,0:T(8,128)(2,1)S(1)} %copy-done.51), channel_id=1, source_target_pairs={{0,1},{1,0},{2,3},{3,2},{4,5},{5,4},{6,7},{7,6},{8,9},{9,8},{10,11... | collective-permute-start | bytes 2359304 | tf_op jit(solution)/shard_map/ppermute | solution.py:70
  407.4 47.5 %collective-permute-start.52 = (bf16[1,192,1152]{2,1,0:T(8,128)(2,1)}, bf16[1,192,1152]{2,1,0:T(8,128)(2,1)}, u32[]{:S(2)}, u32[]{:S(2)}) collective-permute-start(bf16[1,192,1152]{2,1,0:T(8,128)(2,1)} %add_convert_fusion.7), channel_id=1, source_target_pairs={{0,16},{8,24},{16,0},{24,8},{1,17},{9,25},{17,1},{25,9},{2,18},{10... | collective-permute-start | bytes 1327112 | tf_op jit(solution)/shard_map/ppermute | solution.py:70
  408.2 49.7 %collective-permute-start.51 = (bf16[768,768]{1,0:T(8,128)(2,1)S(1)}, bf16[768,768]{1,0:T(8,128)(2,1)S(1)}, u32[]{:S(2)}, u32[]{:S(2)}) collective-permute-start(bf16[768,768]{1,0:T(8,128)(2,1)S(1)} %bitcast.126), channel_id=1, source_target_pairs={{0,1},{1,0},{2,3},{3,2},{4,5},{5,4},{6,7},{7,6},{8,9},{9,8},{10,11... | collective-permute-start | bytes 3538952 | tf_op jit(solution)/shard_map/ppermute | solution.py:70
  424.5 53.1 %collective-permute-start.50 = (bf16[1,288,768]{2,1,0:T(8,128)(2,1)}, bf16[1,288,768]{2,1,0:T(8,128)(2,1)}, u32[]{:S(2)}, u32[]{:S(2)}) collective-permute-start(bf16[1,288,768]{2,1,0:T(8,128)(2,1)} %add_convert_fusion.4), channel_id=1, source_target_pairs={{0,16},{8,24},{16,0},{24,8},{1,17},{9,25},{17,1},{25,9},{2,18},{10... | collective-permute-start | bytes 1327112 | tf_op jit(solution)/shard_map/ppermute | solution.py:70
  451.3 35.9 %collective-permute-start.59 = (bf16[1,192,1152]{2,1,0:T(8,128)(2,1)}, bf16[1,192,1152]{2,1,0:T(8,128)(2,1)}, u32[]{:S(2)}, u32[]{:S(2)}) collective-permute-start(bf16[1,192,1152]{2,1,0:T(8,128)(2,1)} %bitcast.49), channel_id=1, source_target_pairs={{0,16},{8,24},{16,0},{24,8},{1,17},{9,25},{17,1},{25,9},{2,18},{10... | collective-permute-start | bytes 1327112 | tf_op jit(solution)/shard_map/ppermute | solution.py:70
  454.9 35.4 %collective-permute-start.58 = (bf16[768,768]{1,0:T(8,128)(2,1)}, bf16[768,768]{1,0:T(8,128)(2,1)}, u32[]{:S(2)}, u32[]{:S(2)}) collective-permute-start(bf16[768,768]{1,0:T(8,128)(2,1)} %bitcast.48), channel_id=1, source_target_pairs={{0,1},{1,0},{2,3},{3,2},{4,5},{5,4},{6,7},{7,6},{8,9},{9,8},{10,11... | collective-permute-start | bytes 3538952 | tf_op jit(solution)/shard_map/ppermute | solution.py:70
  457.9 37.9 %collective-permute-start.57 = (bf16[1,192,1152]{2,1,0:T(8,128)(2,1)}, bf16[1,192,1152]{2,1,0:T(8,128)(2,1)}, u32[]{:S(2)}, u32[]{:S(2)}) collective-permute-start(bf16[1,192,1152]{2,1,0:T(8,128)(2,1)} %add_convert_fusion.2), channel_id=1, source_target_pairs={{0,16},{8,24},{16,0},{24,8},{1,17},{9,25},{17,1},{25,9},{2,18},{10... | collective-permute-start | bytes 1327112 | tf_op jit(solution)/shard_map/ppermute | solution.py:70
  481.5 33.3 %collective-permute-start.55 = (bf16[2,288,768]{2,1,0:T(8,128)(2,1)}, bf16[2,288,768]{2,1,0:T(8,128)(2,1)}, u32[]{:S(2)}, u32[]{:S(2)}) collective-permute-start(bf16[2,288,768]{2,1,0:T(8,128)(2,1)} %pad_maximum_fusion.4), channel_id=1, source_target_pairs={{0,8},{8,0},{16,24},{24,16},{1,9},{9,1},{17,25},{25,17},{2,10},{10... | collective-permute-start | bytes 2654216 | tf_op jit(solution)/shard_map/ppermute | solution.py:70
  490.3 43.5 %collective-permute-start.65 = (bf16[2,192,1152]{2,1,0:T(8,128)(2,1)}, bf16[2,192,1152]{2,1,0:T(8,128)(2,1)}, u32[]{:S(2)}, u32[]{:S(2)}) collective-permute-start(bf16[2,192,1152]{2,1,0:T(8,128)(2,1)} %pad_maximum_fusion.5), channel_id=1, source_target_pairs={{0,8},{8,0},{16,24},{24,16},{1,9},{9,1},{17,25},{25,17},{2,10},{10... | collective-permute-start | bytes 2654216 | tf_op jit(solution)/shard_map/ppermute | solution.py:70
  495.8 41.4 %collective-permute-start.64 = (bf16[4,96,768]{2,1,0:T(8,128)(2,1)}, bf16[4,96,768]{2,1,0:T(8,128)(2,1)}, u32[]{:S(2)}, u32[]{:S(2)}) collective-permute-start(bf16[4,96,768]{2,1,0:T(8,128)(2,1)} %get-tuple-element.296), channel_id=1, source_target_pairs={{0,4},{4,0},{1,5},{5,1},{2,6},{6,2},{3,7},{7,3},{8,12},{12,8},{9,1... | collective-permute-start | bytes 1769480 | tf_op jit(solution)/shard_map/ppermute | solution.py:70
  499.7 52.9 %collective-permute-start.63 = (bf16[2,192,1152]{2,1,0:T(8,128)(2,1)}, bf16[2,192,1152]{2,1,0:T(8,128)(2,1)}, u32[]{:S(2)}, u32[]{:S(2)}) collective-permute-start(bf16[2,192,1152]{2,1,0:T(8,128)(2,1)} %pad_maximum_fusion.6), channel_id=1, source_target_pairs={{0,8},{8,0},{16,24},{24,16},{1,9},{9,1},{17,25},{25,17},{2,10},{10... | collective-permute-start | bytes 2654216 | tf_op jit(solution)/shard_map/ppermute | solution.py:70
  516.4 49.4 %collective-permute-start.61 = (bf16[4,288,768]{2,1,0:T(8,128)(2,1)S(1)}, bf16[4,288,768]{2,1,0:T(8,128)(2,1)S(1)}, u32[]{:S(2)}, u32[]{:S(2)}) collective-permute-start(bf16[4,288,768]{2,1,0:T(8,128)(2,1)S(1)} %pad_maximum_fusion.refs_0_), channel_id=1, source_target_pairs={{0,4},{4,0},{1,5},{5,1},{2,6},{6,2},{3,7},{7,3},{8,12},{12,8},{9,1... | collective-permute-start | bytes 5308424 | tf_op jit(solution)/shard_map/ppermute | solution.py:70
  535.4 102.2 %collective-permute-start.71 = (bf16[4,192,1152]{2,1,0:T(8,128)(2,1)S(1)}, bf16[4,192,1152]{2,1,0:T(8,128)(2,1)S(1)}, u32[]{:S(2)}, u32[]{:S(2)}) collective-permute-start(bf16[4,192,1152]{2,1,0:T(8,128)(2,1)S(1)} %pad_maximum_fusion.1.refs_0_), channel_id=1, source_target_pairs={{0,4},{4,0},{1,5},{5,1},{2,6},{6,2},{3,7},{7,3},{8,12},{12,8},{9,1... | collective-permute-start | bytes 5308424 | tf_op jit(solution)/shard_map/ppermute | solution.py:70
  554.3 90.7 %collective-permute-start.69 = (bf16[4,192,1152]{2,1,0:T(8,128)(2,1)S(1)}, bf16[4,192,1152]{2,1,0:T(8,128)(2,1)S(1)}, u32[]{:S(2)}, u32[]{:S(2)}) collective-permute-start(bf16[4,192,1152]{2,1,0:T(8,128)(2,1)S(1)} %pad_maximum_fusion.2.refs_0_), channel_id=1, source_target_pairs={{0,4},{4,0},{1,5},{5,1},{2,6},{6,2},{3,7},{7,3},{8,12},{12,8},{9,1... | collective-permute-start | bytes 5308424 | tf_op jit(solution)/shard_map/ppermute | solution.py:70
  556.1 99.3 %collective-permute-start.67 = (bf16[4,288,768]{2,1,0:T(8,128)(2,1)S(1)}, bf16[4,288,768]{2,1,0:T(8,128)(2,1)S(1)}, u32[]{:S(2)}, u32[]{:S(2)}) collective-permute-start(bf16[4,288,768]{2,1,0:T(8,128)(2,1)S(1)} %pad_maximum_fusion.refs_0_), channel_id=1, source_target_pairs={{0,2},{2,0},{1,3},{3,1},{4,6},{6,4},{5,7},{7,5},{8,10},{10,8},{9,1... | collective-permute-start | bytes 5308424 | tf_op jit(solution)/shard_map/ppermute | solution.py:70
  565.5 71.5 %collective-permute-start.60 = (bf16[4,96,256]{2,1,0:T(8,128)(2,1)S(1)}, bf16[4,96,256]{2,1,0:T(8,128)(2,1)S(1)}, u32[]{:S(2)}, u32[]{:S(2)}) collective-permute-start(bf16[4,96,256]{2,1,0:T(8,128)(2,1)S(1)} %get-tuple-element.297), channel_id=1, source_target_pairs={{0,4},{4,0},{1,5},{5,1},{2,6},{6,2},{3,7},{7,3},{8,12},{12,8},{9,1... | collective-permute-start | bytes 589832 | tf_op jit(solution)/shard_map/ppermute | solution.py:70
  565.9 90.0 %collective-permute-start.72 = (bf16[4,288,768]{2,1,0:T(8,128)(2,1)S(1)}, bf16[4,288,768]{2,1,0:T(8,128)(2,1)S(1)}, u32[]{:S(2)}, u32[]{:S(2)}) collective-permute-start(bf16[4,288,768]{2,1,0:T(8,128)(2,1)S(1)} %collective-permute-done.61.refs_1_), channel_id=1, source_target_pairs={{0,2},{2,0},{1,3},{3,1},{4,6},{6,4},{5,7},{7,5},{8,10},{10,8},{9,1... | collective-permute-start | bytes 5308424 | tf_op jit(solution)/shard_map/ppermute | solution.py:70
  637.7 35.0 %collective-permute-start.77 = (bf16[4,192,1152]{2,1,0:T(8,128)(2,1)S(1)}, bf16[4,192,1152]{2,1,0:T(8,128)(2,1)S(1)}, u32[]{:S(2)}, u32[]{:S(2)}) collective-permute-start(bf16[4,192,1152]{2,1,0:T(8,128)(2,1)S(1)} %pad_maximum_fusion.1.refs_0_), channel_id=1, source_target_pairs={{0,2},{2,0},{1,3},{3,1},{4,6},{6,4},{5,7},{7,5},{8,10},{10,8},{9,1... | collective-permute-start | bytes 5308424 | tf_op jit(solution)/shard_map/ppermute | solution.py:70
  655.3 32.3 %collective-permute-start.75 = (bf16[4,192,1152]{2,1,0:T(8,128)(2,1)S(1)}, bf16[4,192,1152]{2,1,0:T(8,128)(2,1)S(1)}, u32[]{:S(2)}, u32[]{:S(2)}) collective-permute-start(bf16[4,192,1152]{2,1,0:T(8,128)(2,1)S(1)} %pad_maximum_fusion.2.refs_0_), channel_id=1, source_target_pairs={{0,2},{2,0},{1,3},{3,1},{4,6},{6,4},{5,7},{7,5},{8,10},{10,8},{9,1... | collective-permute-start | bytes 5308424 | tf_op jit(solution)/shard_map/ppermute | solution.py:70
  655.4 32.2 %collective-permute-start.79 = (bf16[4,192,1152]{2,1,0:T(8,128)(2,1)S(1)}, bf16[4,192,1152]{2,1,0:T(8,128)(2,1)}, u32[]{:S(2)}, u32[]{:S(2)}) collective-permute-start(bf16[4,192,1152]{2,1,0:T(8,128)(2,1)S(1)} %collective-permute-done.69.refs_1_), channel_id=1, source_target_pairs={{0,2},{2,0},{1,3},{3,1},{4,6},{6,4},{5,7},{7,5},{8,10},{10,8},{9,1... | collective-permute-start | bytes 5308424 | tf_op jit(solution)/shard_map/ppermute | solution.py:70
  (172 other events, 2450.1 us)

commit v3 on v2

v3 whole, which is shorter than its diff:
```python
import functools
import math

import jax
import jax.numpy as jnp
from jax import lax
from jax.experimental import pallas as pl
from jax.experimental.pallas import tpu as pltpu
from jax.sharding import Mesh
from jax.sharding import PartitionSpec as P

H = 12
HD = 128
FF = 4608
WINDOW = 1024
EPSILON = 1e-06
BF = jnp.bfloat16
F32 = jnp.float32
VMEM_LIMIT = 48 * 1024 * 1024


def tables(places, width):
    half_width = width // 2
    frequency = jnp.exp(
        jnp.arange(half_width, dtype=jnp.float32) * (-2.0 * math.log(10000.0) / width)
    )
    angles = places.astype(jnp.float32)[:, None] * frequency[None, :]
    return (jnp.cos(angles), jnp.sin(angles))


def rotate(values, cosine, sine):
    turned = jnp.concatenate([values[:, HD // 2 :], values[:, : HD // 2]], axis=1)
    return values * cosine + turned * sine


def rms_factor(values):
    return lax.rsqrt(jnp.mean(values * values, axis=-1, keepdims=True) + EPSILON)


def segment_info(places, seq_lengths):
    seq_ends = jnp.cumsum(seq_lengths)
    passed = places[:, None] >= seq_ends[None, :]
    segment = jnp.sum(passed.astype(jnp.int32), axis=1)
    seq_start = jnp.sum(jnp.where(passed, seq_lengths[None, :], 0), axis=1)
    return (segment, places - seq_start)


def dot(a, b):
    return jnp.dot(a, b, preferred_element_type=F32)


def dot_t(a, b):
    return lax.dot_general(a, b, (((1,), (1,)), ((), ())), preferred_element_type=F32)


def t_dot(a, b):
    return lax.dot_general(a, b, (((0,), (0,)), ((), ())), preferred_element_type=F32)


def after(value, *earlier):
    return lax.optimization_barrier((value,) + earlier)[0]


def shift(array, axis, mask):
    return lax.ppermute(array, axis, [(i, i ^ mask) for i in range(lax.axis_size(axis))])


def bit(axis, k=0):
    return (lax.axis_index(axis) >> k) & 1


def pick(array, index, dim):
    return lax.dynamic_index_in_dim(array, index, dim, keepdims=False)


def add(a, b):
    return (a.astype(F32) + b.astype(F32)).astype(BF)


def by_place(entries, axis_name):
    if len(entries) == 2:
        low, high = jnp.stack(entries), jnp.stack(entries[::-1])
        return jnp.where(lax.axis_index(axis_name) == 0, low, high)
    order = jnp.arange(len(entries), dtype=jnp.int32) ^ lax.axis_index(axis_name)
    return jnp.take(jnp.stack(entries), order, axis=0)


def kernel_call(function, **options):
    return pl.pallas_call(
        function,
        compiler_params=pltpu.CompilerParams(vmem_limit_bytes=VMEM_LIMIT),
        cost_estimate=pl.CostEstimate(flops=1000, bytes_accessed=1000, transcendentals=0),
        **options,
    )


def whole_spec(array):
    zeros = (0,) * array.ndim
    return pl.BlockSpec(array.shape, lambda *_: zeros)


ANY = pl.BlockSpec(memory_space=pl.ANY)


def load_rows(target, pieces, rows, sem):
    copies = []
    for n, piece in enumerate(pieces):
        start = pl.multiple_of(rows[n], 16)
        copies.append(
            pltpu.make_async_copy(piece, target.at[pl.ds(start, piece.shape[0])], sem.at[n])
        )
    for copy in copies:
        copy.start()
    return copies


def copy_kernel(blocks, spots, *refs):
    parts, out, sem = refs[:-2], refs[-2], refs[-1]
    copies = []
    for n, (part, rows, columns) in enumerate(blocks):
        at = [pl.multiple_of(spots[n, 0], 16), pl.multiple_of(spots[n, 1], 128)]
        to = [pl.multiple_of(spots[n, 2], 16), pl.multiple_of(spots[n, 3], 128)]
        copies.append(
            pltpu.make_async_copy(
                parts[part].at[pl.ds(at[0], rows), pl.ds(at[1], columns)],
                out.at[pl.ds(to[0], rows), pl.ds(to[1], columns)],
                sem.at[n],
            )
        )
    for copy in copies:
        copy.start()
    for copy in copies:
        copy.wait()


def lay_out(shape, parts, moves):
    aligned = all(size[0] % 16 == 0 and size[1] % 128 == 0 for _, size, _, _ in moves)
    if not aligned:
        out = jnp.zeros(shape, parts[0].dtype)
        for part, size, at, to in moves:
            out = lax.dynamic_update_slice(out, lax.dynamic_slice(parts[part], at, size), to)
        return out
    spots = jnp.stack(
        [jnp.stack([jnp.asarray(v, jnp.int32) for v in at + to]) for _, _, at, to in moves]
    )
    blocks = tuple((part,) + size for part, size, _, _ in moves)
    return kernel_call(
        functools.partial(copy_kernel, blocks),
        out_shape=jax.ShapeDtypeStruct(shape, parts[0].dtype),
        in_specs=[pl.BlockSpec(memory_space=pltpu.SMEM)] + [ANY] * len(parts),
        out_specs=pl.BlockSpec(memory_space=pltpu.VMEM),
        scratch_shapes=[pltpu.SemaphoreType.DMA((len(moves),))],
    )(spots, *parts)


def widen_kernel(count, maps, *refs):
    parts, out = refs[:count], refs[-1]
    source = pl.program_id(1) ^ maps[0]
    for n in range(count):

        @pl.when(source == n)
        def _(n=n):
            out[...] = parts[n][...].reshape(out.shape).astype(F32)


def widen(parts, beside, z_places, out_shape, spot, so_far=None):
    count = len(parts)
    z_count, rows, columns = parts[0].shape
    x_at, c_at, y_at = (lax.axis_index(name) for name in ("x", "c", "y"))
    if count == 2:
        flips = [c_at, x_at ^ (1 if beside else 0), y_at]
    else:
        flips = [c_at * 2 + x_at, x_at, y_at]
    if columns % 128 or rows % 16:
        out = jnp.zeros(out_shape, F32) if so_far is None else so_far
        ordered = jnp.stack(parts)
        for z in range(z_count):
            for k in range(count):
                block = ordered[k ^ flips[0], z_places[z]]
                at = spot(z, k, flips[1], y_at) if count == 2 else spot(z, k // 2, k % 2, y_at)
                out = lax.dynamic_update_slice(
                    out, block.astype(F32), (at[0] * rows, at[1] * columns)
                )
        return out
    maps = jnp.concatenate([jnp.stack(flips).astype(jnp.int32), z_places])

    def out_map(z, k, maps):
        if count == 2:
            return spot(z, k, maps[1], maps[2])
        return spot(z, k // 2, k % 2, maps[2])

    specs = [pl.BlockSpec((1, rows, columns), lambda z, k, maps: (maps[3 + z], 0, 0))] * count
    operands = list(parts)
    aliases = {}
    if so_far is not None:
        specs.append(ANY)
        operands.append(so_far)
        aliases = {count + 1: 0}
    return kernel_call(
        functools.partial(widen_kernel, count),
        grid_spec=pltpu.PrefetchScalarGridSpec(
            num_scalar_prefetch=1,
            grid=(z_count, count),
            in_specs=specs,
            out_specs=pl.BlockSpec((rows, columns), out_map),
        ),
        out_shape=jax.ShapeDtypeStruct(out_shape, F32),
        input_output_aliases=aliases,
    )(maps, *operands)


def once_kernel(function, n_in, maps, *refs):
    function(maps, refs[:n_in], refs[n_in:])


def once(function, shapes, *operands, maps=None):
    if maps is None:
        maps = jnp.zeros((1,), jnp.int32)
    return kernel_call(
        functools.partial(once_kernel, function, len(operands)),
        in_specs=[pl.BlockSpec(memory_space=pltpu.SMEM)]
        + [pl.BlockSpec(memory_space=pltpu.VMEM)] * len(operands),
        out_specs=[pl.BlockSpec(memory_space=pltpu.VMEM)] * len(shapes),
        out_shape=[jax.ShapeDtypeStruct(shape, kind) for shape, kind in shapes],
    )(maps, *operands)


def add_halves(kept, got):
    half = kept.shape[0] // 2
    if not half:

        def narrow(_, ins, outs):
            outs[0][...] = (ins[0][...].astype(F32) + ins[1][...].astype(F32)).astype(BF)

        return once(narrow, [(kept.shape, BF)], kept, got)

    def function(_, ins, outs):
        for n in range(2):
            part = pl.ds(n * half, half)
            outs[n][...] = (ins[0][part].astype(F32) + ins[1][part].astype(F32)).astype(BF)

    shape = ((half,) + kept.shape[1:], BF)
    return once(function, [shape, shape], kept, got)


def stack_two(held, got):
    count = held.shape[0]

    def function(_, ins, outs):
        outs[0][:count] = ins[0][...]
        outs[0][count:] = ins[1][...]

    return once(function, [((2 * count,) + held.shape[1:], BF)], held, got)[0]


def kv_kernel(rows, tokens, gain, cosine, sine, *refs):
    pieces = refs[:-4]
    normed, keyval, w_kv, sem = refs[-4:]
    copies = []
    for n, piece in enumerate(pieces):
        start = pl.multiple_of(rows[n], 16)
        copies.append(
            pltpu.make_async_copy(piece, w_kv.at[pl.ds(start, piece.shape[0])], sem.at[n])
        )
    for copy in copies:
        copy.start()
    inputs = tokens[...].astype(F32)
    normed[...] = (inputs * rms_factor(inputs) * gain[...]).astype(BF)
    for copy in copies:
        copy.wait()
    raw = dot(normed[...], w_kv[...])
    keyval[:, :HD] = rotate(raw[:, :HD], cosine[...], sine[...]).astype(BF)
    keyval[:, HD:] = raw[:, HD:].astype(BF)


def norm_back_rows(grad_normed, values, factor, gain):
    scaled = grad_normed * gain
    mean = jnp.mean(scaled * values, axis=-1, keepdims=True)
    return factor * scaled - values * (factor * factor * factor) * mean


def attend_kernel(n_q, n_o, spans, maps, *refs):
    normed, tokens, gain, bias, cosine, sine = refs[:6]
    blocks = refs[6 : 6 + spans]
    at = 6 + spans
    q_pieces, o_pieces = refs[at : at + n_q], refs[at + n_q : at + n_q + n_o]
    queries, attended, hidden, own_norm, factor = refs[at + n_q + n_o : at + n_q + n_o + 5]
    w_q, w_o, keys, values, total, q_sem, o_sem = refs[at + n_q + n_o + 5 :]
    step = pl.program_id(0)
    rows = normed.shape[0]

    @pl.when(step == 0)
    def _():
        first = load_rows(w_q, q_pieces, [maps[spans + n] for n in range(n_q)], q_sem)
        second = load_rows(w_o, o_pieces, [maps[spans + n_q + n] for n in range(n_o)], o_sem)
        for n in range(spans):
            keys[n * rows : (n + 1) * rows, :] = blocks[n][0, :, :HD]
            values[n * rows : (n + 1) * rows, :] = blocks[n][0, :, HD:]
        total[...] = tokens[...].astype(F32)
        for copy in first + second:
            copy.wait()

    columns = pl.ds(pl.multiple_of(step * 2 * HD, 2 * HD), 2 * HD)
    raw = dot(normed[...], w_q[:, columns])
    done = []
    for n in range(2):
        turned = rotate(raw[:, n * HD : (n + 1) * HD], cosine[...], sine[...])
        query = (turned * HD ** (-0.5)).astype(BF)
        queries[:, n * HD : (n + 1) * HD] = query
        scores = dot_t(query, keys[...]) + bias[...]
        weights = jnp.exp(scores - jnp.max(scores, axis=-1, keepdims=True))
        share = 1.0 / jnp.sum(weights, axis=-1, keepdims=True)
        done.append(dot((weights * share).astype(BF), values[...]).astype(BF))
    both = jnp.concatenate(done, axis=1)
    attended[...] = both
    total[...] += dot(both, w_o[columns, :])

    @pl.when(step == pl.num_programs(0) - 1)
    def _():
        out = total[...]
        hidden[...] = out
        scale = rms_factor(out)
        factor[...] = jnp.broadcast_to(scale, factor.shape)
        own_norm[...] = (out * scale * gain[...]).astype(BF)


def attend_back_kernel(n_o, spans, entry_count, maps, *refs):
    d_attn, queries, bias, cosine, sine = refs[:5]
    blocks = refs[5 : 5 + spans]
    pieces = refs[5 + spans : 5 + spans + n_o]
    d_raw, kept, sent = refs[5 + spans + n_o : 8 + spans + n_o]
    w_o, keys, values, d_keys, d_values, d_window, sem = refs[8 + spans + n_o :]
    step = pl.program_id(0)
    rows = d_attn.shape[0]

    @pl.when(step == 0)
    def _():
        base = spans + entry_count
        copies = load_rows(w_o, pieces, [maps[base + n] for n in range(n_o)], sem)
        for n in range(spans):
            keys[n * rows : (n + 1) * rows, :] = blocks[n][0, :, :HD]
            values[n * rows : (n + 1) * rows, :] = blocks[n][0, :, HD:]
        d_keys[...] = jnp.zeros_like(d_keys)
        d_values[...] = jnp.zeros_like(d_values)
        for copy in copies:
            copy.wait()

    w_rows = pl.ds(pl.multiple_of(step * 2 * HD, 2 * HD), 2 * HD)
    d_both = dot_t(d_attn[...], w_o[w_rows, :]).astype(BF)
    for n in range(2):
        query = queries[:, n * HD : (n + 1) * HD]
        d_out = d_both[:, n * HD : (n + 1) * HD]
        scores = dot_t(query, keys[...]) + bias[...]
        weights = jnp.exp(scores - jnp.max(scores, axis=-1, keepdims=True))
        soft = weights * (1.0 / jnp.sum(weights, axis=-1, keepdims=True))
        d_soft = dot_t(d_out, values[...])
        delta = jnp.sum(soft * d_soft, axis=-1, keepdims=True)
        d_scores = (soft * (d_soft - delta)).astype(BF)
        d_query = dot(d_scores, keys[...]) * HD ** (-0.5)
        d_raw[:, n * HD : (n + 1) * HD] = rotate(d_query, cosine[...], -sine[...]).astype(BF)
        d_keys[...] += t_dot(query, d_scores)
        d_values[...] += t_dot(d_out, soft.astype(BF))

    @pl.when(step == pl.num_programs(0) - 1)
    def _():
        d_window[: spans * rows, :HD] = d_keys[...].T.astype(BF)
        d_window[: spans * rows, HD:] = d_values[...].T.astype(BF)
        d_window[spans * rows :, :] = jnp.zeros((rows, 2 * HD), BF)
        for n in range(entry_count):
            out = kept if n < entry_count // 2 else sent
            start = pl.multiple_of(maps[spans + n] * rows, rows)
            out[n % (entry_count // 2)] = d_window[pl.ds(start, rows), :]


ROOT = math.sqrt(2.0 / math.pi)


def forward_kernel(n_tok, maps, *refs):
    pieces = refs[:n_tok]
    cot, w_gate, w_up, w_down = refs[n_tok : n_tok + 4]
    inner, inner_t, d_both, normed_t, normed, sem = refs[n_tok + 4 :]

    @pl.when(pl.program_id(0) == 0)
    def _():
        at = 0
        copies = []
        for n, piece in enumerate(pieces):
            copies.append(
                pltpu.make_async_copy(piece, normed.at[pl.ds(at, piece.shape[0])], sem.at[n])
            )
            at += piece.shape[0]
        for copy in copies:
            copy.start()
        for copy in copies:
            copy.wait()

    wide = normed_t.shape[0]
    columns = pl.ds(pl.multiple_of(pl.program_id(0) * wide, 128), wide)
    gate, up = dot(normed[...], w_gate[...]), dot(normed[...], w_up[...])
    d_inner = dot_t(cot[...], w_down[...])
    square = gate * gate
    bent = jnp.tanh(ROOT * (gate + 0.044715 * (square * gate)))
    half = 0.5 * (1.0 + bent)
    active = gate * half
    slope = half + 0.5 * gate * (1.0 - bent * bent) * (ROOT * (1.0 + 3 * 0.044715 * square))
    result = (active * up).astype(BF)
    inner[...] = result
    inner_t[...] = result.T
    d_both[0] = (d_inner * up * slope).astype(BF)
    d_both[1] = (d_inner * active).astype(BF)
    normed_t[...] = normed[:, columns].T


def cut_rows(result, picks, outs):
    for out, starts in zip(outs, picks, strict=True):
        rows = out.shape[1]
        for n, start in enumerate(starts):
            out[n] = result[start : start + rows].astype(BF)


def back_kernel(picks, d_both, w_gu, *outs):
    units = d_both.shape[2]
    result = dot_t(d_both[0], w_gu[:, :units]) + dot_t(d_both[1], w_gu[:, units:])
    cut_rows(result, picks, outs)


def down_kernel(picks, maps, inner, w_down, *outs):
    cut_rows(dot(inner[...], w_down[...]), picks, outs)


def grad_kernel(turned, groups, block_rows, added, maps, left, right, *refs):
    product = dot if turned else t_dot
    result = product(left[...], right[...].reshape(right.shape[-2:]))
    if added:
        result = result + refs[0][...].astype(F32)
    outs = refs[1:] if added else refs
    if groups is None:
        outs[0][...] = result.astype(BF)
        return
    total = outs[-1]
    total[...] = result
    place = 0
    for n, count in enumerate(groups):
        for k in range(count):
            start = pl.multiple_of(maps[2 + place] * block_rows, 16)
            outs[n][k] = total[pl.ds(start, block_rows), :].astype(BF)
            place += 1


def grad(
    left, left_block, left_columns, right, half, added=None, groups=None, order=None, turned=False
):
    tokens = left.shape[1 if turned else 0]
    if right.ndim == 3:
        columns = right.shape[2]
    else:
        columns = right.shape[1] // 2
    blocks = 0 if groups is None else sum(groups)
    block_rows = 0 if groups is None else left_columns // blocks
    if columns % 128 or left_columns % 128 or block_rows % 16:
        cut = lax.dynamic_slice_in_dim(
            left, left_block * left_columns, left_columns, 0 if turned else 1
        )
        if right.ndim == 3:
            other = pick(right, half, 0)
        else:
            other = lax.dynamic_slice_in_dim(right, half * columns, columns, 1)
        result = dot(cut, other) if turned else t_dot(cut, other)
        if added is not None:
            result = result + added.astype(F32)
        result = result.astype(BF)
        if groups is None:
            return result
        result = jnp.take(result.reshape(blocks, block_rows, columns), order, axis=0)
        outs, at = [], 0
        for count in groups:
            outs.append(result[at : at + count])
            at += count
        return outs
    wide = 384 if columns % 384 == 0 else (256 if columns % 256 == 0 else 128)
    steps = columns // wide
    maps = jnp.stack([jnp.asarray(left_block, jnp.int32), jnp.asarray(half, jnp.int32)])
    if groups is not None:
        maps = jnp.concatenate([maps, order.astype(jnp.int32)])
    if turned:
        in_specs = [pl.BlockSpec((left_columns, tokens), lambda i, maps: (maps[0], 0))]
    else:
        in_specs = [pl.BlockSpec((tokens, left_columns), lambda i, maps: (0, maps[0]))]
    if right.ndim == 3:
        in_specs.append(pl.BlockSpec((1, tokens, wide), lambda i, maps: (maps[1], 0, i)))
    else:
        in_specs.append(pl.BlockSpec((tokens, wide), lambda i, maps: (0, maps[1] * steps + i)))
    operands = [left, right]
    if added is not None:
        in_specs.append(pl.BlockSpec((left_columns, wide), lambda i, maps: (0, i)))
        operands.append(added)
    scratch = []
    if groups is None:
        shapes = [jax.ShapeDtypeStruct((left_columns, columns), BF)]
        out_specs = [pl.BlockSpec((left_columns, wide), lambda i, maps: (0, i))]
    else:
        shapes = [jax.ShapeDtypeStruct((count, block_rows, columns), BF) for count in groups]
        out_specs = [
            pl.BlockSpec((count, block_rows, wide), lambda i, maps: (0, 0, i)) for count in groups
        ]
        scratch = [pltpu.VMEM((left_columns, wide), F32)]
    outs = kernel_call(
        functools.partial(grad_kernel, turned, groups, block_rows, added is not None),
        grid_spec=pltpu.PrefetchScalarGridSpec(
            num_scalar_prefetch=1,
            grid=(steps,),
            in_specs=in_specs,
            out_specs=out_specs,
            scratch_shapes=scratch,
        ),
        out_shape=shapes,
    )(maps, *operands)
    return outs[0] if groups is None else outs


class Clock:
    def __init__(self):
        self.marks = ()

    def tie(self, value):
        return after(value, *self.marks) if self.marks else value

    def mark(self, *values):
        self.marks = values


PLAN = (
    "D",
    "W",
    "D",
    "back",
    "baW",
    "D",
    "down",
    "ae",
    "bO",
    "W",
    "a",
    "b",
    "hid",
    "D",
    "T",
    "att",
    "T",
    "QvOW",
    "Q",
    "D",
    "v",
    "T",
    "Oe",
    "v",
    "D",
    "Q",
    "T",
    "Wv",
    "T",
    "tok",
    "O",
    "eKT",
    "K",
    "WT",
    "DOK",
    "Tf",
    "KQ",
    "O",
    "KQ",
    "TQO",
    "fKW",
    "T",
    "K",
    "Q",
    "D",
    "K",
    "Q",
    "O",
    "W",
    "Q",
    "O",
    "Kf",
    "Q",
    "K",
)


def body(
    tokens,
    cotangent,
    lengths,
    block_of,
    gain_attn,
    w_query,
    w_keyval,
    w_out,
    gain_mlp,
    w_gateup,
    w_down,
):
    tok_rows, width = tokens.shape
    y_count, z_count = lax.axis_size("y"), lax.axis_size("z")
    ctx_count = 4 * z_count
    z_levels = z_count.bit_length() - 1
    x_at, c_at, y_at, z_at = (lax.axis_index(name) for name in ("x", "c", "y", "z"))
    own_index = (z_at * 2 + x_at) * 2 + c_at
    deep = w_query.shape[0]
    quarter = deep // 4
    units = FF // (2 * y_count)
    half_tok = tok_rows // 2
    group = 2 * y_count
    others = range(1, y_count)
    clock = Clock()
    tie, mark = clock.tie, clock.mark

    own_gains = jnp.zeros((16, deep), BF).at[0].set(gain_attn).at[1].set(gain_mlp)
    got_gains = [shift(own_gains, "y", r) for r in others]
    kv_weights = [w_keyval] + [shift(w_keyval, "y", r) for r in others]
    cot_x = shift(cotangent, "x", 1)
    place_cx = c_at * 2 + x_at
    place_cz = c_at * 2 + (z_at & 1)

    def rows_of(weight, place):
        return lax.dynamic_slice_in_dim(weight, place * quarter, quarter, 0)

    wq_piece = after(rows_of(w_query, place_cx), own_gains)
    wq_y = {r: shift(wq_piece, "y", r) for r in others}
    wo_piece = after(rows_of(w_out, place_cx), wq_piece)
    wo_y = {r: shift(wo_piece, "y", r) for r in others}
    gu_sent = {}
    for r in others:
        column = ((y_at ^ r) * 2 + x_at) * units
        moves = [
            (0, (quarter, units), (place_cz * quarter, part * FF + column), (0, part * units))
            for part in (0, 1)
        ]
        gu_sent[r] = lay_out((quarter, 2 * units), [after(w_gateup, wo_piece)], moves)

    def listed(shard, found, place):
        pieces, rows = [shard], [y_at * deep]
        for r, quarters in found.items():
            for s, piece in enumerate(quarters):
                pieces.append(piece)
                rows.append((y_at ^ r) * deep + (place ^ s) * quarter)
        return pieces, rows

    device_ids = jnp.arange(ctx_count, dtype=jnp.int32)
    block_row = block_of[0]
    own_block = jnp.sum(jnp.where(device_ids == own_index, block_row, 0))
    own_start = own_block * tok_rows
    owners = jnp.sum(
        jnp.where(block_row[None, :] == device_ids[:, None], device_ids[None, :], 0), axis=1
    )
    seq_lengths = lengths[0]
    query_places = own_start + jnp.arange(tok_rows, dtype=jnp.int32)
    key_places = own_start - WINDOW + jnp.arange(WINDOW + tok_rows, dtype=jnp.int32)
    query_segment, query_position = segment_info(query_places, seq_lengths)
    key_segment = segment_info(key_places, seq_lengths)[0]
    distance = query_places[:, None] - key_places[None, :]
    allowed = (
        (query_segment[:, None] == key_segment[None, :])
        & (key_places >= 0)[None, :]
        & (distance >= 0)
        & (distance < WINDOW)
    )
    bias = jnp.where(allowed, 0.0, -1e30).astype(F32)
    cosine, sine = tables(query_position, HD)
    cosine = jnp.concatenate([cosine, cosine], axis=1)
    sine = jnp.concatenate([-sine, sine], axis=1)
    spans = WINDOW // tok_rows + 1
    first_block = own_block - (spans - 1)

    def entry_of(ctx_index):
        differ = ctx_index ^ own_index
        return ((differ >> 1) & 1) | ((differ >> 2) << 1) | ((differ & 1) << (z_levels + 1))

    window = first_block + jnp.arange(spans, dtype=jnp.int32)
    window = entry_of(jnp.take(owners, jnp.clip(window, 0, ctx_count - 1)))
    entries = jnp.arange(ctx_count, dtype=jnp.int32)
    differ = ((entries >> 1) & (z_count - 1)) << 2
    differ = differ | ((entries & 1) << 1) | (entries >> (z_levels + 1))
    entry_block = jnp.take(block_row, differ ^ own_index) - first_block
    entry_block = jnp.where((entry_block >= 0) & (entry_block < spans), entry_block, spans)

    z_places = jnp.zeros((z_count,), jnp.int32)
    z_differ = jnp.arange(z_count, dtype=jnp.int32) ^ z_at
    for n, level in enumerate(reversed(range(z_levels))):
        z_places = z_places | (((z_differ >> level) & 1) << n)
    z_order = jnp.zeros((z_count,), jnp.int32)
    for level in range(z_levels):
        z_order = z_order | (
            ((jnp.arange(z_count, dtype=jnp.int32) >> (z_levels - 1 - level)) & 1) << level
        )
    z_order = z_order ^ z_at

    gains = by_place([own_gains[:2]] + [g[:2] for g in got_gains], "y")
    gains = jnp.swapaxes(gains, 0, 1).reshape(2, width).astype(F32)
    gain_one, gain_two = gains[:1], gains[1:]
    kv_rows = jnp.stack([(y_at ^ r) * deep for r in range(y_count)]).astype(jnp.int32)
    in_vmem = pl.BlockSpec(memory_space=pltpu.VMEM)
    normed, keyval = kernel_call(
        kv_kernel,
        in_specs=[pl.BlockSpec(memory_space=pltpu.SMEM)] + [in_vmem] * 4 + [ANY] * y_count,
        out_specs=[in_vmem, in_vmem],
        out_shape=[
            jax.ShapeDtypeStruct((tok_rows, width), BF),
            jax.ShapeDtypeStruct((tok_rows, 2 * HD), BF),
        ],
        scratch_shapes=[pltpu.VMEM((width, 2 * HD), BF), pltpu.SemaphoreType.DMA((y_count,))],
    )(kv_rows, tokens, gain_one, cosine, sine, *kv_weights)
    mark(keyval, bias, z_order, z_places, entry_block, window)
    held = stack_two(keyval[None], tie(shift(keyval, "x", 1)[None]))
    mark(held)
    over_z = [shift(held, "z", d) for d in range(1, z_count)]
    wq_y = {r: tie(piece) for r, piece in wq_y.items()}
    mark(*wq_y.values())
    wq_found = {r: [piece, shift(piece, "x", 1)] for r, piece in wq_y.items()}
    wo_y = {r: tie(piece) for r, piece in wo_y.items()}
    mark(*wo_y.values())
    cot_y = {r: shift(tie(cotangent), "y", r) for r in others}
    wq_found = {r: [pair[0], tie(pair[1])] for r, pair in wq_found.items()}
    mark(*[pair[1] for pair in wq_found.values()])
    wo_found = {r: [tie(piece), shift(tie(piece), "x", 1)] for r, piece in wo_y.items()}

    def stack_all(_, ins, outs):
        for n, part in enumerate(ins):
            outs[0][n * 2 : n * 2 + 2] = part[...]

    held = once(
        stack_all,
        [((2 * z_count, tok_rows, 2 * HD), BF)],
        held,
        *[tie(part) for part in over_z],
    )[0]
    mark(held)
    across = shift(held, "c", 1)
    wq_found = {r: pair + [shift(tie(p), "c", 1) for p in pair] for r, pair in wq_found.items()}
    cot_x = tie(cot_x)
    cot_corner_b = {r: shift(cot_x[half_tok:], "y", r) for r in others}
    gu_y = {r: shift(tie(piece), "y", r) for r, piece in gu_sent.items()}
    wo_found = {r: [pair[0], tie(pair[1])] for r, pair in wo_found.items()}
    mark(*[pair[1] for pair in wo_found.values()])
    wo_found = {r: pair + [shift(tie(p), "c", 1) for p in pair] for r, pair in wo_found.items()}
    cot_y = {r: tie(part) for r, part in cot_y.items()}
    cot_slices = {r: part[:half_tok] for r, part in cot_y.items()}
    mark(*cot_slices.values())
    cot_corner_a = {r: shift(part, "x", 1) for r, part in cot_slices.items()}

    all_kv = stack_two(held, tie(across))
    q_pieces, q_rows = listed(w_query, wq_found, place_cx)
    o_pieces, o_rows = listed(w_out, wo_found, place_cx)
    n_q, n_o = len(q_pieces), len(o_pieces)
    pairs = H // 2
    kv_specs = [
        pl.BlockSpec((1, tok_rows, 2 * HD), lambda i, maps, n=n: (maps[n], 0, 0))
        for n in range(spans)
    ]
    pair_spec = pl.BlockSpec((tok_rows, 2 * HD), lambda i, maps: (0, i))
    token_spec = pl.BlockSpec((tok_rows, width), lambda i, maps: (0, 0))
    maps = jnp.concatenate([window, jnp.stack(q_rows + o_rows).astype(jnp.int32)])
    small = [gain_two, bias, cosine, sine]
    queries, attended, hidden, own_norm, factor = kernel_call(
        functools.partial(attend_kernel, n_q, n_o, spans),
        grid_spec=pltpu.PrefetchScalarGridSpec(
            num_scalar_prefetch=1,
            grid=(pairs,),
            in_specs=[token_spec, token_spec]
            + [whole_spec(a) for a in small]
            + kv_specs
            + [ANY] * (n_q + n_o),
            out_specs=[
                pair_spec,
                pair_spec,
                token_spec,
                token_spec,
                pl.BlockSpec((tok_rows, HD), lambda i, maps: (0, 0)),
            ],
            scratch_shapes=[
                pltpu.VMEM((width, H * HD), BF),
                pltpu.VMEM((H * HD, width), BF),
                pltpu.VMEM((spans * tok_rows, HD), BF),
                pltpu.VMEM((spans * tok_rows, HD), BF),
                pltpu.VMEM((tok_rows, width), F32),
                pltpu.SemaphoreType.DMA((n_q,)),
                pltpu.SemaphoreType.DMA((n_o,)),
            ],
        ),
        out_shape=[
            jax.ShapeDtypeStruct((tok_rows, H * HD), BF),
            jax.ShapeDtypeStruct((tok_rows, H * HD), BF),
            jax.ShapeDtypeStruct((tok_rows, width), F32),
            jax.ShapeDtypeStruct((tok_rows, width), BF),
            jax.ShapeDtypeStruct((tok_rows, HD), F32),
        ],
    )(maps, normed, tokens, *small, *([all_kv] * spans), *q_pieces, *o_pieces)
    mark(own_norm)

    norm_y = {r: shift(own_norm, "y", r) for r in others}
    norm_x = shift(own_norm, "x", 1)
    gu_z = {r: shift(tie(piece), "z", 1) for r, piece in gu_y.items()}
    norm_slices = {r: tie(part)[:half_tok] for r, part in norm_y.items()}
    norm_slice = tie(norm_x)[half_tok:]
    mark(norm_slice, *norm_slices.values())
    norm_a = {r: shift(part, "x", 1) for r, part in norm_slices.items()}
    norm_b = {r: shift(norm_slice, "y", r) for r in others}
    cot_parts = [cotangent, *[cot_y[r] for r in others], cot_x]
    norm_parts = [own_norm, *[norm_y[r] for r in others], norm_x]
    for r in others:
        cot_parts += [cot_corner_a[r], cot_corner_b[r]]
        norm_parts += [norm_a[r], norm_b[r]]
    cot_all = jnp.concatenate([tie(part) for part in cot_parts], axis=0)
    gu_found = {r: [gu_y[r], tie(gu_z[r])] for r in others}
    gu_found = {r: pair + [shift(tie(p), "c", 1) for p in pair] for r, pair in gu_found.items()}
    gu_moves = [
        (0, (deep, units), (0, part * FF + (y_at * 2 + x_at) * units), (y_at * deep, part * units))
        for part in (0, 1)
    ]
    gu_pieces, gu_rows = listed(w_gateup, gu_found, place_cz)
    for n in range(1, len(gu_pieces)):
        gu_moves.append((n, (quarter, 2 * units), (0, 0), (gu_rows[n], 0)))
    w_gu = lay_out((width, 2 * units), gu_pieces, gu_moves)
    many = group * tok_rows
    fits = units % 128 == 0
    picks = [
        [r * tok_rows for r in range(y_count)],
        [(y_count + r) * tok_rows for r in range(y_count)],
        [half_tok, y_count * tok_rows + half_tok],
    ]
    picks += [[r * tok_rows + half_tok, (y_count + r) * tok_rows + half_tok] for r in others]
    cut_shapes = [jax.ShapeDtypeStruct((len(pick_), half_tok, width), BF) for pick_ in picks]
    x_maps = jnp.stack([x_at]).astype(jnp.int32)

    def cut(result):
        return [
            jnp.stack([result[start : start + half_tok].astype(BF) for start in starts])
            for starts in picks
        ]

    if fits:
        wide = 384 if units % 384 == 0 else 128
        steps = units // wide
        turn = width // steps
        block = 512
        cut_specs = [
            pl.BlockSpec((len(starts), half_tok, block), lambda i, *_: (0, 0, i))
            for starts in picks
        ]
        n_tok = len(norm_parts)
        inner_act, inner_t, d_both, normed_t = kernel_call(
            functools.partial(forward_kernel, n_tok),
            grid_spec=pltpu.PrefetchScalarGridSpec(
                num_scalar_prefetch=1,
                grid=(steps,),
                in_specs=[ANY] * n_tok
                + [
                    pl.BlockSpec((many, width), lambda i, maps: (0, 0)),
                    pl.BlockSpec((width, wide), lambda i, maps: (0, i)),
                    pl.BlockSpec((width, wide), lambda i, maps: (0, steps + i)),
                    pl.BlockSpec((wide, width), lambda i, maps: (maps[0] * steps + i, 0)),
                ],
                out_specs=[
                    pl.BlockSpec((many, wide), lambda i, maps: (0, i)),
                    pl.BlockSpec((wide, many), lambda i, maps: (i, 0)),
                    pl.BlockSpec((2, many, wide), lambda i, maps: (0, 0, i)),
                    pl.BlockSpec((turn, many), lambda i, maps: (i, 0)),
                ],
                scratch_shapes=[
                    pltpu.VMEM((many, width), BF),
                    pltpu.SemaphoreType.DMA((n_tok,)),
                ],
            ),
            out_shape=[
                jax.ShapeDtypeStruct((many, units), BF),
                jax.ShapeDtypeStruct((units, many), BF),
                jax.ShapeDtypeStruct((2, many, units), BF),
                jax.ShapeDtypeStruct((width, many), BF),
            ],
        )(x_maps, *norm_parts, cot_all, w_gu, w_gu, w_down)

        def back_cut():
            return kernel_call(
                functools.partial(back_kernel, picks),
                grid=(width // block,),
                in_specs=[
                    whole_spec(d_both),
                    pl.BlockSpec((block, 2 * units), lambda i: (i, 0)),
                ],
                out_specs=cut_specs,
                out_shape=cut_shapes,
            )(tie(d_both), w_gu)

        def down_cut():
            return kernel_call(
                functools.partial(down_kernel, picks),
                grid_spec=pltpu.PrefetchScalarGridSpec(
                    num_scalar_prefetch=1,
                    grid=(width // block,),
                    in_specs=[
                        pl.BlockSpec((many, units), lambda i, maps: (0, 0)),
                        pl.BlockSpec((units, block), lambda i, maps: (maps[0], i)),
                    ],
                    out_specs=cut_specs,
                ),
                out_shape=cut_shapes,
            )(x_maps, tie(inner_act), w_down)

    else:
        normed2 = jnp.concatenate(norm_parts, axis=0)
        w_dn = lax.dynamic_slice_in_dim(w_down, x_at * units, units, 0)
        d_inner = dot_t(cot_all, w_dn)
        both_parts = dot(normed2, w_gu)
        active, back = jax.vjp(
            lambda values: jax.nn.gelu(values, approximate=True), both_parts[:, :units]
        )
        up_part = both_parts[:, units:]
        inner_act = (active * up_part).astype(BF)
        d_both = jnp.stack([back(d_inner * up_part)[0], d_inner * active]).astype(BF)
        inner_t, normed_t = inner_act.T, normed2.T

        def back_cut():
            both = tie(d_both)
            return cut(dot_t(both[0], w_gu[:, :units]) + dot_t(both[1], w_gu[:, units:]))

        def down_cut():
            return cut(dot(tie(inner_act), w_dn))

    mark(d_both)

    def back_a(cuts_in, result):
        keep, send = cuts_in[0], cuts_in[1]
        got = yield [(send, "x", 1)]

        def function(_, ins, outs):
            for n in range(y_count):
                outs[n][...] = (ins[0][n].astype(F32) + ins[1][n].astype(F32)).astype(BF)

        left = once(function, [((half_tok, width), BF)] * y_count, keep, got[0])
        got = yield [(left[r], "y", r) for r in others]
        result.append([left[0]] + got)

    def back_b(cuts_in, result):
        keep, send = cuts_in[2], cuts_in[3:]
        got = yield [(part, "y", r) for r, part in zip(others, send, strict=True)]

        def function(_, ins, outs):
            for n in range(2):
                outs[n][...] = sum(ref[n].astype(F32) for ref in ins).astype(BF)

        left = once(function, [((half_tok, width), BF)] * 2, keep, *got)
        got = yield [(left[1], "x", 1)]
        result.append([left[0]] + got)

    def sum_rows(ins, n_first):
        first = sum(ref[...].astype(F32) for ref in ins[:n_first])
        second = sum(ref[...].astype(F32) for ref in ins[n_first : n_first + 2])
        return jnp.concatenate([first, second], axis=0)

    def scatter_z(kept, sent):
        for level in range(z_levels):
            got = yield [(sent, "z", 1 << level)]
            sums = add_halves(kept, got[0])
            kept, sent = sums[0], sums[-1]
        return kept

    def spread(piece, finish, split=True):
        held = piece
        for level in reversed(range(z_levels)):
            got = yield [(held, "z", 1 << level)]
            held = stack_two(held, got[0])
        beside, across = yield [(held, "x", 1), (held, "c", 1)]
        corner = yield [(beside, "c", 1)]
        if split:
            mark(finish([tie(held), across], False))
            mark(finish([tie(beside), corner[0]], True))
        else:
            mark(finish([tie(held), beside, across, corner[0]], False))

    z_groups = [z_count // 2, z_count // 2]

    found = {}

    def finish_down(parts, beside):
        found["down"] = widen(
            parts,
            beside,
            z_places,
            (w_down.shape[0], width),
            lambda z, c, x, y: (x * z_count + z, c),
            found.get("down"),
        )
        return found["down"]

    def finish_up(r):
        def finish(parts, beside):
            found["up"] = widen(
                parts,
                beside,
                z_places,
                (deep, 2 * FF),
                lambda z, c, x, y: (z, (c * y_count + (y ^ r)) * 2 + x),
                found.get("up"),
            )
            return found["up"]

        return finish

    def finish_attn(name, columns):
        def finish(parts, beside):
            found[name] = widen(
                parts, beside, z_places, (deep, columns), lambda z, c, x, y: (z * 2 + x, c)
            )
            return found[name]

        return finish

    def ffn_chain(job, finish, r):
        left, left_block, left_rows, right = job
        theirs = grad(tie(left), left_block, left_rows, right, 1 - c_at, turned=True)
        got = yield [(theirs, "c", 1)]
        kept, sent = grad(
            left, left_block, left_rows, right, c_at, got[0], z_groups, z_order, turned=True
        )
        piece = yield from scatter_z(kept, sent)
        if r:
            got = yield [(piece, "y", r)]
            piece = got[0]
        yield from spread(piece, finish)

    y_order = jnp.arange(y_count, dtype=jnp.int32) ^ y_at
    xz_maps = jnp.concatenate([z_order * 2 + x_at, z_order * 2 + (1 - x_at)])

    def attn_chain(left, right, finish, column=None):
        cols = right.shape[1] // 2
        theirs = grad(tie(left), 0, width, right, 1 - c_at)
        if column is not None:
            lane = jnp.arange(HD) == 0
            own = jnp.where(c_at == 0, column[0], column[1]).reshape(width, 1)
            other = jnp.where(c_at == 0, column[1], column[0]).reshape(width, 1)
            theirs = jnp.concatenate([theirs, jnp.where(lane, other, 0).astype(BF)], axis=1)
        got = yield [(theirs, "c", 1)]
        got = got[0]
        parts = grad(left, 0, width, right, c_at, got[:, :cols], [1] * y_count, y_order)
        parts = [part[0] for part in parts]
        if column is not None:
            extra = add(jnp.where(lane, own, 0), got[:, cols:]).reshape(y_count, deep, HD)
            parts = [
                jnp.concatenate([part, pick(extra, y_at ^ r, 0)], axis=1)
                for r, part in enumerate(parts)
            ]
        got = yield [(part, "y", r) for r, part in zip(others, parts[1:], strict=True)]
        cols = parts[0].shape[1]
        rows = deep // (2 * z_count)
        if rows % 16:
            total = sum(v.astype(F32) for v in [parts[0]] + got).astype(BF)
            blocks = jnp.take(total.reshape(2 * z_count, rows, cols), xz_maps, axis=0)
            kept, sent = blocks[:z_count], blocks[z_count:]
        else:

            def function(maps, ins, outs):
                for n in range(2 * z_count):
                    block = pl.ds(pl.multiple_of(maps[n] * rows, 16), rows)
                    total = sum(ref[block, :].astype(F32) for ref in ins)
                    outs[n // z_count][n % z_count] = total.astype(BF)

            kept, sent = once(
                function, [((z_count, rows, cols), BF)] * 2, parts[0], *got, maps=xz_maps
            )
        got = yield [(sent, "x", 1)]
        sums = add_halves(kept, got[0])
        piece = yield from scatter_z(sums[0], sums[1])
        yield from spread(piece, finish, split=False)

    chains, pending = {}, {}

    def advance(names):
        names = [name for name in names.split() if chains.get(name) is not None]
        waited = [part for name in names for part in pending.get(name, [])]
        if waited:
            waited = list(lax.optimization_barrier(tuple(waited) + clock.marks))[: len(waited)]
            mark(*waited)
        for name in names:
            count = len(pending.get(name, []))
            got, waited = waited[:count], waited[count:]
            try:
                if name in pending:
                    got = list(lax.optimization_barrier(tuple(got) + clock.marks))[: len(got)]
                    sends = chains[name].send(got)
                else:
                    sends = [(tie(part), axis, mask) for part, axis, mask in next(chains[name])]
            except StopIteration:
                chains[name] = None
                continue
            mark(*[part for part, _, _ in sends])
            pending[name] = [shift(*send) for send in sends]

    d_result, out_result = [], []
    jobs = [
        ffn_chain((normed_t, y_at ^ r, deep, d_both), finish_up(r), r) for r in list(others) + [0]
    ]
    ups = [f"U{r}" for r in others]
    for name, chain in zip(ups + ["W"], jobs, strict=True):
        chains[name] = chain
    first_up = " ".join(ups)
    chains["D"] = ffn_chain((inner_t, 0, units, cot_all), finish_down, 0)

    def do_back():
        d_cut = back_cut()
        mark(*d_cut)
        chains["a"], chains["b"] = back_a(d_cut, d_result), back_b(d_cut, d_result)

    def do_down():
        out_cut = down_cut()
        mark(*out_cut)
        chains["e"], chains["f"] = back_a(out_cut, out_result), back_b(out_cut, out_result)

    def hidden_back(_, ins, outs):
        grads = sum_rows(ins, y_count)
        values, scale, upstream, gain = (ref[...] for ref in ins[y_count + 2 :])
        scale = scale[:, :1]
        back = upstream.astype(F32) + norm_back_rows(grads, values, scale, gain)
        outs[0][...] = back
        outs[1][...] = back.astype(BF)
        outs[2][...] = jnp.sum(grads * values * scale, axis=0, keepdims=True)

    def do_hidden():
        found["d_hidden"], found["d_attn"], found["d_gain_mlp"] = once(
            hidden_back,
            [((tok_rows, width), F32), ((tok_rows, width), BF), ((1, width), F32)],
            *[tie(part) for found_part in d_result for part in found_part],
            hidden,
            factor,
            cotangent,
            gain_two,
        )
        mark(found["d_attn"], found["d_gain_mlp"])
        chains["T"] = attn_chain(attended, found["d_attn"], finish_attn("out", width))

    maps = jnp.concatenate([window, entry_block, jnp.stack(o_rows).astype(jnp.int32)])
    entry_spec = pl.BlockSpec((ctx_count // 2, tok_rows, 2 * HD), lambda i, maps: (0, 0, 0))
    entry_shape = jax.ShapeDtypeStruct((ctx_count // 2, tok_rows, 2 * HD), BF)
    small = [bias, cosine, sine]
    def do_attention():
        found["d_raw"], found["d_kept"], found["d_sent"] = kernel_call(
            functools.partial(attend_back_kernel, n_o, spans, ctx_count),
            grid_spec=pltpu.PrefetchScalarGridSpec(
                num_scalar_prefetch=1,
                grid=(pairs,),
                in_specs=[token_spec, pair_spec]
                + [whole_spec(a) for a in small]
                + kv_specs
                + [ANY] * n_o,
                out_specs=[pair_spec, entry_spec, entry_spec],
                scratch_shapes=[
                    pltpu.VMEM((H * HD, width), BF),
                    pltpu.VMEM((spans * tok_rows, HD), BF),
                    pltpu.VMEM((spans * tok_rows, HD), BF),
                    pltpu.VMEM((HD, spans * tok_rows), F32),
                    pltpu.VMEM((HD, spans * tok_rows), F32),
                    pltpu.VMEM(((spans + 1) * tok_rows, 2 * HD), BF),
                    pltpu.SemaphoreType.DMA((n_o,)),
                ],
            ),
            out_shape=[jax.ShapeDtypeStruct((tok_rows, H * HD), BF), entry_shape, entry_shape],
        )(maps, tie(found["d_attn"]), queries, *small, *([all_kv] * spans), *o_pieces)
        mark(found["d_sent"])
        chains["Q"] = attn_chain(normed, found["d_raw"], finish_attn("query", width))
        chains["v"] = kv_back(kv_result)

    def kv_back(result):
        got = yield [(found["d_sent"], "c", 1)]

        def first(_, ins, outs):
            for n in range(2 * z_count):
                outs[n % 2][n // 2] = (ins[0][n].astype(F32) + ins[1][n].astype(F32)).astype(BF)

        shape = ((z_count, tok_rows, 2 * HD), BF)
        kept, sent = once(first, [shape, shape], found["d_kept"], got[0])
        got = yield [(sent, "x", 1)]

        def second(_, ins, outs):
            for n in range(z_count):
                outs[n][...] = (ins[0][n].astype(F32) + ins[1][n].astype(F32)).astype(BF)

        left = once(second, [((tok_rows, 2 * HD), BF)] * z_count, kept, got[0])
        got = yield [(left[d], "z", d) for d in range(1, z_count)]
        result += [left[0]] + got

    kv_result = []
    def tokens_kernel(maps, *refs):
        n_kv = y_count
        d_raw, cosine_ref, sine_ref, tokens_ref, gain, back_hidden = refs[:6]
        parts = refs[6 : 6 + z_count]
        kv_pieces = refs[6 + z_count : 6 + z_count + n_kv]
        pieces = refs[6 + z_count + n_kv : 6 + z_count + n_kv + n_q]
        outs = refs[6 + z_count + n_kv + n_q :]
        d_kv, back, d_gain, whole_q, whole_kv, q_sem, kv_sem = outs
        copies = load_rows(whole_q, pieces, [maps[n] for n in range(n_q)], q_sem)
        copies += load_rows(whole_kv, kv_pieces, [maps[n_q + n] for n in range(n_kv)], kv_sem)
        total = sum(ref[...].astype(F32) for ref in parts)
        d_kv[:, :HD] = rotate(total[:, :HD], cosine_ref[...], -sine_ref[...]).astype(BF)
        d_kv[:, HD:] = total[:, HD:].astype(BF)
        inputs = tokens_ref[...].astype(F32)
        scale = rms_factor(inputs)
        for copy in copies:
            copy.wait()
        grads = dot_t(d_raw[...], whole_q[...]) + dot_t(d_kv[...], whole_kv[...])
        back[...] = back_hidden[...] + norm_back_rows(grads, inputs, scale, gain[...])
        d_gain[...] = jnp.sum(grads * inputs * scale, axis=0, keepdims=True)

    q_maps = jnp.concatenate([jnp.stack(q_rows).astype(jnp.int32), kv_rows])
    def do_tokens():
        d_kv_raw, found["tokens"], d_gain = kernel_call(
            tokens_kernel,
            in_specs=[pl.BlockSpec(memory_space=pltpu.SMEM)]
            + [in_vmem] * (6 + z_count)
            + [ANY] * (y_count + n_q),
            out_specs=[in_vmem] * 3,
            out_shape=[
                jax.ShapeDtypeStruct((tok_rows, 2 * HD), BF),
                jax.ShapeDtypeStruct((tok_rows, width), F32),
                jax.ShapeDtypeStruct((1, width), F32),
            ],
            scratch_shapes=[
                pltpu.VMEM((width, H * HD), BF),
                pltpu.VMEM((width, 2 * HD), BF),
                pltpu.SemaphoreType.DMA((n_q,)),
                pltpu.SemaphoreType.DMA((y_count,)),
            ],
        )(
            q_maps,
            found["d_raw"],
            cosine,
            sine,
            tokens,
            gain_one,
            found["d_hidden"],
            *[tie(part) for part in kv_result],
            *kv_weights,
            *q_pieces,
        )
        mark(d_kv_raw, d_gain, found["tokens"])
        chains["K"] = attn_chain(
            normed, d_kv_raw, finish_attn("keyval", 4 * HD), (d_gain, found["d_gain_mlp"])
        )

    works = {
        "back": do_back,
        "down": do_down,
        "hid": do_hidden,
        "att": do_attention,
        "tok": do_tokens,
    }
    for entry in PLAN:
        if entry in works:
            works[entry]()
        else:
            advance(" ".join(first_up if letter == "O" else letter for letter in entry))
    while any(chain is not None for chain in chains.values()):
        advance(" ".join(chains))

    def finish_output(_, ins, outs):
        outs[0][...] = (ins[-1][...] + sum_rows(ins, y_count)).astype(BF)

    block_output = once(
        finish_output, [((tok_rows, width), BF)], *[part for found_part in out_result for part in found_part], hidden
    )[0]
    last = found["keyval"]
    grad_keyval = jnp.concatenate([last[:, :HD], last[:, 2 * HD : 3 * HD]], axis=1)
    return (
        block_output,
        found["tokens"],
        last[:, HD],
        found["query"],
        grad_keyval,
        found["out"],
        last[:, 3 * HD],
        found["up"],
        found["down"],
    )


def solution(mesh):
    ctx_count, y_count = mesh.shape["ctx"], mesh.shape["fsdp"]
    fine = Mesh(mesh.devices.reshape(ctx_count // 4, 2, 2, y_count), ("z", "x", "c", "y"))
    rows, shard = P(("z", "x", "c", "y"), None), P("y", None)
    in_specs = (rows, rows, shard, shard, P("y"), shard, shard, shard, P("y"), shard, shard)
    out_specs = (rows, rows, P("y"), shard, shard, shard, P("y"), shard, shard)
    return jax.shard_map(body, mesh=fine, in_specs=in_specs, out_specs=out_specs, check_vma=False)
```

time: 764 us -> 607 us (0.79)
  waiting for transfers between devices: 334 us -> 215 us
  other arithmetic: 73 us -> 10.2 us
  Pallas kernels: 199 us -> 243 us
  starting transfers between devices: 95.9 us -> 85.4 us
    ppermute x94 -> x95, waiting for transfers between devices: 334 us -> 215 us  [shift(): lax.ppermute(array, axis, [(i, i ^ mask) for i in range(lax.axis_size(axi...]
    pallas_call x22 -> x68, Pallas kernels: 165 us -> 209 us  [the longest x9 58.8 us: widen(): kernel_call(functools.partial(widen_kernel, count), grid_spec=pltpu.Prefe...]
    convert_element_type x20 -> x1, other arithmetic: 21.2 us -> 1.32 us  [add(): return (a.astype(F32) + b.astype(F32)).astype(BF)]
    concatenate x19 -> x4, other arithmetic: 15.9 us -> 0.37 us  [the longest x2 0.16 us: widen(): maps = jnp.concatenate([jnp.stack(flips).astype(jnp.int32), z_places])]
    ppermute x94 -> x95, starting transfers between devices: 95.9 us -> 85.4 us  [shift(): lax.ppermute(array, axis, [(i, i ^ mask) for i in range(lax.axis_size(axi...]
    unnamed x233 -> x194, local copies, waits for them, and re-layouts: 17 us -> 27.2 us
    convert_element_type x9 -> x1, other arithmetic: 9.35 us -> 0.01 us  [body(): gains = jnp.swapaxes(gains, 0, 1).reshape(2, width).astype(F32)]
    gather x6 -> x0, local copies, waits for them, and re-layouts: 7.81 us -> none  [the longest x3 4.48 us: attn_chain(): sent = jnp.take(pick(blocks, 1 - x_at, 1), z_order, axis=0)]
  transfers between devices with their start and end apart: 94 -> 95, of which waited for: 37 -> 36; matrix products, arithmetic and copies ran while one was open for 13% -> 3% of each run, Pallas kernels for 20% -> 35%
where the time goes in v3:
time: 607 us; the launch traced here: 595 us
  Pallas kernels  243 us (40%)
  waiting for transfers between devices  215 us (35%)
  starting transfers between devices  85.4 us (14%)
  local copies, waits for them, and re-layouts  38.2 us (6%)
  other arithmetic  10.2 us (2%)
    ppermute x95, waiting for transfers between devices, shift(): lax.ppermute(array, axis, [(i, i ^ mask) for i in range(lax.axis_size(axi...  215 us
    ppermute x95, starting transfers between devices, shift(): lax.ppermute(array, axis, [(i, i ^ mask) for i in range(lax.axis_size(axi...  85.4 us
    pallas_call x9, Pallas kernels, widen(): kernel_call(functools.partial(widen_kernel, count), grid_spec=pltpu.Prefe...  58.8 us
    pallas_call x12, Pallas kernels, grad(): kernel_call(functools.partial(grad_kernel, turned, groups, block_rows, ad...  50.5 us
    pallas_call x41, Pallas kernels, once(): kernel_call(functools.partial(once_kernel, function, len(operands)), in_s...  27.8 us
    unnamed x194, local copies, waits for them, and re-layouts  27.2 us
    pallas_call x1, Pallas kernels, body(): kernel_call(functools.partial(attend_kernel, n_q, n_o, spans), grid_spec=...  24 us
    pallas_call x1, Pallas kernels, do_attention(): kernel_call(functools.partial(attend_back_kernel, n_o, spans, ctx_count),...  22.4 us
  transfers between devices with their start and end apart: 95, of which 36 were waited for; matrix products, arithmetic and copies ran while one was open for 3% of the time, Pallas kernels for 35%

profile of v3, /device:TPU:0, one launch (start us, length us, event | category | flops | bytes accessed | tf_op | source)
XLA Modules:
  0.0 595.2 jit_solution(1206360787877456416)
XLA Ops:
  42.6 11.9 %collective-permute-done.7.refs_2_ = bf16[2,256,256]{2,1,0:T(8,128)(2,1)S(1)} collective-permute-done((bf16[2,256,256]{2,1,0:T(8,128)(2,1)S(1)}, bf16[2,256,256]{2,1,0:T(8,128)(2,1)S(1)}, u32[]{:S(2)}, u32[]{:S(2)}) %collective-permute-start.7) | collective-permute-done | bytes 262176 | tf_op jit(solution)/shard_map/ppermute | solution.py:65
  60.2 11.3 %collective-permute-done.11.refs_18_.refs_12_ = bf16[192,1536]{1,0:T(8,128)(2,1)} collective-permute-done((bf16[192,1536]{1,0:T(8,128)(2,1)}, bf16[192,1536]{1,0:T(8,128)(2,1)}, u32[]{:S(2)}, u32[]{:S(2)}) %collective-permute-start.11) | collective-permute-done | bytes 589856 | tf_op jit(solution)/shard_map/ppermute | solution.py:65
  80.8 24.0 %shard_map.182 = (bf16[256,1536]{1,0:T(8,128)(2,1)S(1)}, bf16[256,1536]{1,0:T(8,128)(2,1)}, f32[256,1536]{1,0:T(8,128)}, bf16[256,1536]{1,0:T(8,128)(2,1)}, f32[256,128]{1,0:T(8,128)S(1)}) custom-call(s32[15]{0:T(128)S(1)} %concatenate.67.maps, bf16[256,1536]{1,0:T(8,128)(2,1)} %copy-done.3, bf16[256,1536]{1,0:T(8,128)(2,1)} %refs_3_.1, ...), custom_call_target="tpu_custom_call" | custom-call | flops 1000 | bytes 1000 | tf_op jit(solution)/shard_map/pallas_call | solution.py:764
  111.8 14.5 %collective-permute-done.17.refs_2_ = bf16[256,1536]{1,0:T(8,128)(2,1)S(1)} collective-permute-done((bf16[256,1536]{1,0:T(8,128)(2,1)}, bf16[256,1536]{1,0:T(8,128)(2,1)S(1)}, u32[]{:S(2)}, u32[]{:S(2)}) %collective-permute-start.17) | collective-permute-done | bytes 786464 | tf_op jit(solution)/shard_map/ppermute | solution.py:65
  129.5 6.8 %collective-permute-done.22 = bf16[128,1536]{1,0:T(8,128)(2,1)S(1)} collective-permute-done((bf16[128,1536]{1,0:T(8,128)(2,1)}, bf16[128,1536]{1,0:T(8,128)(2,1)S(1)}, u32[]{:S(2)}, u32[]{:S(2)}) %collective-permute-start.22) | collective-permute-done | bytes 393248 | tf_op jit(solution)/shard_map/ppermute | solution.py:65
  140.4 6.9 %shard_map.184.refs_6_.refs_7_.w_gu = bf16[1536,2304]{1,0:T(8,128)(2,1)} custom-call(s32[6,4]{1,0:T(8,128)S(1)} %stack.235.spots, bf16[768,9216]{1,0:T(8,128)(2,1)} %refs_0_.4, bf16[192,2304]{1,0:T(8,128)(2,1)} %collective-permute-done.23.refs_1_, bf16[192,2304]{1,0:T(8,128)(2,1)} %collective-permute-done.24.refs_2_, ...), custom_call_target="tpu_custom_call" | custom-call | flops 1000 | bytes 1000 | tf_op jit(solution)/shard_map/pallas_call | solution.py:147
  147.3 21.9 %shard_map.185 = (bf16[1024,1152]{1,0:T(8,128)(2,1)S(1)}, bf16[1152,1024]{1,0:T(8,128)(2,1)}, bf16[2,1024,1152]{2,1,0:T(8,128)(2,1)}, bf16[1536,1024]{1,0:T(8,128)(2,1)}) custom-call(s32[1]{0:T(128)} %bitcast.maps, bf16[256,1536]{1,0:T(8,128)(2,1)S(1)} %copy-done.39, bf16[256,1536]{1,0:T(8,128)(2,1)S(1)} %collective-permute-done.16.refs_1_, ...), custom_call_target="tpu_custom_call" | custom-call | flops 1000 | bytes 1000 | tf_op jit(solution)/shard_map/pallas_call | solution.py:851
  176.5 5.9 shard_map.187
  188.7 12.7 %shard_map.189 = (bf16[2,128,1536]{2,1,0:T(8,128)(2,1)S(1)}, bf16[2,128,1536]{2,1,0:T(8,128)(2,1)}, bf16[2,128,1536]{2,1,0:T(8,128)(2,1)S(1)}, bf16[2,128,1536]{2,1,0:T(8,128)(2,1)}) custom-call(bf16[2,1024,1152]{2,1,0:T(8,128)(2,1)} %get-tuple-element.338.right.d_both, bf16[1536,2304]{1,0:T(8,128)(2,1)} %shard_map.184.refs_6_.refs_7_.w_gu), custom_call_target="tpu_custom_call" | custom-call | flops 1000 | bytes 1000 | tf_op jit(solution)/shard_map/pallas_call | solution.py:883
  203.0 6.4 %shard_map.190 = (bf16[2,192,1152]{2,1,0:T(8,128)(2,1)S(1)}, bf16[2,192,1152]{2,1,0:T(8,128)(2,1)}) custom-call(s32[6]{0:T(128)S(1)} %get-tuple-element.569.maps, bf16[1536,1024]{1,0:T(8,128)(2,1)} %get-tuple-element.360.left, bf16[2,1024,1152]{2,1,0:T(8,128)(2,1)} %get-tuple-element.338.right.d_both, bf16[768,1152]{1,0:T(8,128)(2,1)S(1)} %collective-permute-done.29.refs_0_), custom_call_target="tpu_custom_call" | custom-call | flops 1000 | bytes 1000 | tf_op jit(solution)/shard_map/pallas_call | solution.py:507
  213.3 6.7 %shard_map.192 = (bf16[2,128,1536]{2,1,0:T(8,128)(2,1)S(1)}, bf16[2,128,1536]{2,1,0:T(8,128)(2,1)}, bf16[2,128,1536]{2,1,0:T(8,128)(2,1)S(1)}, bf16[2,128,1536]{2,1,0:T(8,128)(2,1)S(1)}) custom-call(s32[1]{0:T(128)} %bitcast.maps, bf16[1024,1152]{1,0:T(8,128)(2,1)S(1)} %get-tuple-element.350.inner, bf16[2304,1536]{1,0:T(8,128)(2,1)} %w_down.1), custom_call_target="tpu_custom_call" | custom-call | flops 1000 | bytes 1000 | tf_op jit(solution)/shard_map/pallas_call | solution.py:895
  231.7 8.3 %collective-permute-done.33.refs_1_ = bf16[2,192,1152]{2,1,0:T(8,128)(2,1)S(1)} collective-permute-done((bf16[2,192,1152]{2,1,0:T(8,128)(2,1)}, bf16[2,192,1152]{2,1,0:T(8,128)(2,1)S(1)}, u32[]{:S(2)}, u32[]{:S(2)}) %collective-permute-start.33) | collective-permute-done | bytes 884768 | tf_op jit(solution)/shard_map/ppermute | solution.py:65
  249.9 22.4 %shard_map.200 = (bf16[256,1536]{1,0:T(8,128)(2,1)S(1)}, bf16[8,256,256]{2,1,0:T(8,128)(2,1)S(1)}, bf16[8,256,256]{2,1,0:T(8,128)(2,1)}) custom-call(s32[26]{0:T(128)S(1)} %concatenate.75.maps, bf16[256,1536]{1,0:T(8,128)(2,1)S(1)} %get-tuple-element.384.right.refs_0_, bf16[256,1536]{1,0:T(8,128)(2,1)S(1)} %copy-done.45, f32[256,1280]{1,0:T(8,128)} %fusion.2.refs_3_.refs_2_, ...), custom_call_target="tpu_custom_call" | custom-call | flops 1000 | bytes 1000 | tf_op jit(solution)/shard_map/pallas_call | solution.py:1145
  284.4 6.7 %shard_map.203 = (bf16[2,192,1152]{2,1,0:T(8,128)(2,1)S(1)}, bf16[2,192,1152]{2,1,0:T(8,128)(2,1)}) custom-call(s32[6]{0:T(128)S(1)} %copy-done.77, bf16[1536,1024]{1,0:T(8,128)(2,1)} %get-tuple-element.360.left, bf16[2,1024,1152]{2,1,0:T(8,128)(2,1)} %get-tuple-element.338.right.d_both, bf16[768,1152]{1,0:T(8,128)(2,1)} %collective-permute-done.32.refs_0_), custom_call_target="tpu_custom_call" | custom-call | flops 1000 | bytes 1000 | tf_op jit(solution)/shard_map/pallas_call | solution.py:507
  312.5 18.0 %collective-permute-done.39.refs_1_ = bf16[2,192,1152]{2,1,0:T(8,128)(2,1)} collective-permute-done((bf16[2,192,1152]{2,1,0:T(8,128)(2,1)}, bf16[2,192,1152]{2,1,0:T(8,128)(2,1)}, u32[]{:S(2)}, u32[]{:S(2)}) %collective-permute-start.39) | collective-permute-done | bytes 884768 | tf_op jit(solution)/shard_map/ppermute | solution.py:65
  336.3 15.7 %collective-permute-done.48.refs_1_ = bf16[2,288,768]{2,1,0:T(8,128)(2,1)S(1)} collective-permute-done((bf16[2,288,768]{2,1,0:T(8,128)(2,1)S(1)}, bf16[2,288,768]{2,1,0:T(8,128)(2,1)S(1)}, u32[]{:S(2)}, u32[]{:S(2)}) %collective-permute-start.48) | collective-permute-done | bytes 884768 | tf_op jit(solution)/shard_map/ppermute | solution.py:65
  363.8 11.0 %collective-permute-done.52.refs_7_ = bf16[256,256]{1,0:T(8,128)(2,1)} collective-permute-done((bf16[256,256]{1,0:T(8,128)(2,1)}, bf16[256,256]{1,0:T(8,128)(2,1)}, u32[]{:S(2)}, u32[]{:S(2)}) %collective-permute-start.52) | collective-permute-done | bytes 131104 | tf_op jit(solution)/shard_map/ppermute | solution.py:65
  380.5 11.6 %collective-permute-start.55 = (bf16[1,96,768]{2,1,0:T(8,128)(2,1)S(1)}, bf16[1,96,768]{2,1,0:T(8,128)(2,1)S(1)}, u32[]{:S(2)}, u32[]{:S(2)}) collective-permute-start(bf16[1,96,768]{2,1,0:T(8,128)(2,1)S(1)} %get-tuple-element.435), channel_id=1, source_target_pairs={{0,16},{8,24},{16,0},{24,8},{1,17},{9,25},{17,1},{25,9},{2,18},{10... | collective-permute-start | bytes 442376 | tf_op jit(solution)/shard_map/ppermute | solution.py:65
  395.0 6.7 %shard_map.217 = (bf16[256,256]{1,0:T(8,128)(2,1)S(1)}, f32[256,1536]{1,0:T(8,128)}, f32[1,1536]{1,0:T(1,128)S(1)}) custom-call(s32[7]{0:T(128)S(1)} %concatenate.77.maps, bf16[256,1536]{1,0:T(8,128)(2,1)S(1)} %copy-done.9, f32[256,128]{1,0:T(8,128)S(1)} %copy-done.14, f32[256,128]{1,0:T(8,128)S(1)} %copy-done.16, bf16[256,1536]{1,0:T(8,128)(2,1)S(1)} %copy-done.7, ...), custom_call_target="tpu_custom_call" | custom-call | flops 1000 | bytes 1000 | tf_op jit(solution)/shard_map/pallas_call | solution.py:1214
  414.4 14.5 %collective-permute-done.58.refs_1_ = bf16[1,96,768]{2,1,0:T(8,128)(2,1)S(1)} collective-permute-done((bf16[1,96,768]{2,1,0:T(8,128)(2,1)S(1)}, bf16[1,96,768]{2,1,0:T(8,128)(2,1)S(1)}, u32[]{:S(2)}, u32[]{:S(2)}) %collective-permute-start.58) | collective-permute-done | bytes 147488 | tf_op jit(solution)/shard_map/ppermute | solution.py:65
  434.4 11.3 %collective-permute-done.61.refs_0_ = bf16[4,288,768]{2,1,0:T(8,128)(2,1)} collective-permute-done((bf16[4,288,768]{2,1,0:T(8,128)(2,1)S(1)}, bf16[4,288,768]{2,1,0:T(8,128)(2,1)}, u32[]{:S(2)}, u32[]{:S(2)}) %collective-permute-start.61) | collective-permute-done | bytes 1769504 | tf_op jit(solution)/shard_map/ppermute | solution.py:65
  448.6 9.6 %collective-permute-done.67.refs_1_ = bf16[4,96,768]{2,1,0:T(8,128)(2,1)S(1)} collective-permute-done((bf16[4,96,768]{2,1,0:T(8,128)(2,1)S(1)}, bf16[4,96,768]{2,1,0:T(8,128)(2,1)S(1)}, u32[]{:S(2)}, u32[]{:S(2)}) %collective-permute-start.67) | collective-permute-done | bytes 589856 | tf_op jit(solution)/shard_map/ppermute | solution.py:65
  466.6 8.3 %collective-permute-done.68.refs_1_ = bf16[2,96,256]{2,1,0:T(8,128)(2,1)S(1)} collective-permute-done((bf16[2,96,256]{2,1,0:T(8,128)(2,1)S(1)}, bf16[2,96,256]{2,1,0:T(8,128)(2,1)S(1)}, u32[]{:S(2)}, u32[]{:S(2)}) %collective-permute-start.68) | collective-permute-done | bytes 98336 | tf_op jit(solution)/shard_map/ppermute | solution.py:65
  477.3 15.7 %collective-permute-done.76.refs_1_ = bf16[1,96,768]{2,1,0:T(8,128)(2,1)S(1)} collective-permute-done((bf16[1,96,768]{2,1,0:T(8,128)(2,1)S(1)}, bf16[1,96,768]{2,1,0:T(8,128)(2,1)S(1)}, u32[]{:S(2)}, u32[]{:S(2)}) %collective-permute-start.76) | collective-permute-done | bytes 147488 | tf_op jit(solution)/shard_map/ppermute | solution.py:65
  503.8 9.3 %collective-permute-done.72.refs_0_ = bf16[4,192,1152]{2,1,0:T(8,128)(2,1)} collective-permute-done((bf16[4,192,1152]{2,1,0:T(8,128)(2,1)S(1)}, bf16[4,192,1152]{2,1,0:T(8,128)(2,1)}, u32[]{:S(2)}, u32[]{:S(2)}) %collective-permute-start.72) | collective-permute-done | bytes 1769504 | tf_op jit(solution)/shard_map/ppermute | solution.py:65
  518.9 6.7 %shard_map.235 = f32[768,1536]{1,0:T(8,128)} custom-call(s32[7]{0:T(128)S(1)} %add_add_fusion.3.maps, bf16[4,96,768]{2,1,0:T(8,128)(2,1)S(1)} %shard_map.225.refs_0_, bf16[4,96,768]{2,1,0:T(8,128)(2,1)S(1)} %collective-permute-done.74.refs_1_, bf16[4,96,768]{2,1,0:T(8,128)(2,1)S(1)} %collective-permute-done.75.refs_2_, ...), custom_call_target="tpu_custom_call" | custom-call | flops 1000 | bytes 1000 | tf_op jit(solution)/shard_map/pallas_call | solution.py:199
  530.8 7.1 %shard_map.238.refs_2_ = f32[2304,1536]{1,0:T(8,128)} custom-call(s32[7]{0:T(128)S(1)} %get-tuple-element.566.maps, bf16[4,288,768]{2,1,0:T(8,128)(2,1)S(1)} %shard_map.212.refs_0_, bf16[4,288,768]{2,1,0:T(8,128)(2,1)} %collective-permute-done.62.refs_1_), custom_call_target="tpu_custom_call" | custom-call | flops 1000 | bytes 1000 | tf_op jit(solution)/shard_map/pallas_call | solution.py:199
  537.9 8.9 %shard_map.239 = f32[2304,1536]{1,0:T(8,128)} custom-call(s32[7]{0:T(128)S(1)} %get-tuple-element.567.maps, bf16[4,288,768]{2,1,0:T(8,128)(2,1)} %collective-permute-done.61.refs_0_, bf16[4,288,768]{2,1,0:T(8,128)(2,1)} %collective-permute-done.81.refs_1_, f32[2304,1536]{1,0:T(8,128)} %shard_map.238.refs_2_), custom_call_target="tpu_custom_call", output_to_operand_aliasing={{}: (3, {})} | custom-call | flops 1000 | bytes 1000 | tf_op jit(solution)/shard_map/pallas_call | solution.py:199
  557.2 8.6 %shard_map.243.refs_2_ = f32[768,9216]{1,0:T(8,128)} custom-call(s32[7]{0:T(128)S(1)} %get-tuple-element.567.maps, bf16[4,192,1152]{2,1,0:T(8,128)(2,1)} %collective-permute-done.72.refs_0_, bf16[4,192,1152]{2,1,0:T(8,128)(2,1)} %collective-permute-done.92.refs_1_, f32[768,9216]{1,0:T(8,128)} %shard_map.242.refs_2_), custom_call_target="tpu_custom_call", output_to_operand_aliasing={{}: (3, {})} | custom-call | flops 1000 | bytes 1000 | tf_op jit(solution)/shard_map/pallas_call | solution.py:199
  568.5 7.1 %shard_map.244.refs_2_ = f32[768,9216]{1,0:T(8,128)} custom-call(s32[7]{0:T(128)S(1)} %get-tuple-element.566.maps, bf16[4,192,1152]{2,1,0:T(8,128)(2,1)S(1)} %shard_map.232.refs_0_, bf16[4,192,1152]{2,1,0:T(8,128)(2,1)} %collective-permute-done.87.refs_1_, f32[768,9216]{1,0:T(8,128)} %shard_map.243.refs_2_), custom_call_target="tpu_custom_call", output_to_operand_aliasing={{}: (3, {})} | custom-call | flops 1000 | bytes 1000 | tf_op jit(solution)/shard_map/pallas_call | solution.py:199
  575.6 7.1 %shard_map.245 = f32[768,9216]{1,0:T(8,128)} custom-call(s32[7]{0:T(128)S(1)} %get-tuple-element.567.maps, bf16[4,192,1152]{2,1,0:T(8,128)(2,1)} %collective-permute-done.86.refs_0_, bf16[4,192,1152]{2,1,0:T(8,128)(2,1)S(1)} %collective-permute-done.89.refs_1_, f32[768,9216]{1,0:T(8,128)} %shard_map.244.refs_2_), custom_call_target="tpu_custom_call", output_to_operand_aliasing={{}: (3, {})} | custom-call | flops 1000 | bytes 1000 | tf_op jit(solution)/shard_map/pallas_call | solution.py:199
  583.4 6.7 %shard_map.247 = f32[768,1536]{1,0:T(8,128)} custom-call(s32[7]{0:T(128)S(1)} %add_add_fusion.3.maps, bf16[4,96,768]{2,1,0:T(8,128)(2,1)S(1)} %shard_map.241.refs_0_, bf16[4,96,768]{2,1,0:T(8,128)(2,1)S(1)} %collective-permute-done.90.refs_1_, bf16[4,96,768]{2,1,0:T(8,128)(2,1)S(1)} %collective-permute-done.91.refs_2_, ...), custom_call_target="tpu_custom_call" | custom-call | flops 1000 | bytes 1000 | tf_op jit(solution)/shard_map/pallas_call | solution.py:199
  (491 shorter events, 241.0 us)
Async XLA Ops:
  9.5 31.8 %collective-permute-start.6 = (bf16[192,1536]{1,0:T(8,128)(2,1)}, bf16[192,1536]{1,0:T(8,128)(2,1)}, u32[]{:S(2)}, u32[]{:S(2)}) collective-permute-start(bf16[192,1536]{1,0:T(8,128)(2,1)} %get-tuple-element.297), channel_id=1, source_target_pairs={{0,1},{1,0},{2,3},{3,2},{4,5},{5,4},{6,7},{7,6},{8,9},{9,8},{10,11... | collective-permute-start | bytes 1769480 | tf_op jit(solution)/shard_map/ppermute | solution.py:65
  59.1 49.1 %collective-permute-start.23 = (bf16[192,2304]{1,0:T(8,128)(2,1)}, bf16[192,2304]{1,0:T(8,128)(2,1)}, u32[]{:S(2)}, u32[]{:S(2)}) collective-permute-start(bf16[192,2304]{1,0:T(8,128)(2,1)} %shard_map.183), channel_id=1, source_target_pairs={{0,1},{1,0},{2,3},{3,2},{4,5},{5,4},{6,7},{7,6},{8,9},{9,8},{10,11... | collective-permute-start | bytes 2654216 | tf_op jit(solution)/shard_map/ppermute | solution.py:65
  75.7 32.5 %collective-permute-start.20 = (bf16[256,1536]{1,0:T(8,128)(2,1)S(1)}, bf16[256,1536]{1,0:T(8,128)(2,1)}, u32[]{:S(2)}, u32[]{:S(2)}) collective-permute-start(bf16[256,1536]{1,0:T(8,128)(2,1)S(1)} %copy-done.17), channel_id=1, source_target_pairs={{0,4},{4,0},{1,5},{5,1},{2,6},{6,2},{3,7},{7,3},{8,12},{12,8},{9,1... | collective-permute-start | bytes 2359304 | tf_op jit(solution)/shard_map/ppermute | solution.py:65
  108.2 28.1 %collective-permute-start.24 = (bf16[192,2304]{1,0:T(8,128)(2,1)}, bf16[192,2304]{1,0:T(8,128)(2,1)}, u32[]{:S(2)}, u32[]{:S(2)}) collective-permute-start(bf16[192,2304]{1,0:T(8,128)(2,1)} %collective-permute-done.23.refs_1_), channel_id=1, source_target_pairs={{0,8},{8,0},{16,24},{24,16},{1,9},{9,1},{17,25},{25,17},{2,10},{10... | collective-permute-start | bytes 2654216 | tf_op jit(solution)/shard_map/ppermute | solution.py:65
  110.0 26.3 %collective-permute-start.22 = (bf16[128,1536]{1,0:T(8,128)(2,1)}, bf16[128,1536]{1,0:T(8,128)(2,1)S(1)}, u32[]{:S(2)}, u32[]{:S(2)}) collective-permute-start(bf16[128,1536]{1,0:T(8,128)(2,1)} %slice.86), channel_id=1, source_target_pairs={{0,1},{1,0},{2,3},{3,2},{4,5},{5,4},{6,7},{7,6},{8,9},{9,8},{10,11... | collective-permute-start | bytes 1179656 | tf_op jit(solution)/shard_map/ppermute | solution.py:65
  111.0 25.3 %collective-permute-start.21 = (bf16[128,1536]{1,0:T(8,128)(2,1)}, bf16[128,1536]{1,0:T(8,128)(2,1)}, u32[]{:S(2)}, u32[]{:S(2)}) collective-permute-start(bf16[128,1536]{1,0:T(8,128)(2,1)} %slice.83), channel_id=1, source_target_pairs={{0,4},{4,0},{1,5},{5,1},{2,6},{6,2},{3,7},{7,3},{8,12},{12,8},{9,1... | collective-permute-start | bytes 1179656 | tf_op jit(solution)/shard_map/ppermute | solution.py:65
  209.3 30.7 %collective-permute-start.33 = (bf16[2,192,1152]{2,1,0:T(8,128)(2,1)}, bf16[2,192,1152]{2,1,0:T(8,128)(2,1)S(1)}, u32[]{:S(2)}, u32[]{:S(2)}) collective-permute-start(bf16[2,192,1152]{2,1,0:T(8,128)(2,1)} %get-tuple-element.347), channel_id=1, source_target_pairs={{0,8},{8,0},{16,24},{24,16},{1,9},{9,1},{17,25},{25,17},{2,10},{10... | collective-permute-start | bytes 2654216 | tf_op jit(solution)/shard_map/ppermute | solution.py:65
  212.2 33.3 %collective-permute-start.37 = (bf16[1,288,768]{2,1,0:T(8,128)(2,1)}, bf16[1,288,768]{2,1,0:T(8,128)(2,1)S(1)}, u32[]{:S(2)}, u32[]{:S(2)}) collective-permute-start(bf16[1,288,768]{2,1,0:T(8,128)(2,1)} %get-tuple-element.349), channel_id=1, source_target_pairs={{0,16},{8,24},{16,0},{24,8},{1,17},{9,25},{17,1},{25,9},{2,18},{10... | collective-permute-start | bytes 1327112 | tf_op jit(solution)/shard_map/ppermute | solution.py:65
  248.5 28.4 %collective-permute-start.32 = (bf16[768,1152]{1,0:T(8,128)(2,1)}, bf16[768,1152]{1,0:T(8,128)(2,1)}, u32[]{:S(2)}, u32[]{:S(2)}) collective-permute-start(bf16[768,1152]{1,0:T(8,128)(2,1)} %shard_map.195), channel_id=1, source_target_pairs={{0,2},{2,0},{1,3},{3,1},{4,6},{6,4},{5,7},{7,5},{8,10},{10,8},{9,1... | collective-permute-start | bytes 5308424 | tf_op jit(solution)/shard_map/ppermute | solution.py:65
  249.0 27.9 %collective-permute-start.34 = (bf16[1,192,1152]{2,1,0:T(8,128)(2,1)}, bf16[1,192,1152]{2,1,0:T(8,128)(2,1)}, u32[]{:S(2)}, u32[]{:S(2)}) collective-permute-start(bf16[1,192,1152]{2,1,0:T(8,128)(2,1)} %get-tuple-element.364), channel_id=1, source_target_pairs={{0,16},{8,24},{16,0},{24,8},{1,17},{9,25},{17,1},{25,9},{2,18},{10... | collective-permute-start | bytes 1327112 | tf_op jit(solution)/shard_map/ppermute | solution.py:65
  279.6 29.1 %collective-permute-start.41 = (bf16[768,768]{1,0:T(8,128)(2,1)}, bf16[768,768]{1,0:T(8,128)(2,1)}, u32[]{:S(2)}, u32[]{:S(2)}) collective-permute-start(bf16[768,768]{1,0:T(8,128)(2,1)} %bitcast.41), channel_id=1, source_target_pairs={{0,1},{1,0},{2,3},{3,2},{4,5},{5,4},{6,7},{7,6},{8,9},{9,8},{10,11... | collective-permute-start | bytes 3538952 | tf_op jit(solution)/shard_map/ppermute | solution.py:65
  282.9 29.1 %collective-permute-start.40 = (bf16[2,128,1536]{2,1,0:T(8,128)(2,1)}, bf16[2,128,1536]{2,1,0:T(8,128)(2,1)}, u32[]{:S(2)}, u32[]{:S(2)}) collective-permute-start(bf16[2,128,1536]{2,1,0:T(8,128)(2,1)} %get-tuple-element.357), channel_id=1, source_target_pairs={{0,4},{4,0},{1,5},{5,1},{2,6},{6,2},{3,7},{7,3},{8,12},{12,8},{9,1... | collective-permute-start | bytes 2359304 | tf_op jit(solution)/shard_map/ppermute | solution.py:65
  300.0 52.1 %collective-permute-start.47 = (bf16[768,768]{1,0:T(8,128)(2,1)}, bf16[768,768]{1,0:T(8,128)(2,1)}, u32[]{:S(2)}, u32[]{:S(2)}) collective-permute-start(bf16[768,768]{1,0:T(8,128)(2,1)} %bitcast.43), channel_id=1, source_target_pairs={{0,1},{1,0},{2,3},{3,2},{4,5},{5,4},{6,7},{7,6},{8,9},{9,8},{10,11... | collective-permute-start | bytes 3538952 | tf_op jit(solution)/shard_map/ppermute | solution.py:65
  302.9 27.6 %collective-permute-start.39 = (bf16[2,192,1152]{2,1,0:T(8,128)(2,1)}, bf16[2,192,1152]{2,1,0:T(8,128)(2,1)}, u32[]{:S(2)}, u32[]{:S(2)}) collective-permute-start(bf16[2,192,1152]{2,1,0:T(8,128)(2,1)} %get-tuple-element.396), channel_id=1, source_target_pairs={{0,8},{8,0},{16,24},{24,16},{1,9},{9,1},{17,25},{25,17},{2,10},{10... | collective-permute-start | bytes 2654216 | tf_op jit(solution)/shard_map/ppermute | solution.py:65
  303.0 49.0 %collective-permute-start.48 = (bf16[2,288,768]{2,1,0:T(8,128)(2,1)S(1)}, bf16[2,288,768]{2,1,0:T(8,128)(2,1)S(1)}, u32[]{:S(2)}, u32[]{:S(2)}) collective-permute-start(bf16[2,288,768]{2,1,0:T(8,128)(2,1)S(1)} %shard_map.206.refs_0_), channel_id=1, source_target_pairs={{0,8},{8,0},{16,24},{24,16},{1,9},{9,1},{17,25},{25,17},{2,10},{10... | collective-permute-start | bytes 2654216 | tf_op jit(solution)/shard_map/ppermute | solution.py:65
  310.4 45.2 %collective-permute-start.46 = (bf16[4,96,768]{2,1,0:T(8,128)(2,1)S(1)}, bf16[4,96,768]{2,1,0:T(8,128)(2,1)S(1)}, u32[]{:S(2)}, u32[]{:S(2)}) collective-permute-start(bf16[4,96,768]{2,1,0:T(8,128)(2,1)S(1)} %get-tuple-element.407), channel_id=1, source_target_pairs={{0,4},{4,0},{1,5},{5,1},{2,6},{6,2},{3,7},{7,3},{8,12},{12,8},{9,1... | collective-permute-start | bytes 1769480 | tf_op jit(solution)/shard_map/ppermute | solution.py:65
  330.5 31.2 %collective-permute-start.51 = (bf16[1,192,1152]{2,1,0:T(8,128)(2,1)}, bf16[1,192,1152]{2,1,0:T(8,128)(2,1)}, u32[]{:S(2)}, u32[]{:S(2)}) collective-permute-start(bf16[1,192,1152]{2,1,0:T(8,128)(2,1)} %shard_map.204.refs_0_), channel_id=1, source_target_pairs={{0,16},{8,24},{16,0},{24,8},{1,17},{9,25},{17,1},{25,9},{2,18},{10... | collective-permute-start | bytes 1327112 | tf_op jit(solution)/shard_map/ppermute | solution.py:65
  361.7 40.3 %collective-permute-start.56 = (bf16[1,192,1152]{2,1,0:T(8,128)(2,1)}, bf16[1,192,1152]{2,1,0:T(8,128)(2,1)S(1)}, u32[]{:S(2)}, u32[]{:S(2)}) collective-permute-start(bf16[1,192,1152]{2,1,0:T(8,128)(2,1)} %copy-done.82), channel_id=1, source_target_pairs={{0,16},{8,24},{16,0},{24,8},{1,17},{9,25},{17,1},{25,9},{2,18},{10... | collective-permute-start | bytes 1327112 | tf_op jit(solution)/shard_map/ppermute | solution.py:65
  374.8 27.4 %collective-permute-start.45 = (bf16[128,1536]{1,0:T(8,128)(2,1)}, bf16[128,1536]{1,0:T(8,128)(2,1)S(1)}, u32[]{:S(2)}, u32[]{:S(2)}) collective-permute-start(bf16[128,1536]{1,0:T(8,128)(2,1)} %copy-done.85), channel_id=1, source_target_pairs={{0,1},{1,0},{2,3},{3,2},{4,5},{5,4},{6,7},{7,6},{8,9},{9,8},{10,11... | collective-permute-start | bytes 1179656 | tf_op jit(solution)/shard_map/ppermute | solution.py:65
  404.2 41.5 %collective-permute-start.61 = (bf16[4,288,768]{2,1,0:T(8,128)(2,1)S(1)}, bf16[4,288,768]{2,1,0:T(8,128)(2,1)}, u32[]{:S(2)}, u32[]{:S(2)}) collective-permute-start(bf16[4,288,768]{2,1,0:T(8,128)(2,1)S(1)} %shard_map.212.refs_0_), channel_id=1, source_target_pairs={{0,4},{4,0},{1,5},{5,1},{2,6},{6,2},{3,7},{7,3},{8,12},{12,8},{9,1... | collective-permute-start | bytes 5308424 | tf_op jit(solution)/shard_map/ppermute | solution.py:65
  405.7 40.0 %collective-permute-start.62 = (bf16[4,288,768]{2,1,0:T(8,128)(2,1)S(1)}, bf16[4,288,768]{2,1,0:T(8,128)(2,1)}, u32[]{:S(2)}, u32[]{:S(2)}) collective-permute-start(bf16[4,288,768]{2,1,0:T(8,128)(2,1)S(1)} %shard_map.212.refs_0_), channel_id=1, source_target_pairs={{0,2},{2,0},{1,3},{3,1},{4,6},{6,4},{5,7},{7,5},{8,10},{10,8},{9,1... | collective-permute-start | bytes 5308424 | tf_op jit(solution)/shard_map/ppermute | solution.py:65
  405.9 27.1 %collective-permute-start.63 = (bf16[1,192,1152]{2,1,0:T(8,128)(2,1)}, bf16[1,192,1152]{2,1,0:T(8,128)(2,1)S(1)}, u32[]{:S(2)}, u32[]{:S(2)}) collective-permute-start(bf16[1,192,1152]{2,1,0:T(8,128)(2,1)} %copy-done.54), channel_id=1, source_target_pairs={{0,1},{1,0},{2,3},{3,2},{4,5},{5,4},{6,7},{7,6},{8,9},{9,8},{10,11... | collective-permute-start | bytes 1327112 | tf_op jit(solution)/shard_map/ppermute | solution.py:65
  431.1 27.1 %collective-permute-start.67 = (bf16[4,96,768]{2,1,0:T(8,128)(2,1)S(1)}, bf16[4,96,768]{2,1,0:T(8,128)(2,1)S(1)}, u32[]{:S(2)}, u32[]{:S(2)}) collective-permute-start(bf16[4,96,768]{2,1,0:T(8,128)(2,1)S(1)} %copy-done.81), channel_id=1, source_target_pairs={{0,4},{4,0},{1,5},{5,1},{2,6},{6,2},{3,7},{7,3},{8,12},{12,8},{9,1... | collective-permute-start | bytes 1769480 | tf_op jit(solution)/shard_map/ppermute | solution.py:65
  448.0 27.9 %collective-permute-start.74 = (bf16[4,96,768]{2,1,0:T(8,128)(2,1)S(1)}, bf16[4,96,768]{2,1,0:T(8,128)(2,1)S(1)}, u32[]{:S(2)}, u32[]{:S(2)}) collective-permute-start(bf16[4,96,768]{2,1,0:T(8,128)(2,1)S(1)} %shard_map.225.refs_0_), channel_id=1, source_target_pairs={{0,4},{4,0},{1,5},{5,1},{2,6},{6,2},{3,7},{7,3},{8,12},{12,8},{9,1... | collective-permute-start | bytes 1769480 | tf_op jit(solution)/shard_map/ppermute | solution.py:65
  462.7 50.4 %collective-permute-start.72 = (bf16[4,192,1152]{2,1,0:T(8,128)(2,1)S(1)}, bf16[4,192,1152]{2,1,0:T(8,128)(2,1)}, u32[]{:S(2)}, u32[]{:S(2)}) collective-permute-start(bf16[4,192,1152]{2,1,0:T(8,128)(2,1)S(1)} %shard_map.222.refs_0_), channel_id=1, source_target_pairs={{0,4},{4,0},{1,5},{5,1},{2,6},{6,2},{3,7},{7,3},{8,12},{12,8},{9,1... | collective-permute-start | bytes 5308424 | tf_op jit(solution)/shard_map/ppermute | solution.py:65
  466.5 30.4 %collective-permute-start.77 = (bf16[2,192,1152]{2,1,0:T(8,128)(2,1)S(1)}, bf16[2,192,1152]{2,1,0:T(8,128)(2,1)S(1)}, u32[]{:S(2)}, u32[]{:S(2)}) collective-permute-start(bf16[2,192,1152]{2,1,0:T(8,128)(2,1)S(1)} %shard_map.228.refs_0_), channel_id=1, source_target_pairs={{0,8},{8,0},{16,24},{24,16},{1,9},{9,1},{17,25},{25,17},{2,10},{10... | collective-permute-start | bytes 2654216 | tf_op jit(solution)/shard_map/ppermute | solution.py:65
  474.8 29.0 %collective-permute-start.65 = (bf16[2,128,1536]{2,1,0:T(8,128)(2,1)S(1)}, bf16[2,128,1536]{2,1,0:T(8,128)(2,1)S(1)}, u32[]{:S(2)}, u32[]{:S(2)}) collective-permute-start(bf16[2,128,1536]{2,1,0:T(8,128)(2,1)S(1)} %copy-done.79), channel_id=1, source_target_pairs={{0,1},{1,0},{2,3},{3,2},{4,5},{5,4},{6,7},{7,6},{8,9},{9,8},{10,11... | collective-permute-start | bytes 2359304 | tf_op jit(solution)/shard_map/ppermute | solution.py:65
  476.0 37.2 %collective-permute-start.73 = (bf16[4,192,1152]{2,1,0:T(8,128)(2,1)S(1)}, bf16[4,192,1152]{2,1,0:T(8,128)(2,1)S(1)}, u32[]{:S(2)}, u32[]{:S(2)}) collective-permute-start(bf16[4,192,1152]{2,1,0:T(8,128)(2,1)S(1)} %shard_map.222.refs_0_), channel_id=1, source_target_pairs={{0,2},{2,0},{1,3},{3,1},{4,6},{6,4},{5,7},{7,5},{8,10},{10,8},{9,1... | collective-permute-start | bytes 5308424 | tf_op jit(solution)/shard_map/ppermute | solution.py:65
  493.0 36.4 %collective-permute-start.81 = (bf16[4,288,768]{2,1,0:T(8,128)(2,1)}, bf16[4,288,768]{2,1,0:T(8,128)(2,1)}, u32[]{:S(2)}, u32[]{:S(2)}) collective-permute-start(bf16[4,288,768]{2,1,0:T(8,128)(2,1)} %collective-permute-done.61.refs_0_), channel_id=1, source_target_pairs={{0,2},{2,0},{1,3},{3,1},{4,6},{6,4},{5,7},{7,5},{8,10},{10,8},{9,1... | collective-permute-start | bytes 5308424 | tf_op jit(solution)/shard_map/ppermute | solution.py:65
  502.3 48.3 %collective-permute-start.86 = (bf16[4,192,1152]{2,1,0:T(8,128)(2,1)S(1)}, bf16[4,192,1152]{2,1,0:T(8,128)(2,1)}, u32[]{:S(2)}, u32[]{:S(2)}) collective-permute-start(bf16[4,192,1152]{2,1,0:T(8,128)(2,1)S(1)} %shard_map.232.refs_0_), channel_id=1, source_target_pairs={{0,4},{4,0},{1,5},{5,1},{2,6},{6,2},{3,7},{7,3},{8,12},{12,8},{9,1... | collective-permute-start | bytes 5308424 | tf_op jit(solution)/shard_map/ppermute | solution.py:65
  503.8 46.8 %collective-permute-start.87 = (bf16[4,192,1152]{2,1,0:T(8,128)(2,1)S(1)}, bf16[4,192,1152]{2,1,0:T(8,128)(2,1)}, u32[]{:S(2)}, u32[]{:S(2)}) collective-permute-start(bf16[4,192,1152]{2,1,0:T(8,128)(2,1)S(1)} %shard_map.232.refs_0_), channel_id=1, source_target_pairs={{0,2},{2,0},{1,3},{3,1},{4,6},{6,4},{5,7},{7,5},{8,10},{10,8},{9,1... | collective-permute-start | bytes 5308424 | tf_op jit(solution)/shard_map/ppermute | solution.py:65
  518.8 33.5 %collective-permute-start.92 = (bf16[4,192,1152]{2,1,0:T(8,128)(2,1)}, bf16[4,192,1152]{2,1,0:T(8,128)(2,1)}, u32[]{:S(2)}, u32[]{:S(2)}) collective-permute-start(bf16[4,192,1152]{2,1,0:T(8,128)(2,1)} %collective-permute-done.72.refs_0_), channel_id=1, source_target_pairs={{0,2},{2,0},{1,3},{3,1},{4,6},{6,4},{5,7},{7,5},{8,10},{10,8},{9,1... | collective-permute-start | bytes 5308424 | tf_op jit(solution)/shard_map/ppermute | solution.py:65
  (158 other events, 2477.6 us)
